TPU v7x, 256 devices: a whole 4x4x8 slice. The times are simulated.
256 devices in a mesh: ctx: 64 (over z, x, core), kvh: 4 (over y).
Axes of the slice: x: 4, y: 4, z: 8, core: 2. Of those that a mesh axis runs over, the one named last changes fastest.
Arguments:
- hidden: bfloat16 [8192, 4096], P('ctx', 'kvh'), may hold values from -16 to 16
- query_weight: bfloat16 [4096, 2048], P('ctx', 'kvh'), may hold values from -0.09375 to 0.09375
- probe_vector: bfloat16 [4096, 2048], P('ctx', 'kvh'), may hold values from -6 to 6
- key_rows: bfloat16 [8192, 512], P('ctx', 'kvh'), may hold values from -6 to 6
- value_rows: bfloat16 [8192, 512], P('ctx', 'kvh'), may hold values from -6 to 6
- upstream: bfloat16 [8192, 2048], P('ctx', 'kvh'), may hold values from -1.25 to 1.25
- lengths: int32 [16], replicated, may hold values from 1 to 2048, 8192 in all
- block_order: int32 [128], replicated, may hold values from 0 to 127, each once
Outputs:
- curvature: float32 [4096, 2048], P('ctx', 'kvh')
Inputs may be any that keep to these rules, and one draw needn't show every extreme that they name: The lengths sum to 8192. `block_order`: each block number appears once.
All inputs are finite; a program needn't handle non-finite values.
Results may differ from a plain program's by a relative error of at most 0.01.
Values may be sent and summed in bfloat16 or wider, within the bound.
No kernel may reach another device: no remote copies, remote signals or barrier semaphores. Data moves between devices by JAX's collectives and lax.ppermute only.
A program may use at most 64 MiB of HBM per device.

v0:
```python
import math

import jax
import jax.numpy as jnp
from jax import lax
from jax.sharding import PartitionSpec as P

HD = 128


def layout_of(first_row, row_count, block_order, doc_ends, block_rows):
    layout = first_row + jnp.arange(row_count, dtype=jnp.int32)
    block_of = layout // block_rows
    block_ids = jnp.arange(block_order.shape[0], dtype=jnp.int32)
    picked = jnp.sum(
        jnp.where(block_of[:, None] == block_ids[None, :], block_order[None, :], 0), axis=1
    )
    position = picked * block_rows + layout % block_rows
    document = jnp.sum((position[:, None] >= doc_ends[None, :]).astype(jnp.int32), axis=1)
    return (position, document)


def per_device(
    hidden, query_weight, probe_vector, key_rows, value_rows, upstream, lengths, block_order
):
    row_count = hidden.shape[0]
    block_rows = row_count // 2
    head_width = query_weight.shape[1]
    kv_local = key_rows.shape[1] // HD
    group_size = head_width // HD // kv_local
    score_scale = 1.0 / math.sqrt(HD)
    features_all = lax.all_gather(hidden, "kvh", axis=1, tiled=True)
    shards = (
        lax.all_gather(query_weight, "ctx", axis=0, tiled=True),
        lax.all_gather(probe_vector, "ctx", axis=0, tiled=True),
    )
    query_full = jnp.dot(features_all, shards[0], preferred_element_type=jnp.float32)
    tangent_full = jnp.dot(features_all, shards[1], preferred_element_type=jnp.float32)
    query_heads = query_full.astype(jnp.bfloat16).reshape(row_count, kv_local, group_size, HD)
    tangent_heads = tangent_full.astype(jnp.bfloat16).reshape(row_count, kv_local, group_size, HD)
    upstream_heads = upstream.reshape(row_count, kv_local, group_size, HD)
    doc_ends = jnp.cumsum(lengths)
    position, document = layout_of(
        lax.axis_index("ctx") * row_count, row_count, block_order, doc_ends, block_rows
    )

    def allowed_of(key_count, offset):
        key_position, key_document = layout_of(offset, key_count, block_order, doc_ends, block_rows)
        return (document[:, None] == key_document[None, :]) & (
            key_position[None, :] <= position[:, None]
        )

    def scored_of(key_block, value_block, allowed):
        key_count = key_block.shape[0]
        key_heads = key_block.reshape(key_count, kv_local, HD)
        value_heads = value_block.reshape(key_count, kv_local, HD)
        scores = (
            jnp.einsum("rkgd,nkd->rkgn", query_heads, key_heads, preferred_element_type=jnp.float32)
            * score_scale
        )
        tangent_scores = (
            jnp.einsum(
                "rkgd,nkd->rkgn", tangent_heads, key_heads, preferred_element_type=jnp.float32
            )
            * score_scale
        )
        value_match = jnp.einsum(
            "rkgd,nkd->rkgn", upstream_heads, value_heads, preferred_element_type=jnp.float32
        )
        exp_scores = jnp.where(allowed[:, None, None, :], jnp.exp(scores), 0.0)
        return (exp_scores, tangent_scores, value_match, key_heads)

    def block_step_of(update):

        def block_step(running, key_block, value_block, offset):
            allowed = allowed_of(key_block.shape[0], offset)
            return update(running, scored_of(key_block, value_block, allowed))

        return block_step

    def sweep_keys(block_step, running, shards):
        key_all, value_all = shards
        key_count = key_all.shape[0]
        block_size = 512

        def advance(turn_index, carried):
            first_key = turn_index * block_size
            key_block = lax.dynamic_slice_in_dim(key_all, first_key, block_size, 0)
            value_block = lax.dynamic_slice_in_dim(value_all, first_key, block_size, 0)
            return block_step(carried, key_block, value_block, first_key)

        return lax.fori_loop(0, key_count // block_size, advance, running)

    def add_statistics(running, scored):
        exp_scores, tangent_scores, value_match, key_heads = scored
        return (
            running[0] + jnp.sum(exp_scores, axis=-1),
            running[1] + jnp.sum(exp_scores * value_match, axis=-1),
            running[2] + jnp.sum(exp_scores * tangent_scores, axis=-1),
            running[3] + jnp.sum(exp_scores * value_match * tangent_scores, axis=-1),
        )

    zero_stat = jnp.zeros((row_count, kv_local, group_size), jnp.float32)
    stat_start = (zero_stat, zero_stat, zero_stat, zero_stat)
    first_step = block_step_of(add_statistics)

    def finish_statistics(statistics_out):
        weight_sum, value_sum, tangent_sum, joint_sum = statistics_out
        value_mean = value_sum / weight_sum
        tangent_mean = tangent_sum / weight_sum
        value_drift = joint_sum / weight_sum - tangent_mean * value_mean

        def add_keys(running, scored):
            exp_scores, tangent_scores, value_match, key_heads = scored
            weight = (
                exp_scores
                / weight_sum[..., None]
                * (
                    (tangent_scores - tangent_mean[..., None])
                    * (value_match - value_mean[..., None])
                    - value_drift[..., None]
                )
            ).astype(jnp.bfloat16)
            return running + jnp.einsum(
                "rkgn,nkd->rkgd", weight, key_heads, preferred_element_type=jnp.float32
            )

        return block_step_of(add_keys)

    zero_acc = jnp.zeros((row_count, kv_local, group_size, HD), jnp.float32)
    statistics_out = sweep_keys(
        first_step,
        stat_start,
        (
            lax.all_gather(key_rows, "ctx", axis=0, tiled=True),
            lax.all_gather(value_rows, "ctx", axis=0, tiled=True),
        ),
    )
    second_step = finish_statistics(statistics_out)
    accumulated = sweep_keys(
        second_step,
        zero_acc,
        (
            lax.all_gather(key_rows, "ctx", axis=0, tiled=True),
            lax.all_gather(value_rows, "ctx", axis=0, tiled=True),
        ),
    )
    second_order = (accumulated * score_scale).astype(jnp.bfloat16).reshape(row_count, head_width)
    return lax.psum_scatter(
        lax.dot_general(
            features_all, second_order, (((0,), (0,)), ((), ())), preferred_element_type=jnp.float32
        ),
        "ctx",
        scatter_dimension=0,
        tiled=True,
    )


def solution(mesh):
    in_specs = (
        P("ctx", "kvh"),
        P("ctx", "kvh"),
        P("ctx", "kvh"),
        P("ctx", "kvh"),
        P("ctx", "kvh"),
        P("ctx", "kvh"),
        P(),
        P(),
    )
    out_specs = P("ctx", "kvh")
    return jax.shard_map(
        per_device, mesh=mesh, in_specs=in_specs, out_specs=out_specs, check_vma=False
    )
```

profile of v0, /device:TPU:8, one launch (start us, length us, event | category | flops | bytes accessed | tf_op | source)
XLA Modules:
  0.0 668.7 jit_solution(8767175065505285253)
XLA Ops:
  13.0 24.7 %all-gather.8.cloned.1.call-done = bf16[128,4096]{1,0:T(8,128)(2,1)} async-done(((bf16[128,1024]{1,0:T(8,128)(2,1)}), bf16[128,4096]{1,0:T(8,128)(2,1)}) %all-gather.8.cloned.1.call-update) | async-done | bytes 1048592 | tf_op jit(solution)/shard_map/all_gather | solution.py:32
  37.7 83.0 %all-gather.10.cloned.1.call-done = bf16[4096,512]{1,0:T(8,128)(2,1)} async-done(((bf16[64,512]{1,0:T(8,128)(2,1)}), bf16[4096,512]{1,0:T(8,128)(2,1)}) %all-gather.10.cloned.1.call-update) | async-done | bytes 4194320 | tf_op jit(solution)/shard_map/all_gather | solution.py:34
  120.7 3.2 convolution_convert_fusion.1
  124.0 75.8 %all-gather.14.cloned.1.call-done = bf16[4096,512]{1,0:T(8,128)(2,1)} async-done(((bf16[64,512]{1,0:T(8,128)(2,1)}), bf16[4096,512]{1,0:T(8,128)(2,1)}) %all-gather.14.cloned.1.call-update) | async-done | bytes 4194320 | tf_op jit(solution)/shard_map/all_gather | solution.py:35
  199.8 2.9 convolution_convert_fusion
  202.8 74.1 %all-gather.6.cloned.1.call-done = bf16[8192,128]{1,0:T(8,128)(2,1)} async-done(((bf16[128,128]{1,0:T(8,128)(2,1)}), bf16[8192,128]{1,0:T(8,128)(2,1)}) %all-gather.6.cloned.1.call-update) | async-done | bytes 2097168 | tf_op jit(solution)/shard_map/all_gather | solution.py:144
  276.9 77.6 %all-gather.12.cloned.1.call-done = bf16[8192,128]{1,0:T(8,128)(2,1)} async-done(((bf16[128,128]{1,0:T(8,128)(2,1)}), bf16[8192,128]{1,0:T(8,128)(2,1)}) %all-gather.12.cloned.1.call-update) | async-done | bytes 2097168 | tf_op jit(solution)/shard_map/all_gather | solution.py:145
  354.5 69.9 %while.38 = (s32[]{:T(128)}, f32[128,1,4]{0,2,1:T(4,128)S(1)}, f32[128,1,4]{0,2,1:T(4,128)S(1)}, f32[128,1,4]{0,2,1:T(4,128)S(1)}, f32[128,1,4]{0,2,1:T(4,128)S(...) while((s32[]{:T(128)}, f32[128,1,4]{0,2,1:T(4,128)S(1)}, ...), condition=%wide.region_10.11_spmd.clone, body=%wide.region_3.10_spmd.clone.sunk | while | flops 204382208 | bytes 5164858 | solution.py:92
  357.5 1.3 multiply_reduce_fusion.3
  359.4 1.2 fusion.90
  361.9 1.3 multiply_reduce_fusion.3
  366.2 1.3 multiply_reduce_fusion.3
  368.2 1.2 fusion.90
  370.6 1.3 multiply_reduce_fusion.3
  375.0 1.3 multiply_reduce_fusion.3
  376.9 1.2 fusion.90
  379.4 1.3 multiply_reduce_fusion.3
  383.7 1.3 multiply_reduce_fusion.3
  385.6 1.2 fusion.90
  388.1 1.3 multiply_reduce_fusion.3
  392.5 1.3 multiply_reduce_fusion.3
  396.8 1.3 multiply_reduce_fusion.3
  401.2 1.3 multiply_reduce_fusion.3
  405.6 1.3 multiply_reduce_fusion.3
  409.9 1.3 multiply_reduce_fusion.3
  414.3 1.3 multiply_reduce_fusion.3
  418.7 1.3 multiply_reduce_fusion.3
  423.1 1.3 multiply_reduce_fusion.3
  424.4 73.6 %while.39 = (s32[]{:T(128)}, f32[128,1,4,128]{0,3,2,1:T(8,128)S(1)}, bf16[8192,128]{1,0:T(8,128)(2,1)}, s32[128]{0:T(128)S(1)}, s32[128]{0:T(128)S(1)}, /*index=...) while((s32[]{:T(128)}, ...), condition=%wide.region_14.15_spmd.clone, body=%wide.region_11.14_spmd.clone.sunk | while | flops 271620096 | bytes 5797180 | solution.py:92
  425.0 1.3 fusion.99
  427.5 1.5 fusion.101
  429.6 1.3 fusion.99
  432.1 1.5 fusion.101
  434.2 1.3 fusion.99
  436.7 1.5 fusion.101
  438.8 1.3 fusion.99
  441.3 1.5 fusion.101
  443.4 1.3 fusion.99
  445.9 1.5 fusion.101
  448.0 1.3 fusion.99
  450.5 1.5 fusion.101
  452.6 1.3 fusion.99
  455.1 1.5 fusion.101
  457.2 1.3 fusion.99
  459.7 1.5 fusion.101
  461.8 1.3 fusion.99
  464.3 1.5 fusion.101
  466.4 1.3 fusion.99
  468.9 1.5 fusion.101
  471.0 1.3 fusion.99
  473.5 1.5 fusion.101
  475.6 1.3 fusion.99
  478.1 1.5 fusion.101
  480.2 1.3 fusion.99
  482.7 1.5 fusion.101
  484.8 1.3 fusion.99
  487.2 1.5 fusion.101
  489.4 1.3 fusion.99
  491.8 1.5 fusion.101
  494.0 1.3 fusion.99
  496.4 1.5 fusion.101
  498.0 5.7 convolution_bitcast_fusion.3
  503.7 9.0 %copy.53 = f32[4096,512]{1,0:T(8,128)} copy(f32[4096,512]{0,1:T(8,128)} %convolution_bitcast_fusion.3) | data formatting | bytes 16777216
  512.7 149.2 %reduce-scatter.4.cloned.1.call-done = f32[64,512]{1,0:T(8,128)} async-done(((f32[4096,512]{1,0:T(8,128)}), f32[64,512]{1,0:T(8,128)}) %reduce-scatter.4.cloned.1.call-update) | async-done | bytes 131088 | tf_op jit(solution)/shard_map/reduce_scatter | solution.py:149
  (272 shorter events, 78.1 us)
Async XLA Ops:
  6.5 31.2 %all-gather.8.cloned.1.call-start = ((), (), s32[]{:S(2)}) async-start(), calls=%async_computation.2 | async-start | bytes 1310720 | tf_op jit(solution)/shard_map/all_gather | solution.py:32
  7.3 113.5 %all-gather.10.cloned.1.call-start = ((), (), s32[]{:S(2)}) async-start(), calls=%async_computation.3 | async-start | bytes 4259840 | tf_op jit(solution)/shard_map/all_gather | solution.py:34
  8.0 191.8 %all-gather.14.cloned.1.call-start = ((), (), s32[]{:S(2)}) async-start(), calls=%async_computation.5 | async-start | bytes 4259840 | tf_op jit(solution)/shard_map/all_gather | solution.py:35
  8.7 268.2 %all-gather.6.cloned.1.call-start = ((), (), s32[]{:S(2)}) async-start(), calls=%async_computation.1 | async-start | bytes 2129920 | tf_op jit(solution)/shard_map/all_gather | solution.py:144
  9.3 345.2 %all-gather.12.cloned.1.call-start = ((), (), s32[]{:S(2)}) async-start(), calls=%async_computation.4 | async-start | bytes 2129920 | tf_op jit(solution)/shard_map/all_gather | solution.py:145
  9.9 652.0 %reduce-scatter.4.cloned.1.call-start = ((), (), s32[]{:S(2)}) async-start(), calls=%async_computation.6 | async-start | bytes 8519680 | tf_op jit(solution)/shard_map/reduce_scatter | solution.py:149
  37.7 162.1 %copy-start = (bf16[128,4096]{1,0:T(8,128)(2,1)S(1)}, bf16[128,4096]{1,0:T(8,128)(2,1)}, u32[]{:S(2)}) copy-start(bf16[128,4096]{1,0:T(8,128)(2,1)} %all-gather.8.cloned.1.call-done) | copy-start | bytes 3145732
  124.0 230.5 %copy-start.1 = (s32[128]{0:T(128)S(1)}, s32[128]{0:T(128)}, u32[]{:S(2)}) copy-start(s32[128]{0:T(128)} %param.19) | copy-start | bytes 1540
Sparse Core Ops, SparseCore 0:
  9.2 28.4 all-gather.7
  40.5 80.2 all-gather.9
  123.5 76.2 all-gather.13
  202.4 74.4 all-gather.5
  279.5 74.9 all-gather.11
  512.8 149.0 reduce-scatter.3
where the time goes:
time: 671 us; the launch traced here: 669 us
  waiting for transfers between devices  487 us (73%)
  matrix products  135 us (20%)
  other arithmetic  19.4 us (3%)
  between operations  13.6 us (2%)
  local copies, waits for them, and re-layouts  11 us (2%)
    reduce_scatter x1, waiting for transfers between devices, per_device(): lax.psum_scatter(lax.dot_general(features_all, second_order, (((0,), (0,)...  149 us
    all_gather x1, waiting for transfers between devices, per_device(): lax.all_gather(query_weight, 'ctx', axis=0, tiled=True)  83 us
    all_gather x1, waiting for transfers between devices, per_device(): lax.all_gather(value_rows, 'ctx', axis=0, tiled=True)  77.6 us
    all_gather x1, waiting for transfers between devices, per_device(): lax.all_gather(probe_vector, 'ctx', axis=0, tiled=True)  75.8 us
    all_gather x1, waiting for transfers between devices, per_device(): lax.all_gather(key_rows, 'ctx', axis=0, tiled=True)  74.1 us
    dot_general x32, matrix products, scored_of(): jnp.einsum('rkgd,nkd->rkgn', query_heads, key_heads, preferred_element_ty...  40 us
    dot_general x32, matrix products, scored_of(): jnp.einsum('rkgd,nkd->rkgn', tangent_heads, key_heads, preferred_element_...  38.6 us
    all_gather x1, waiting for transfers between devices, per_device(): features_all = lax.all_gather(hidden, 'kvh', axis=1, tiled=True)  24.7 us
  transfers between devices with their start and end apart: 6, of which 6 were waited for; matrix products, arithmetic and copies ran while one was open for 1% of the time, Pallas kernels for 0%

commit v1 on v0

v1 whole, which is shorter than its diff:
```python
import functools
import math

import jax
import jax.numpy as jnp
from jax import lax
from jax.experimental import pallas as pl
from jax.experimental.pallas import tpu as pltpu
from jax.sharding import Mesh, PartitionSpec as P

HD = 128
BLK = 64
NDOC = 16
CHUNK_BLOCKS = 8
CHUNK = CHUNK_BLOCKS * BLK
MAX_CHUNKS = 5
SCALE = 1.0 / math.sqrt(HD)
LOG2E = 1.4426950408889634
TOKENS = 8192
D = 4096
BF16 = jnp.bfloat16
F32 = jnp.float32


def fused_kernel(
    where_ref,
    order_ref,
    lengths_ref,
    h1_own,
    h1_right,
    h1_left,
    h1_far_a,
    h1_far_b,
    h2_own,
    h2_right,
    h2_left,
    h2_far_a,
    h2_far_b,
    packed_own,
    packed_other,
    upstream_ref,
    keep_ref,
    send_ref,
    hid,
    weights,
    keys_values,
    query_tangent,
    second_t,
    exp_buf,
    tan_buf,
    val_buf,
    ends,
    sem_h,
    sem_w,
    sem_kv,
):
    z, x, c, y = where_ref[0], where_ref[1], where_ref[2], where_ref[3]

    for dx in range(4):
        xx = lax.rem(x - dx + 4, 4)
        for src, cc in ((packed_own, c), (packed_other, 1 - c)):
            row = pl.multiple_of((xx * 2 + cc) * 64, 64)
            pltpu.make_async_copy(
                src.at[:, pl.ds(dx * 192, 64), :], weights.at[:, pl.ds(row, 64), :], sem_w
            ).start()

    h1_pieces = []
    for dx, src in ((0, h1_own), (1, h1_right), (3, h1_left)):
        h1_pieces += [(dx, dy, src.at[dy]) for dy in range(4)]
    h1_pieces += [(2, 0, h1_far_a.at[0]), (2, 1, h1_far_a.at[1])]
    h1_pieces += [(2, 2, h1_far_b.at[0]), (2, 3, h1_far_b.at[1])]
    for dx, dy, src in h1_pieces:
        group = lax.rem(y - dy + 4, 4) * 2
        pltpu.make_async_copy(src, hid.at[group, pl.ds(dx * 128, 128), :], sem_h).start()
    for dy, row, rows, src in (
        (0, 0, 512, h2_own),
        (1, 0, 512, h2_right),
        (3, 0, 512, h2_left),
        (2, 0, 256, h2_far_a),
        (2, 256, 256, h2_far_b),
    ):
        group = lax.rem(y - dy + 4, 4) * 2 + 1
        pltpu.make_async_copy(src, hid.at[group, pl.ds(row, rows), :], sem_h).start()

    def place(i, carry):
        zz = i // 4
        dx = lax.rem(i, 4)
        xx = lax.rem(x - dx + 4, 4)
        for src, cc in ((packed_own, c), (packed_other, 1 - c)):
            block = ((zz * 4 + xx) * 2 + cc) * 2
            for b in range(2):
                target = pl.multiple_of(order_ref[block + b] * BLK, BLK)
                row = pl.multiple_of(dx * 192 + 64 + b * 64, 64)
                pltpu.make_async_copy(
                    src.at[zz, pl.ds(row, 64), :], keys_values.at[pl.ds(target, BLK), :], sem_kv
                ).start()
        return carry

    lax.fori_loop(0, 32, place, 0)
    keys_values[pl.ds(TOKENS, CHUNK), :] = jnp.zeros((CHUNK, 256), BF16)

    total = jnp.int32(0)
    for d in range(NDOC):
        total = total + lengths_ref[d]
        ends[d] = total

    pltpu.make_async_copy(weights, weights, sem_w).wait()
    pltpu.make_async_copy(hid, hid, sem_h).wait()

    acc = jnp.zeros((512, 256), F32)
    for g in range(8):
        acc = acc + jnp.dot(hid[g], weights[g], preferred_element_type=F32)
    projected = acc.astype(BF16)
    for rb in range(8):
        query_tangent[rb, 0:64, :] = projected[rb * 64 : rb * 64 + 64, 0:128]
        query_tangent[rb, 64:128, :] = projected[rb * 64 : rb * 64 + 64, 128:256]

    whole = keys_values.at[pl.ds(0, TOKENS), :]
    pltpu.make_async_copy(whole, whole, sem_kv).wait()

    def row_block(rb, carry):
        dx = rb // 2
        xx = lax.rem(x - dx + 4, 4)
        p = order_ref[((z * 4 + xx) * 2 + c) * 2 + lax.rem(rb, 2)]
        first_start = jnp.int32(0)
        pos = p * BLK + lax.broadcasted_iota(jnp.int32, (BLK, 1), 0)
        start = jnp.zeros((BLK, 1), jnp.int32)
        for d in range(NDOC):
            end = ends[d]
            first_start = jnp.where(end <= p * BLK, end, first_start)
            start = jnp.where(end <= pos, end, start)
        kb0 = first_start // BLK
        chunks = (p - kb0 + CHUNK_BLOCKS) // CHUNK_BLOCKS
        qt = query_tangent[rb]
        up = upstream_ref[rb]

        def first_pass(j, sums):
            k0 = pl.multiple_of((kb0 + j * CHUNK_BLOCKS) * BLK, BLK)
            kv = keys_values[pl.ds(k0, CHUNK), :]
            st = lax.dot_general(
                qt, kv[:, 0:128], (((1,), (1,)), ((), ())), preferred_element_type=F32
            )
            v = lax.dot_general(
                up, kv[:, 128:256], (((1,), (1,)), ((), ())), preferred_element_type=F32
            )
            s, t = st[0:64], st[64:128]
            key_pos = k0 + lax.broadcasted_iota(jnp.int32, (BLK, CHUNK), 1)
            allowed = (key_pos >= start) & (key_pos <= pos)
            e = jnp.where(allowed, jnp.exp2(s * (SCALE * LOG2E)), 0.0)
            exp_buf[j] = e
            tan_buf[j] = t
            val_buf[j] = v
            ev = e * v
            et = e * t
            evt = ev * t

            def lanes(a):
                out = a[:, 0:128]
                for i in range(1, CHUNK // 128):
                    out = out + a[:, i * 128 : (i + 1) * 128]
                return out

            return (
                sums[0] + lanes(e),
                sums[1] + lanes(ev),
                sums[2] + lanes(et),
                sums[3] + lanes(evt),
            )

        zero = jnp.zeros((BLK, 128), F32)
        sums = lax.fori_loop(0, chunks, first_pass, (zero, zero, zero, zero))
        weight_sum, value_sum, tangent_sum, joint_sum = [
            jnp.sum(a, axis=1, keepdims=True) for a in sums
        ]
        inverse = 1.0 / weight_sum
        value_mean = value_sum * inverse
        tangent_mean = tangent_sum * inverse
        drift = joint_sum * inverse - tangent_mean * value_mean

        def second_pass(j, total):
            k0 = pl.multiple_of((kb0 + j * CHUNK_BLOCKS) * BLK, BLK)
            keys = keys_values[pl.ds(k0, CHUNK), 0:128]
            w = (exp_buf[j] * inverse) * (
                (tan_buf[j] - tangent_mean) * (val_buf[j] - value_mean) - drift
            )
            return total + jnp.dot(w.astype(BF16), keys, preferred_element_type=F32)

        so = lax.fori_loop(0, chunks, second_pass, zero)
        second_t[pl.ds(pl.multiple_of(rb * 64, 64), 64), :] = so * (SCALE * SCALE)
        return carry

    lax.fori_loop(0, 8, row_block, 0)

    so_t = second_t[...].T.astype(BF16)
    for g in range(8):
        out = jnp.dot(so_t, hid[g], preferred_element_type=F32).T
        out = out.reshape(4, 2, 64, 128)
        rows = pl.ds(g * 256, 256)
        keep_ref[rows, :] = jnp.where(c == 0, out[:, 0], out[:, 1]).reshape(256, 128)
        send_ref[rows, :] = (
            jnp.where(c == 0, out[:, 1], out[:, 0]).reshape(256, 128).astype(BF16)
        )


def fused(scalars, pieces, interpret=False):
    any_spec = pl.BlockSpec(memory_space=pl.ANY)
    smem = pl.BlockSpec(memory_space=pltpu.SMEM)
    vmem = pl.BlockSpec(memory_space=pltpu.VMEM)
    return pl.pallas_call(
        fused_kernel,
        out_shape=(
            jax.ShapeDtypeStruct((2048, 128), F32),
            jax.ShapeDtypeStruct((2048, 128), BF16),
        ),
        in_specs=[smem] * 3 + [any_spec] * 12 + [vmem],
        out_specs=(vmem, vmem),
        scratch_shapes=[
            pltpu.VMEM((8, 512, 512), BF16),
            pltpu.VMEM((8, 512, 256), BF16),
            pltpu.VMEM((TOKENS + CHUNK, 256), BF16),
            pltpu.VMEM((8, 128, 128), BF16),
            pltpu.VMEM((512, 128), F32),
            pltpu.VMEM((MAX_CHUNKS, BLK, CHUNK), F32),
            pltpu.VMEM((MAX_CHUNKS, BLK, CHUNK), F32),
            pltpu.VMEM((MAX_CHUNKS, BLK, CHUNK), F32),
            pltpu.SMEM((NDOC,), jnp.int32),
            pltpu.SemaphoreType.DMA,
            pltpu.SemaphoreType.DMA,
            pltpu.SemaphoreType.DMA,
        ],
        compiler_params=pltpu.CompilerParams(vmem_limit_bytes=40 * 1024 * 1024),
        cost_estimate=pl.CostEstimate(
            flops=6_000_000_000, bytes_accessed=14_000_000, transcendentals=1_000_000
        ),
        interpret=interpret,
    )(*scalars, *pieces)


def shift(value, axis, size, step):
    return lax.ppermute(value, axis, [(i, (i + step) % size) for i in range(size)])


def gather_four(value, axis):
    return [value] + [shift(value, axis, 4, s) for s in (1, 2, 3)]


def ring_four(stack, axis):
    right = shift(stack, axis, 4, 1)
    left = shift(stack, axis, 4, 3)
    half = stack.shape[0] // 2
    far_a = shift(right[:half], axis, 4, 1)
    far_b = shift(left[half:], axis, 4, 3)
    return [stack, right, left, far_a, far_b]


def per_device(
    hidden, query_weight, probe_vector, key_rows, value_rows, upstream, lengths, block_order
):
    z = lax.axis_index("z")
    x = lax.axis_index("x")
    c = lax.axis_index("c")
    y = lax.axis_index("kvh")

    def head_slice(array, dx):
        head = lax.rem(x + dx, 4)
        return lax.dynamic_slice_in_dim(array, head * HD, HD, 1)

    keys_values = jnp.concatenate([key_rows, value_rows], axis=1)

    def pack(dx):
        both = jnp.concatenate([head_slice(query_weight, dx), head_slice(probe_vector, dx)], axis=1)
        return jnp.concatenate([both, keys_values], axis=0)

    packs = [pack(0)] + [shift(pack(dx), "x", 4, dx) for dx in (1, 2, 3)]
    packed_own = lax.all_gather(jnp.concatenate(packs, axis=0), "z", axis=0, tiled=True)

    first, second = hidden[:, :512], hidden[:, 512:]
    stack_1 = jnp.stack(gather_four(first, "kvh"))
    sent = [jnp.concatenate([second, head_slice(upstream, dx)], axis=1) for dx in range(4)]
    sent = [sent[0]] + [shift(sent[dx], "x", 4, dx) for dx in (1, 2, 3)]
    stack_2 = jnp.concatenate([m[:, :512] for m in sent], axis=0)
    upstream_rows = jnp.concatenate([m[:, 512:] for m in sent], axis=0).reshape(8, 64, 128)
    pieces_1 = ring_four(stack_1, "x")
    pieces_2 = ring_four(stack_2, "kvh")

    packed_own, *pieces = lax.optimization_barrier((packed_own, *pieces_1, *pieces_2))
    packed_other = shift(packed_own, "c", 2, 1)

    where = jnp.stack([z, x, c, y]).astype(jnp.int32)
    keep, send = fused(
        (where, block_order, lengths),
        (
            *pieces,
            packed_own.reshape(8, 768, 256),
            packed_other.reshape(8, 768, 256),
            upstream_rows,
        ),
    )
    received = shift(send, "c", 2, 1)
    partial = (keep + received.astype(F32)).astype(BF16)
    shares = lax.all_to_all(partial, ("z", "x"), 0, 0, tiled=True)
    summed = jnp.sum(shares.reshape(8, 4, 64, 128).astype(F32), axis=0)
    return summed.transpose(1, 0, 2).reshape(64, 512)


def solution(mesh):
    fine = Mesh(mesh.devices.reshape(8, 4, 2, 4), ("z", "x", "c", "kvh"))
    ctx = ("z", "x", "c")
    split = P(ctx, "kvh")
    return jax.shard_map(
        per_device,
        mesh=fine,
        in_specs=(split,) * 6 + (P(), P()),
        out_specs=split,
        check_vma=False,
    )
```

time: 671 us -> 129 us (0.19)
  waiting for transfers between devices: 487 us -> 34.6 us
  matrix products: 135 us -> 0 us
  starting transfers between devices: 0.19 us -> 26.3 us
  blocking collectives: 0 us -> 25.9 us
  other arithmetic: 19.4 us -> 0.49 us
  Pallas kernels: 0 us -> 14.5 us
    all_gather x5 -> x1, waiting for transfers between devices: 335 us -> 7.36 us  [per_device(): lax.all_gather(jnp.concatenate(packs, axis=0), 'z', axis=0, tiled=True)]
    reduce_scatter x1 -> x0, waiting for transfers between devices: 149 us -> none  [per_device(): lax.psum_scatter(lax.dot_general(features_all, second_order, (((0,), (0,)...]
    dot_general x99 -> x0, matrix products: 135 us -> none  [the longest x32 40 us: scored_of(): jnp.einsum('rkgd,nkd->rkgn', query_heads, key_heads, preferred_element_ty...]
    ppermute x0 -> x19, waiting for transfers between devices: none -> 27.2 us  [shift(): lax.ppermute(value, axis, [(i, (i + step) % size) for i in range(size)])]
    ppermute x0 -> x19, starting transfers between devices: none -> 26.3 us  [shift(): lax.ppermute(value, axis, [(i, (i + step) % size) for i in range(size)])]
    all_to_all x0 -> x1, blocking collectives: none -> 25.9 us  [per_device(): shares = lax.all_to_all(partial, ('z', 'x'), 0, 0, tiled=True)]
    pallas_call x0 -> x1, Pallas kernels: none -> 14.5 us  [fused(): pl.pallas_call(fused_kernel, out_shape=(jax.ShapeDtypeStruct((2048, 128),...]
    reduce_sum x66 -> x1, other arithmetic: 11.2 us -> 0.08 us  [per_device(): summed = jnp.sum(shares.reshape(8, 4, 64, 128).astype(F32), axis=0)]
  transfers between devices with their start and end apart: 6 -> 20, of which waited for: 6 -> 12; matrix products, arithmetic and copies ran while one was open for 1% -> 2% of each run, Pallas kernels for 0% -> 0%
where the time goes in v1:
time: 129 us
  waiting for transfers between devices  34.6 us (27%)
  starting transfers between devices  26.3 us (20%)
  blocking collectives  25.9 us (20%)
  Pallas kernels  14.5 us (11%)
  between operations  13.6 us (11%)
  local copies, waits for them, and re-layouts  13.3 us (10%)
    ppermute x19, waiting for transfers between devices, shift(): lax.ppermute(value, axis, [(i, (i + step) % size) for i in range(size)])  27.2 us
    ppermute x19, starting transfers between devices, shift(): lax.ppermute(value, axis, [(i, (i + step) % size) for i in range(size)])  26.3 us
    all_to_all x1, blocking collectives, per_device(): shares = lax.all_to_all(partial, ('z', 'x'), 0, 0, tiled=True)  25.9 us
    pallas_call x1, Pallas kernels, fused(): pl.pallas_call(fused_kernel, out_shape=(jax.ShapeDtypeStruct((2048, 128),...  14.5 us
    unnamed x29, local copies, waits for them, and re-layouts  9.1 us
    all_gather x1, waiting for transfers between devices, per_device(): lax.all_gather(jnp.concatenate(packs, axis=0), 'z', axis=0, tiled=True)  7.36 us
  transfers between devices with their start and end apart: 20, of which 12 were waited for; matrix products, arithmetic and copies ran while one was open for 2% of the time, Pallas kernels for 0%

profile of v1, /device:TPU:8, one launch (start us, length us, event | category | flops | bytes accessed | tf_op | source)
XLA Modules:
  0.0 128.7 jit_solution(13127116800326982550)
XLA Ops:
  6.5 0.8 constant_dynamic-slice_fusion.4
  7.4 0.8 constant_dynamic-update-slice_fusion.1
  8.2 0.8 constant_dynamic-update-slice_fusion
  9.0 1.6 %collective-permute-start = (bf16[192,256]{1,0:T(8,128)(2,1)S(1)}, bf16[192,256]{1,0:T(8,128)(2,1)S(1)}, u32[]{:S(2)}, u32[]{:S(2)}) collective-permute-start(bf16[192,256]{1,0:T(8,128)(2,1)S(1)} %get-tuple-element.43), channel_id=1, source_target_pairs={{0,8},{8,16},{16,24},{24,0},{1,9},{9,17},{17,25},{25,1},{2,10},{10... | collective-permute-start | bytes 294920 | tf_op jit(solution)/shard_map/ppermute | solution.py:240
  10.6 1.7 %collective-permute-start.2 = (bf16[192,256]{1,0:T(8,128)(2,1)S(1)}, bf16[192,256]{1,0:T(8,128)(2,1)S(1)}, u32[]{:S(2)}, u32[]{:S(2)}) collective-permute-start(bf16[192,256]{1,0:T(8,128)(2,1)S(1)} %get-tuple-element.41), channel_id=1, source_target_pairs={{0,24},{8,0},{16,8},{24,16},{1,25},{9,1},{17,9},{25,17},{2,26},{10... | collective-permute-start | bytes 294920 | tf_op jit(solution)/shard_map/ppermute | solution.py:240
  12.3 1.8 %collective-permute-start.1 = (bf16[192,256]{1,0:T(8,128)(2,1)S(1)}, bf16[192,256]{1,0:T(8,128)(2,1)S(1)}, u32[]{:S(2)}, u32[]{:S(2)}) collective-permute-start(bf16[192,256]{1,0:T(8,128)(2,1)S(1)} %get-tuple-element.42), channel_id=1, source_target_pairs={{0,16},{8,24},{16,0},{24,8},{1,17},{9,25},{17,1},{25,9},{2,18},{10... | collective-permute-start | bytes 294920 | tf_op jit(solution)/shard_map/ppermute | solution.py:240
  14.1 0.8 collective-permute-done
  14.9 3.5 %collective-permute-done.1 = bf16[192,256]{1,0:T(8,128)(2,1)S(1)} collective-permute-done((bf16[192,256]{1,0:T(8,128)(2,1)S(1)}, bf16[192,256]{1,0:T(8,128)(2,1)S(1)}, u32[]{:S(2)}, u32[]{:S(2)}) %collective-permute-start.1) | collective-permute-done | bytes 98336 | tf_op jit(solution)/shard_map/ppermute | solution.py:240
  18.4 0.0 collective-permute-done.2
  18.5 0.7 copy-done.9
  19.2 0.0 all-gather.2.cloned.1.call-update
  19.3 1.0 fusion
  20.3 2.4 %collective-permute-start.4 = (bf16[128,512]{1,0:T(8,128)(2,1)S(1)}, bf16[128,512]{1,0:T(8,128)(2,1)S(1)}, u32[]{:S(2)}, u32[]{:S(2)}) collective-permute-start(bf16[128,512]{1,0:T(8,128)(2,1)S(1)} %get-tuple-element.33), channel_id=1, source_target_pairs={{0,2},{1,3},{2,0},{3,1},{4,6},{5,7},{6,4},{7,5},{8,10},{9,11},{10,... | collective-permute-start | bytes 393224 | tf_op jit(solution)/shard_map/ppermute | solution.py:240
  22.6 1.4 %collective-permute-start.3 = (bf16[128,512]{1,0:T(8,128)(2,1)S(1)}, bf16[128,512]{1,0:T(8,128)(2,1)S(1)}, u32[]{:S(2)}, u32[]{:S(2)}) collective-permute-start(bf16[128,512]{1,0:T(8,128)(2,1)S(1)} %get-tuple-element.33), channel_id=1, source_target_pairs={{0,1},{1,2},{2,3},{3,0},{4,5},{5,6},{6,7},{7,4},{8,9},{9,10},{10,1... | collective-permute-start | bytes 393224 | tf_op jit(solution)/shard_map/ppermute | solution.py:240
  24.0 0.7 collective-permute-start.5
  24.7 0.8 constant_dynamic-slice_fusion
  25.5 0.0 copy-start.7
  25.5 0.0 copy-start.8
  25.6 0.8 collective-permute-start.10
  26.3 2.6 %collective-permute-start.11 = (bf16[128,640]{1,0:T(8,128)(2,1)S(1)}, bf16[128,640]{1,0:T(8,128)(2,1)S(1)}, u32[]{:S(2)}, u32[]{:S(2)}) collective-permute-start(bf16[128,640]{1,0:T(8,128)(2,1)S(1)} %get-tuple-element.39), channel_id=1, source_target_pairs={{0,16},{8,24},{16,0},{24,8},{1,17},{9,25},{17,1},{25,9},{2,18},{10... | collective-permute-start | bytes 491528 | tf_op jit(solution)/shard_map/ppermute | solution.py:240
  28.9 0.0 collective-permute-done.4
  28.9 1.2 collective-permute-start.12
  30.1 0.0 collective-permute-done.3
  30.1 0.0 collective-permute-done.5
  30.1 0.1 pad_maximum_fusion.h1_own
  30.2 0.6 collective-permute-start.7
  30.8 1.5 %collective-permute-start.6 = (bf16[4,128,512]{2,1,0:T(8,128)(2,1)S(1)}, bf16[4,128,512]{2,1,0:T(8,128)(2,1)S(1)}, u32[]{:S(2)}, u32[]{:S(2)}) collective-permute-start(bf16[4,128,512]{2,1,0:T(8,128)(2,1)S(1)} %pad_maximum_fusion.h1_own), channel_id=1, source_target_pairs={{0,8},{8,16},{16,24},{24,0},{1,9},{9,17},{17,25},{25,1},{2,10},{10... | collective-permute-start | bytes 1572872 | tf_op jit(solution)/shard_map/ppermute | solution.py:240
  32.3 0.6 collective-permute-done.10
  32.9 4.5 %collective-permute-done.11 = bf16[128,640]{1,0:T(8,128)(2,1)S(1)} collective-permute-done((bf16[128,640]{1,0:T(8,128)(2,1)S(1)}, bf16[128,640]{1,0:T(8,128)(2,1)S(1)}, u32[]{:S(2)}, u32[]{:S(2)}) %collective-permute-start.11) | collective-permute-done | bytes 163872 | tf_op jit(solution)/shard_map/ppermute | solution.py:240
  37.5 0.9 collective-permute-done.12
  38.4 0.7 copy-done.12
  39.0 0.0 slice-start
  39.0 0.0 slice-start.1
  39.1 0.0 slice-start.2
  39.1 2.6 %collective-permute-start.14 = (bf16[512,512]{1,0:T(8,128)(2,1)S(1)}, bf16[512,512]{1,0:T(8,128)(2,1)S(1)}, u32[]{:S(2)}, u32[]{:S(2)}) collective-permute-start(bf16[512,512]{1,0:T(8,128)(2,1)S(1)} %pad_maximum_fusion.1.h2_own), channel_id=1, source_target_pairs={{0,3},{1,0},{2,1},{3,2},{4,7},{5,4},{6,5},{7,6},{8,11},{9,8},{10,9... | collective-permute-start | bytes 1572872 | tf_op jit(solution)/shard_map/ppermute | solution.py:240
  41.7 0.0 collective-permute-start.13
  41.7 4.5 %collective-permute-done.7.h1_left = bf16[4,128,512]{2,1,0:T(8,128)(2,1)S(1)} collective-permute-done((bf16[4,128,512]{2,1,0:T(8,128)(2,1)S(1)}, bf16[4,128,512]{2,1,0:T(8,128)(2,1)S(1)}, u32[]{:S(2)}, u32[]{:S(2)}) %collective-permute-start.7) | collective-permute-done | bytes 524320 | tf_op jit(solution)/shard_map/ppermute | solution.py:240
  46.3 2.3 %collective-permute-start.9 = (bf16[2,128,512]{2,1,0:T(8,128)(2,1)S(1)}, bf16[2,128,512]{2,1,0:T(8,128)(2,1)S(1)}, u32[]{:S(2)}, u32[]{:S(2)}) collective-permute-start(bf16[2,128,512]{2,1,0:T(8,128)(2,1)S(1)} %slice.49), channel_id=1, source_target_pairs={{0,24},{8,0},{16,8},{24,16},{1,25},{9,1},{17,9},{25,17},{2,26},{10... | collective-permute-start | bytes 786440 | tf_op jit(solution)/shard_map/ppermute | solution.py:240
  48.5 0.0 collective-permute-done.6.h1_right
  48.6 0.1 collective-permute-start.8
  48.7 0.0 collective-permute-done.14.h2_left
  48.7 2.8 %collective-permute-start.16 = (bf16[256,512]{1,0:T(8,128)(2,1)S(1)}, bf16[256,512]{1,0:T(8,128)(2,1)S(1)}, u32[]{:S(2)}, u32[]{:S(2)}) collective-permute-start(bf16[256,512]{1,0:T(8,128)(2,1)S(1)} %slice.54), channel_id=1, source_target_pairs={{0,3},{1,0},{2,1},{3,2},{4,7},{5,4},{6,5},{7,6},{8,11},{9,8},{10,9... | collective-permute-start | bytes 786440 | tf_op jit(solution)/shard_map/ppermute | solution.py:240
  51.5 0.1 collective-permute-start.15
  51.6 1.1 collective-permute-done.9.h1_far_b
  52.7 3.5 %collective-permute-done.8.h1_far_a = bf16[2,128,512]{2,1,0:T(8,128)(2,1)S(1)} collective-permute-done((bf16[2,128,512]{2,1,0:T(8,128)(2,1)S(1)}, bf16[2,128,512]{2,1,0:T(8,128)(2,1)S(1)}, u32[]{:S(2)}, u32[]{:S(2)}) %collective-permute-start.8) | collective-permute-done | bytes 262176 | tf_op jit(solution)/shard_map/ppermute | solution.py:240
  56.2 0.7 copy-done.1
  56.9 0.0 collective-permute-done.16.h2_far_b
  57.0 0.7 copy-done.3
  57.7 0.3 collective-permute-done.15.h2_far_a
  58.0 0.7 copy-done.5
  58.7 7.4 %all-gather.2.cloned.1.call-done = bf16[6144,256]{1,0:T(8,128)(2,1)} async-done(((bf16[768,256]{1,0:T(8,128)(2,1)}), bf16[6144,256]{1,0:T(8,128)(2,1)}) %all-gather.2.cloned.1.call-update) | async-done | bytes 3145744 | tf_op jit(solution)/shard_map/all_gather | solution.py:275
  66.1 0.1 pad_add_fusion.where_ref
  66.2 5.9 %collective-permute-done.17 = bf16[6144,256]{1,0:T(8,128)(2,1)} collective-permute-done((bf16[6144,256]{1,0:T(8,128)(2,1)}, bf16[6144,256]{1,0:T(8,128)(2,1)}, u32[]{:S(2)}, u32[]{:S(2)}) %collective-permute-start.17) | collective-permute-done | bytes 3145760 | tf_op jit(solution)/shard_map/ppermute | solution.py:240
  72.1 1.9 %copy-done = bf16[6144,256]{1,0:T(8,128)(2,1)S(1)} copy-done((bf16[6144,256]{1,0:T(8,128)(2,1)S(1)}, bf16[6144,256]{1,0:T(8,128)(2,1)}, u32[]{:S(2)}) %copy-start) | copy-done | bytes 3145752
  74.0 0.9 copy-done.2
  74.9 0.9 copy-done.4
  75.9 0.9 copy-done.6
  76.8 14.5 %shard_map.82 = (f32[2048,128]{1,0:T(8,128)S(1)}, bf16[2048,128]{1,0:T(8,128)(2,1)S(1)}) custom-call(s32[4]{0:T(128)S(1)} %pad_add_fusion.where_ref, s32[128]{0:T(128)S(1)} %copy-done.7, s32[16]{0:T(128)S(1)} %copy-done.8, bf16[4,128,512]{2,1,0:T(8,128)(2,1)S(1)} %pad_maximum_fusion.h1_own, bf16[4,128,512]{2,1,0:T(8,128)(2,1)S(1)} %collective-permute-done.6.h1_right, ...), custom_call_target="tpu_custom_call" | custom-call | flops 6000000000 | bytes 14000000 | tf_op jit(solution)/shard_map/pallas_call | solution.py:209
  91.3 2.2 %collective-permute-start.18 = (bf16[2048,128]{1,0:T(8,128)(2,1)S(1)}, bf16[2048,128]{1,0:T(8,128)(2,1)S(1)}, u32[]{:S(2)}, u32[]{:S(2)}) collective-permute-start(bf16[2048,128]{1,0:T(8,128)(2,1)S(1)} %get-tuple-element.30), channel_id=1, source_target_pairs={{0,4},{4,0},{1,5},{5,1},{2,6},{6,2},{3,7},{7,3},{8,12},{12,8},{9,1... | collective-permute-start | bytes 1572872 | tf_op jit(solution)/shard_map/ppermute | solution.py:240
  93.6 1.5 %collective-permute-done.18 = bf16[2048,128]{1,0:T(8,128)(2,1)S(1)} collective-permute-done((bf16[2048,128]{1,0:T(8,128)(2,1)S(1)}, bf16[2048,128]{1,0:T(8,128)(2,1)S(1)}, u32[]{:S(2)}, u32[]{:S(2)}) %collective-permute-start.18) | collective-permute-done | bytes 524320 | tf_op jit(solution)/shard_map/ppermute | solution.py:240
  95.1 0.1 add_convert_fusion
  95.2 25.9 %all_to_all.9 = bf16[32,64,128]{2,1,0:T(8,128)(2,1)S(1)} all-to-all(bf16[32,64,128]{2,1,0:T(8,128)(2,1)S(1)} %bitcast.24), channel_id=1, replica_groups=mesh['z'=8,'x'=4,'c'=2,'kvh'=4] {'z','x'}, dimensions={0} | all-to-all | bytes 1048576 | tf_op jit(solution)/shard_map/all_to_all | solution.py:301
  121.2 0.1 convert_reduce_fusion
  121.2 0.7 copy_bitcast_fusion
  (36 shorter events, 0.3 us)
Async XLA Ops:
  6.5 59.5 %all-gather.2.cloned.1.call-start = ((), (), s32[]{:S(2)}) async-start(), calls=%async_computation.1 | async-start | bytes 3538944 | tf_op jit(solution)/shard_map/all_gather | solution.py:275
  9.0 5.9 %collective-permute-start = (bf16[192,256]{1,0:T(8,128)(2,1)S(1)}, bf16[192,256]{1,0:T(8,128)(2,1)S(1)}, u32[]{:S(2)}, u32[]{:S(2)}) collective-permute-start(bf16[192,256]{1,0:T(8,128)(2,1)S(1)} %get-tuple-element.43), channel_id=1, source_target_pairs={{0,8},{8,16},{16,24},{24,0},{1,9},{9,17},{17,25},{25,1},{2,10},{10... | collective-permute-start | bytes 294920 | tf_op jit(solution)/shard_map/ppermute | solution.py:240
  10.6 7.9 %collective-permute-start.2 = (bf16[192,256]{1,0:T(8,128)(2,1)S(1)}, bf16[192,256]{1,0:T(8,128)(2,1)S(1)}, u32[]{:S(2)}, u32[]{:S(2)}) collective-permute-start(bf16[192,256]{1,0:T(8,128)(2,1)S(1)} %get-tuple-element.41), channel_id=1, source_target_pairs={{0,24},{8,0},{16,8},{24,16},{1,25},{9,1},{17,9},{25,17},{2,26},{10... | collective-permute-start | bytes 294920 | tf_op jit(solution)/shard_map/ppermute | solution.py:240
  12.3 6.1 %collective-permute-start.1 = (bf16[192,256]{1,0:T(8,128)(2,1)S(1)}, bf16[192,256]{1,0:T(8,128)(2,1)S(1)}, u32[]{:S(2)}, u32[]{:S(2)}) collective-permute-start(bf16[192,256]{1,0:T(8,128)(2,1)S(1)} %get-tuple-element.42), channel_id=1, source_target_pairs={{0,16},{8,24},{16,0},{24,8},{1,17},{9,25},{17,1},{25,9},{2,18},{10... | collective-permute-start | bytes 294920 | tf_op jit(solution)/shard_map/ppermute | solution.py:240
  18.5 0.8 copy-start.9
  20.3 8.6 %collective-permute-start.4 = (bf16[128,512]{1,0:T(8,128)(2,1)S(1)}, bf16[128,512]{1,0:T(8,128)(2,1)S(1)}, u32[]{:S(2)}, u32[]{:S(2)}) collective-permute-start(bf16[128,512]{1,0:T(8,128)(2,1)S(1)} %get-tuple-element.33), channel_id=1, source_target_pairs={{0,2},{1,3},{2,0},{3,1},{4,6},{5,7},{6,4},{7,5},{8,10},{9,11},{10,... | collective-permute-start | bytes 393224 | tf_op jit(solution)/shard_map/ppermute | solution.py:240
  22.6 7.5 %collective-permute-start.3 = (bf16[128,512]{1,0:T(8,128)(2,1)S(1)}, bf16[128,512]{1,0:T(8,128)(2,1)S(1)}, u32[]{:S(2)}, u32[]{:S(2)}) collective-permute-start(bf16[128,512]{1,0:T(8,128)(2,1)S(1)} %get-tuple-element.33), channel_id=1, source_target_pairs={{0,1},{1,2},{2,3},{3,0},{4,5},{5,6},{6,7},{7,4},{8,9},{9,10},{10,1... | collective-permute-start | bytes 393224 | tf_op jit(solution)/shard_map/ppermute | solution.py:240
  24.0 6.1 %collective-permute-start.5 = (bf16[128,512]{1,0:T(8,128)(2,1)S(1)}, bf16[128,512]{1,0:T(8,128)(2,1)S(1)}, u32[]{:S(2)}, u32[]{:S(2)}) collective-permute-start(bf16[128,512]{1,0:T(8,128)(2,1)S(1)} %get-tuple-element.33), channel_id=1, source_target_pairs={{0,3},{1,0},{2,1},{3,2},{4,7},{5,4},{6,5},{7,6},{8,11},{9,8},{10,9... | collective-permute-start | bytes 393224 | tf_op jit(solution)/shard_map/ppermute | solution.py:240
  25.5 46.6 %copy-start.7 = (s32[128]{0:T(128)S(1)}, s32[128]{0:T(128)}, u32[]{:S(2)}) copy-start(s32[128]{0:T(128)} %order_ref.1) | copy-start | bytes 1540
  25.5 46.6 %copy-start.8 = (s32[16]{0:T(128)S(1)}, s32[16]{0:T(128)}, u32[]{:S(2)}) copy-start(s32[16]{0:T(128)} %lengths_ref.1) | copy-start | bytes 196
  25.6 7.3 %collective-permute-start.10 = (bf16[128,640]{1,0:T(8,128)(2,1)S(1)}, bf16[128,640]{1,0:T(8,128)(2,1)S(1)}, u32[]{:S(2)}, u32[]{:S(2)}) collective-permute-start(bf16[128,640]{1,0:T(8,128)(2,1)S(1)} %get-tuple-element.38), channel_id=1, source_target_pairs={{0,8},{8,16},{16,24},{24,0},{1,9},{9,17},{17,25},{25,1},{2,10},{10... | collective-permute-start | bytes 491528 | tf_op jit(solution)/shard_map/ppermute | solution.py:240
  26.3 11.1 %collective-permute-start.11 = (bf16[128,640]{1,0:T(8,128)(2,1)S(1)}, bf16[128,640]{1,0:T(8,128)(2,1)S(1)}, u32[]{:S(2)}, u32[]{:S(2)}) collective-permute-start(bf16[128,640]{1,0:T(8,128)(2,1)S(1)} %get-tuple-element.39), channel_id=1, source_target_pairs={{0,16},{8,24},{16,0},{24,8},{1,17},{9,25},{17,1},{25,9},{2,18},{10... | collective-permute-start | bytes 491528 | tf_op jit(solution)/shard_map/ppermute | solution.py:240
  28.9 9.5 %collective-permute-start.12 = (bf16[128,640]{1,0:T(8,128)(2,1)S(1)}, bf16[128,640]{1,0:T(8,128)(2,1)S(1)}, u32[]{:S(2)}, u32[]{:S(2)}) collective-permute-start(bf16[128,640]{1,0:T(8,128)(2,1)S(1)} %get-tuple-element.40), channel_id=1, source_target_pairs={{0,24},{8,0},{16,8},{24,16},{1,25},{9,1},{17,9},{25,17},{2,26},{10... | collective-permute-start | bytes 491528 | tf_op jit(solution)/shard_map/ppermute | solution.py:240
  30.2 16.1 %collective-permute-start.7 = (bf16[4,128,512]{2,1,0:T(8,128)(2,1)S(1)}, bf16[4,128,512]{2,1,0:T(8,128)(2,1)S(1)}, u32[]{:S(2)}, u32[]{:S(2)}) collective-permute-start(bf16[4,128,512]{2,1,0:T(8,128)(2,1)S(1)} %pad_maximum_fusion.h1_own), channel_id=1, source_target_pairs={{0,24},{8,0},{16,8},{24,16},{1,25},{9,1},{17,9},{25,17},{2,26},{10... | collective-permute-start | bytes 1572872 | tf_op jit(solution)/shard_map/ppermute | solution.py:240
  30.8 17.7 %collective-permute-start.6 = (bf16[4,128,512]{2,1,0:T(8,128)(2,1)S(1)}, bf16[4,128,512]{2,1,0:T(8,128)(2,1)S(1)}, u32[]{:S(2)}, u32[]{:S(2)}) collective-permute-start(bf16[4,128,512]{2,1,0:T(8,128)(2,1)S(1)} %pad_maximum_fusion.h1_own), channel_id=1, source_target_pairs={{0,8},{8,16},{16,24},{24,0},{1,9},{9,17},{17,25},{25,1},{2,10},{10... | collective-permute-start | bytes 1572872 | tf_op jit(solution)/shard_map/ppermute | solution.py:240
  32.9 5.5 %copy-start.10 = (bf16[128,640]{1,0:T(8,128)(2,1)}, bf16[128,640]{1,0:T(8,128)(2,1)S(1)}, u32[]{:S(2)}) copy-start(bf16[128,640]{1,0:T(8,128)(2,1)S(1)} %collective-permute-done.10) | copy-start | bytes 491524
  37.5 0.9 copy-start.11
  38.4 0.7 copy-start.12
  39.0 27.1 %slice-start = ((bf16[128,640]{1,0:T(8,128)(2,1)}), bf16[128,128]{1,0:T(8,128)(2,1)S(1)}, s32[]{:S(2)}) async-start(bf16[128,640]{1,0:T(8,128)(2,1)} %copy-done.10), calls=%async_computation.2 | async-start | bytes 65536 | tf_op jit(solution)/shard_map/slice | solution.py:282
  39.0 27.1 %slice-start.1 = ((bf16[128,640]{1,0:T(8,128)(2,1)}), bf16[128,128]{1,0:T(8,128)(2,1)S(1)}, s32[]{:S(2)}) async-start(bf16[128,640]{1,0:T(8,128)(2,1)} %copy-done.11), calls=%async_computation.3 | async-start | bytes 65536 | tf_op jit(solution)/shard_map/slice | solution.py:282
  39.1 27.1 %slice-start.2 = ((bf16[128,640]{1,0:T(8,128)(2,1)}), bf16[128,128]{1,0:T(8,128)(2,1)S(1)}, s32[]{:S(2)}) async-start(bf16[128,640]{1,0:T(8,128)(2,1)} %copy-done.12), calls=%async_computation.4 | async-start | bytes 65536 | tf_op jit(solution)/shard_map/slice | solution.py:282
  39.1 9.6 %collective-permute-start.14 = (bf16[512,512]{1,0:T(8,128)(2,1)S(1)}, bf16[512,512]{1,0:T(8,128)(2,1)S(1)}, u32[]{:S(2)}, u32[]{:S(2)}) collective-permute-start(bf16[512,512]{1,0:T(8,128)(2,1)S(1)} %pad_maximum_fusion.1.h2_own), channel_id=1, source_target_pairs={{0,3},{1,0},{2,1},{3,2},{4,7},{5,4},{6,5},{7,6},{8,11},{9,8},{10,9... | collective-permute-start | bytes 1572872 | tf_op jit(solution)/shard_map/ppermute | solution.py:240
  41.7 9.8 %collective-permute-start.13 = (bf16[512,512]{1,0:T(8,128)(2,1)S(1)}, bf16[512,512]{1,0:T(8,128)(2,1)S(1)}, u32[]{:S(2)}, u32[]{:S(2)}) collective-permute-start(bf16[512,512]{1,0:T(8,128)(2,1)S(1)} %pad_maximum_fusion.1.h2_own), channel_id=1, source_target_pairs={{0,1},{1,2},{2,3},{3,0},{4,5},{5,6},{6,7},{7,4},{8,9},{9,10},{10,1... | collective-permute-start | bytes 1572872 | tf_op jit(solution)/shard_map/ppermute | solution.py:240
  46.3 6.4 %collective-permute-start.9 = (bf16[2,128,512]{2,1,0:T(8,128)(2,1)S(1)}, bf16[2,128,512]{2,1,0:T(8,128)(2,1)S(1)}, u32[]{:S(2)}, u32[]{:S(2)}) collective-permute-start(bf16[2,128,512]{2,1,0:T(8,128)(2,1)S(1)} %slice.49), channel_id=1, source_target_pairs={{0,24},{8,0},{16,8},{24,16},{1,25},{9,1},{17,9},{25,17},{2,26},{10... | collective-permute-start | bytes 786440 | tf_op jit(solution)/shard_map/ppermute | solution.py:240
  48.6 7.7 %collective-permute-start.8 = (bf16[2,128,512]{2,1,0:T(8,128)(2,1)S(1)}, bf16[2,128,512]{2,1,0:T(8,128)(2,1)S(1)}, u32[]{:S(2)}, u32[]{:S(2)}) collective-permute-start(bf16[2,128,512]{2,1,0:T(8,128)(2,1)S(1)} %slice.48), channel_id=1, source_target_pairs={{0,8},{8,16},{16,24},{24,0},{1,9},{9,17},{17,25},{25,1},{2,10},{10... | collective-permute-start | bytes 786440 | tf_op jit(solution)/shard_map/ppermute | solution.py:240
  48.7 8.3 %collective-permute-start.16 = (bf16[256,512]{1,0:T(8,128)(2,1)S(1)}, bf16[256,512]{1,0:T(8,128)(2,1)S(1)}, u32[]{:S(2)}, u32[]{:S(2)}) collective-permute-start(bf16[256,512]{1,0:T(8,128)(2,1)S(1)} %slice.54), channel_id=1, source_target_pairs={{0,3},{1,0},{2,1},{3,2},{4,7},{5,4},{6,5},{7,6},{8,11},{9,8},{10,9... | collective-permute-start | bytes 786440 | tf_op jit(solution)/shard_map/ppermute | solution.py:240
  51.5 6.4 %collective-permute-start.15 = (bf16[256,512]{1,0:T(8,128)(2,1)S(1)}, bf16[256,512]{1,0:T(8,128)(2,1)S(1)}, u32[]{:S(2)}, u32[]{:S(2)}) collective-permute-start(bf16[256,512]{1,0:T(8,128)(2,1)S(1)} %slice.53), channel_id=1, source_target_pairs={{0,1},{1,2},{2,3},{3,0},{4,5},{5,6},{6,7},{7,4},{8,9},{9,10},{10,1... | collective-permute-start | bytes 786440 | tf_op jit(solution)/shard_map/ppermute | solution.py:240
  56.2 0.7 copy-start.1
  56.9 0.7 copy-start.3
  58.0 0.7 copy-start.5
  66.1 6.0 %collective-permute-start.17 = (bf16[6144,256]{1,0:T(8,128)(2,1)}, bf16[6144,256]{1,0:T(8,128)(2,1)}, u32[]{:S(2)}, u32[]{:S(2)}) collective-permute-start(bf16[6144,256]{1,0:T(8,128)(2,1)} %all-gather.2.cloned.1.call-done), channel_id=1, source_target_pairs={{0,4},{4,0},{1,5},{5,1},{2,6},{6,2},{3,7},{7,3},{8,12},{12,8},{9,1... | collective-permute-start | bytes 9437192 | tf_op jit(solution)/shard_map/ppermute | solution.py:240
  72.1 1.9 %copy-start = (bf16[6144,256]{1,0:T(8,128)(2,1)S(1)}, bf16[6144,256]{1,0:T(8,128)(2,1)}, u32[]{:S(2)}) copy-start(bf16[6144,256]{1,0:T(8,128)(2,1)} %all-gather.2.cloned.1.call-done) | copy-start | bytes 9437188
  74.0 0.9 copy-start.2
  74.9 0.9 copy-start.4
  75.9 0.9 copy-start.6
  91.3 3.8 %collective-permute-start.18 = (bf16[2048,128]{1,0:T(8,128)(2,1)S(1)}, bf16[2048,128]{1,0:T(8,128)(2,1)S(1)}, u32[]{:S(2)}, u32[]{:S(2)}) collective-permute-start(bf16[2048,128]{1,0:T(8,128)(2,1)S(1)} %get-tuple-element.30), channel_id=1, source_target_pairs={{0,4},{4,0},{1,5},{5,1},{2,6},{6,2},{3,7},{7,3},{8,12},{12,8},{9,1... | collective-permute-start | bytes 1572872 | tf_op jit(solution)/shard_map/ppermute | solution.py:240
Sparse Core Ops, SparseCore 0:
  19.4 46.6 all-gather.1

commit v2 on v0

v2 whole, which is shorter than its diff:
```python
import math

import jax
import jax.numpy as jnp
from jax import lax
from jax.experimental import pallas as pl
from jax.experimental.pallas import tpu as pltpu
from jax.sharding import Mesh, PartitionSpec as P

HD = 128
BLK = 64
NDOC = 16
CHUNK = 512
LANES = 128
ROW_BLOCKS = 8
MOST_EXTRA = ROW_BLOCKS * 4
SCALE = 1.0 / math.sqrt(HD)
LOG2E = 1.4426950408889634
TOKENS = 8192
BF16 = jnp.bfloat16
F32 = jnp.float32
I32 = jnp.int32


def prepare_kernel(
    where_ref,
    hidden_hbm,
    query_hbm,
    probe_hbm,
    key_hbm,
    value_hbm,
    upstream_hbm,
    pack0_ref,
    pack1_ref,
    pack2_ref,
    pack3_ref,
    keep_ref,
    send_ref,
    hidden_ref,
    query_ref,
    probe_ref,
    key_ref,
    value_ref,
    upstream_ref,
    sems,
):
    x, c = where_ref[1], where_ref[2]
    copies = [
        pltpu.make_async_copy(src, dst, sems.at[i])
        for i, (src, dst) in enumerate(
            (
                (query_hbm, query_ref),
                (probe_hbm, probe_ref),
                (key_hbm, key_ref),
                (value_hbm, value_ref),
                (upstream_hbm, upstream_ref),
                (hidden_hbm, hidden_ref),
            )
        )
    ]
    for copy in copies:
        copy.start()
    for copy in copies[:5]:
        copy.wait()
    for dx, pack in enumerate((pack0_ref, pack1_ref, pack2_ref, pack3_ref)):
        columns = pl.ds(pl.multiple_of(lax.rem(x + dx, 4) * HD, HD), HD)
        pack[0:64, 0:128] = query_ref[:, columns]
        pack[0:64, 128:256] = probe_ref[:, columns]
        pack[64:192, 0:128] = key_ref[...]
        pack[64:192, 128:256] = value_ref[...]
        pack[192:256, 0:128] = upstream_ref[0:64, columns]
        pack[192:256, 128:256] = upstream_ref[64:128, columns]
    copies[5].wait()
    low = lax.broadcasted_iota(I32, (128, 128), 1) < 64
    for k in range(4):
        a = hidden_ref[:, 256 * k : 256 * k + 128].astype(F32)
        b = hidden_ref[:, 256 * k + 128 : 256 * k + 256].astype(F32)
        first = jnp.where(low, a, pltpu.roll(b, 64, 1))
        second = jnp.where(low, pltpu.roll(a, 64, 1), b)
        cut = slice(128 * k, 128 * k + 128)
        keep_ref[:, cut] = jnp.where(c == 0, first, second).astype(BF16)
        send_ref[:, cut] = jnp.where(c == 0, second, first).astype(BF16)


def hidden_piece(refs, r, s):
    stack, right, left, far_a, far_b = refs
    if r == 2:
        return far_a[s] if s < 2 else far_b[s - 2]
    return (stack, right, None, left)[r][s]


def project_kernel(*refs):
    where_ref, hidden = refs[0], refs[1:6]
    packs, far_r, far_l = refs[6:13], refs[13], refs[14]
    keep_ref, send_ref, weights, total = refs[15:]
    z, x, c, y = where_ref[0], where_ref[1], where_ref[2], where_ref[3]

    def place(pack, dz, places=(0, 1, 2, 3)):
        for i, dx in enumerate(places):
            weights[lax.rem(z - dz + 8, 8), lax.rem(x - dx + 4, 4)] = pack[
                i * 192 : i * 192 + 64, :
            ]

    for pack, dz in zip(packs, (0, 1, 7, 2, 6, 3, 5)):
        place(pack, dz)
    place(far_r, 4, (0, 1))
    place(far_l, 4, (2, 3))

    total[...] = jnp.zeros((4, 256, 256), F32)
    for r in range(4):
        for s in range(4):
            dx = jnp.where(c == 0, r, s)
            dy = jnp.where(c == 0, s, r)
            group = lax.rem(y - dy + 4, 4)
            w = weights[pl.ds(group * 2, 2)].reshape(512, 256)
            total[dx] += jnp.dot(hidden_piece(hidden, r, s), w, preferred_element_type=F32)
    keep_ref[...] = total[:, 0:128, :]
    send_ref[...] = total[:, 128:256, :]


def attend_kernel(*refs):
    where_ref, order_ref, lengths_ref, qt_keep, qt_received = refs[:5]
    packs, far_r, far_l = refs[5:12], refs[12], refs[13]
    swap_a, swap_b, swap_c = refs[14:17]
    upstream_ref, second_ref = refs[17:19]
    (
        keys_values,
        query_tangent,
        starts,
        exp_buf,
        tan_buf,
        val_buf,
        sums,
        stats,
        second,
        ends,
        extra_block,
        extra_row,
    ) = refs[19:]
    z, x, c = where_ref[0], where_ref[1], where_ref[2]

    keys_values[0:CHUNK, :] = jnp.zeros((CHUNK, 256), BF16)

    def place(src, first_row, step, dz, cc, places=(0, 1, 2, 3)):
        zz = lax.rem(z - dz + 8, 8)
        for i, dx in enumerate(places):
            block = ((zz * 4 + lax.rem(x - dx + 4, 4)) * 2 + cc) * 2
            for b in range(2):
                target = pl.multiple_of(CHUNK + order_ref[block + b] * BLK, BLK)
                row = first_row + i * step + b * 64
                keys_values[pl.ds(target, BLK), :] = src[row : row + 64, :]

    for pack, dz in zip(packs, (0, 1, 7, 2, 6, 3, 5)):
        place(pack, 64, 192, dz, c)
    place(far_r, 64, 192, 4, c, (0, 1))
    place(far_l, 64, 192, 4, c, (2, 3))
    for i, dz in enumerate((0, 1, 7)):
        place(swap_a, i * 512, 128, dz, 1 - c)
    for i, dz in enumerate((2, 6, 3, 5)):
        place(swap_b, i * 512, 128, dz, 1 - c)
    place(swap_c, 0, 128, 4, 1 - c)

    for rb in range(ROW_BLOCKS):
        rows = slice((rb % 2) * 64, (rb % 2) * 64 + 64)
        both = (qt_keep[rb // 2, rows, :] + qt_received[rb // 2, rows, :]).astype(BF16)
        query_tangent[rb, 0:64, :] = both[:, 0:128]
        query_tangent[rb, 64:128, :] = both[:, 128:256]

    total = jnp.int32(0)
    for d in range(NDOC):
        total = total + lengths_ref[d]
        ends[d] = total
    packed_block = []
    extras = jnp.int32(0)
    sub = lax.broadcasted_iota(I32, (BLK, LANES), 0)
    lane = lax.broadcasted_iota(I32, (BLK, LANES), 1)
    for rb in range(ROW_BLOCKS):
        xx = lax.rem(x - rb // 2 + 4, 4)
        p = order_ref[((z * 4 + xx) * 2 + c) * 2 + rb % 2]
        packed_block.append(p)
        first = jnp.int32(0)
        start = jnp.zeros((BLK, LANES), I32)
        for d in range(NDOC):
            end = ends[d]
            first = jnp.where(end <= p * BLK, end, first)
            start = jnp.where(end <= p * BLK + sub, end, start)
        starts[rb] = start
        more = (p * BLK + BLK - first + CHUNK - 1) // CHUNK - 1

        def note(j, at, rb=rb, p=p):
            extra_block[at] = rb
            extra_row[at] = p * BLK + BLK - CHUNK * (j + 1)
            return at + 1

        extras = lax.fori_loop(0, more, note, extras)
    extra_block[extras] = ROW_BLOCKS
    extra_row[extras] = 0
    sums[ROW_BLOCKS] = jnp.zeros((4, BLK, LANES), F32)
    stats[ROW_BLOCKS] = jnp.zeros((4, BLK, LANES), F32)
    second[ROW_BLOCKS] = jnp.zeros((BLK, LANES), F32)
    starts[ROW_BLOCKS] = jnp.zeros((BLK, LANES), I32)

    def dot_t(a, b):
        return lax.dot_general(a, b, (((1,), (1,)), ((), ())), preferred_element_type=F32)

    def scored(rb, source, row, slot, last_pos):
        kv = keys_values[pl.ds(pl.multiple_of(row, BLK), CHUNK), :]
        st = dot_t(query_tangent[source], kv[:, 0:128])
        v = dot_t(upstream_ref[source], kv[:, 128:256])
        start = starts[rb]
        parts = [None] * 4
        for i in range(CHUNK // LANES):
            cut = slice(i * LANES, (i + 1) * LANES)
            key_pos = row - CHUNK + i * LANES + lane
            allowed = key_pos >= start
            if last_pos is not None:
                allowed = allowed & (key_pos <= last_pos)
            e = jnp.where(allowed, jnp.exp2(st[0:64, cut] * (SCALE * LOG2E)), 0.0)
            t_i, v_i = st[64:128, cut], v[:, cut]
            exp_buf[slot, :, cut] = e
            tan_buf[slot, :, cut] = t_i
            val_buf[slot, :, cut] = v_i
            ev = e * v_i
            for n, term in enumerate((e, ev, e * t_i, ev * t_i)):
                parts[n] = term if parts[n] is None else parts[n] + term
        return parts

    def weighted(rb, row, slot):
        value_mean, tangent_mean, drift, inverse = [stats[rb, n] for n in range(4)]
        pieces = []
        for i in range(CHUNK // LANES):
            cut = slice(i * LANES, (i + 1) * LANES)
            w = (exp_buf[slot, :, cut] * inverse) * (
                (tan_buf[slot, :, cut] - tangent_mean) * (val_buf[slot, :, cut] - value_mean)
                - drift
            )
            pieces.append(w.astype(BF16))
        keys = keys_values[pl.ds(pl.multiple_of(row, BLK), CHUNK), 0:128]
        return jnp.dot(jnp.concatenate(pieces, axis=1), keys, preferred_element_type=F32)

    for rb in range(ROW_BLOCKS):
        row = packed_block[rb] * BLK + BLK
        parts = scored(rb, rb, row, rb, packed_block[rb] * BLK + sub)
        for n in range(4):
            sums[rb, n] = parts[n]

    pairs = (extras + 1) // 2

    def extra_scores(i, carry):
        for item in (2 * i, 2 * i + 1):
            rb = extra_block[item]
            row = extra_row[item]
            parts = scored(rb, jnp.minimum(rb, ROW_BLOCKS - 1), row, ROW_BLOCKS + item, None)
            for n in range(4):
                sums[rb, n] += parts[n]
        return carry

    lax.fori_loop(0, pairs, extra_scores, 0)

    for rb in range(ROW_BLOCKS):
        weight_sum, value_sum, tangent_sum, joint_sum = [
            jnp.sum(sums[rb, n], axis=1, keepdims=True) for n in range(4)
        ]
        inverse = 1.0 / weight_sum
        value_mean = value_sum * inverse
        tangent_mean = tangent_sum * inverse
        drift = joint_sum * inverse - tangent_mean * value_mean
        for n, stat in enumerate((value_mean, tangent_mean, drift, inverse)):
            stats[rb, n] = jnp.broadcast_to(stat, (BLK, LANES))
    for rb in range(ROW_BLOCKS):
        second[rb] = weighted(rb, packed_block[rb] * BLK + BLK, rb)

    def extra_weights(i, carry):
        for item in (2 * i, 2 * i + 1):
            rb = extra_block[item]
            second[rb] += weighted(rb, extra_row[item], ROW_BLOCKS + item)
        return carry

    lax.fori_loop(0, pairs, extra_weights, 0)

    second_ref[...] = (
        second[0:ROW_BLOCKS].reshape(512, 128) * (SCALE * SCALE)
    ).astype(BF16)


def curvature_kernel(*refs):
    where_ref, hidden = refs[0], refs[1:6]
    second_own, second_other, out_ref, second_t, total = refs[6:]
    c, y = where_ref[2], where_ref[3]
    for dx in range(4):
        rows = slice(dx * 128, dx * 128 + 128)
        both = jnp.concatenate([second_own[rows, :], second_other[rows, :]], axis=0)
        second_t[dx] = both.astype(F32).T.astype(BF16)
    total[...] = jnp.zeros((4, 128, 512), F32)
    for r in range(4):
        for s in range(4):
            dx = jnp.where(c == 0, r, s)
            dy = jnp.where(c == 0, s, r)
            group = lax.rem(y - dy + 4, 4)
            total[group] += jnp.dot(
                second_t[dx], hidden_piece(hidden, r, s), preferred_element_type=F32
            )
    for g in range(4):
        out_ref[g * 512 : g * 512 + 512, :] = total[g].T.astype(BF16)


def gather_kernel(*refs):
    packs, (mine_ref, upstream_ref) = refs[:4], refs[4:]
    for dx, pack in enumerate(packs):
        mine_ref[dx * 192 : dx * 192 + 192, :] = pack[0:192, :]
        upstream_ref[2 * dx] = pack[192:256, 0:128]
        upstream_ref[2 * dx + 1] = pack[192:256, 128:256]


def keys_kernel(*refs):
    packs, out_ref = refs[:-1], refs[-1]
    at = 0
    for pack in packs:
        for dx in range(pack.shape[0] // 192):
            out_ref[at : at + 128, :] = pack[dx * 192 + 64 : dx * 192 + 192, :]
            at += 128


SMEM_SPEC = pl.BlockSpec(memory_space=pltpu.SMEM)
VMEM_SPEC = pl.BlockSpec(memory_space=pltpu.VMEM)


def call(kernel, scalars, arrays, out_shape, scratch, mebibytes, flops):
    return pl.pallas_call(
        kernel,
        out_shape=out_shape,
        in_specs=[SMEM_SPEC] * len(scalars) + [VMEM_SPEC] * len(arrays),
        out_specs=jax.tree.map(lambda _: VMEM_SPEC, out_shape),
        scratch_shapes=scratch,
        compiler_params=pltpu.CompilerParams(vmem_limit_bytes=mebibytes * 1024 * 1024),
        cost_estimate=pl.CostEstimate(flops=flops, bytes_accessed=8_000_000, transcendentals=0),
    )(*scalars, *arrays)


def prepare(where, arrays):
    any_spec = pl.BlockSpec(memory_space=pl.ANY)
    pack = jax.ShapeDtypeStruct((256, 256), BF16)
    half = jax.ShapeDtypeStruct((128, 512), BF16)
    return pl.pallas_call(
        prepare_kernel,
        out_shape=(pack,) * 4 + (half,) * 2,
        in_specs=[SMEM_SPEC] + [any_spec] * 6,
        out_specs=(VMEM_SPEC,) * 6,
        scratch_shapes=[pltpu.VMEM(a.shape, BF16) for a in arrays]
        + [pltpu.SemaphoreType.DMA((6,))],
        compiler_params=pltpu.CompilerParams(vmem_limit_bytes=60 * 1024 * 1024),
        cost_estimate=pl.CostEstimate(flops=1_000_000, bytes_accessed=600_000, transcendentals=0),
    )(where, *arrays)


def gather(packs):
    shapes = (
        jax.ShapeDtypeStruct((768, 256), BF16),
        jax.ShapeDtypeStruct((ROW_BLOCKS, BLK, HD), BF16),
    )
    return call(gather_kernel, (), packs, shapes, [], 2, 100_000)


def keys_of(packs):
    rows = sum(p.shape[0] // 192 * 128 for p in packs)
    return call(keys_kernel, (), packs, jax.ShapeDtypeStruct((rows, 256), BF16), [], 2, 100_000)


def project(where, arrays):
    shape = jax.ShapeDtypeStruct((4, 128, 256), F32)
    scratch = [pltpu.VMEM((8, 4, 64, 256), BF16), pltpu.VMEM((4, 256, 256), F32)]
    return call(project_kernel, (where,), arrays, (shape, shape), scratch, 6, 1_000_000_000)


def attend(scalars, arrays):
    scratch = [
        pltpu.VMEM((CHUNK + TOKENS, 256), BF16),
        pltpu.VMEM((ROW_BLOCKS, 128, 128), BF16),
        pltpu.VMEM((ROW_BLOCKS + 1, BLK, LANES), I32),
        pltpu.VMEM((ROW_BLOCKS + MOST_EXTRA + 1, BLK, CHUNK), F32),
        pltpu.VMEM((ROW_BLOCKS + MOST_EXTRA + 1, BLK, CHUNK), F32),
        pltpu.VMEM((ROW_BLOCKS + MOST_EXTRA + 1, BLK, CHUNK), F32),
        pltpu.VMEM((ROW_BLOCKS + 1, 4, BLK, LANES), F32),
        pltpu.VMEM((ROW_BLOCKS + 1, 4, BLK, LANES), F32),
        pltpu.VMEM((ROW_BLOCKS + 1, BLK, LANES), F32),
        pltpu.SMEM((NDOC,), I32),
        pltpu.SMEM((MOST_EXTRA + 1,), I32),
        pltpu.SMEM((MOST_EXTRA + 1,), I32),
    ]
    shape = jax.ShapeDtypeStruct((512, 128), BF16)
    return call(attend_kernel, scalars, arrays, shape, scratch, 26, 2_000_000_000)


def curvature(where, arrays):
    shape = jax.ShapeDtypeStruct((2048, 128), BF16)
    scratch = [pltpu.VMEM((4, 128, 256), BF16), pltpu.VMEM((4, 128, 512), F32)]
    return call(curvature_kernel, (where,), arrays, shape, scratch, 6, 600_000_000)


def shift(value, axis, size, step):
    return lax.ppermute(value, axis, [(i, (i + step) % size) for i in range(size)])


def swap(value):
    return shift(value, "c", 2, 1)


def shift_plane(value, step, first):
    pairs = []
    for i in range(4):
        for c in range(2):
            for j in range(4):
                along_y = (c == 0) == first
                ii, jj = (i, (j + step) % 4) if along_y else ((i + step) % 4, j)
                pairs.append(((i * 2 + c) * 4 + j, (ii * 2 + c) * 4 + jj))
    return lax.ppermute(value, ("x", "c", "kvh"), pairs)


def per_device(
    hidden, query_weight, probe_vector, key_rows, value_rows, upstream, lengths, block_order
):
    z = lax.axis_index("z")
    x = lax.axis_index("x")
    c = lax.axis_index("c")
    y = lax.axis_index("kvh")
    where = jnp.stack([z, x, c, y]).astype(I32)

    *packs, keep, send = prepare(
        where, (hidden, query_weight, probe_vector, key_rows, value_rows, upstream)
    )
    base = jnp.concatenate([keep, swap(send)], axis=0)
    *packs, base = lax.optimization_barrier((*packs, base))
    packs = [packs[0]] + [shift(packs[dx], "x", 4, dx) for dx in (1, 2, 3)]
    mine, upstream_rows = gather(packs)
    right_1, left_1 = shift(mine, "z", 8, 1), shift(mine, "z", 8, 7)

    stack = jnp.stack([base] + [shift_plane(base, s, True) for s in (1, 2, 3)])
    hid_right = shift_plane(stack, 1, False)
    hid_left = shift_plane(stack, 3, False)

    right_1, left_1, _ = lax.optimization_barrier((right_1, left_1, stack))
    right_2, left_2 = shift(right_1, "z", 8, 1), shift(left_1, "z", 8, 7)

    right_3, left_3 = shift(right_2, "z", 8, 1), shift(left_2, "z", 8, 7)
    swap_a = swap(keys_of((mine, right_1, left_1)))

    hid_far_a = shift_plane(hid_right[:2], 1, False)
    hid_far_b = shift_plane(hid_left[2:], 3, False)
    right_3, left_3, _ = lax.optimization_barrier((right_3, left_3, hid_right))
    far_r, far_l = shift(right_3[:384], "z", 8, 1), shift(left_3[384:], "z", 8, 7)
    swap_b = swap(keys_of((right_2, left_2, right_3, left_3)))
    pieces = (stack, hid_right, hid_left, hid_far_a, hid_far_b)

    ring = (mine, right_1, left_1, right_2, left_2, right_3, left_3)
    qt_keep, qt_send = project(where, (*pieces, *ring, far_r, far_l))
    qt_received = swap(qt_send)
    swap_c = swap(keys_of((far_r, far_l)))
    second_own = attend(
        (where, block_order, lengths),
        (
            qt_keep,
            qt_received,
            *ring,
            far_r,
            far_l,
            swap_a,
            swap_b,
            swap_c,
            upstream_rows,
        ),
    )
    second_other = swap(second_own)
    partial = curvature(where, (*pieces, second_own, second_other))
    shares = lax.all_to_all(partial, ("z", "x"), 0, 0, tiled=True)
    summed = jnp.sum(shares.reshape(8, 4, 64, 128).astype(F32), axis=0)
    return summed.transpose(1, 0, 2).reshape(64, 512)


def solution(mesh):
    fine = Mesh(mesh.devices.reshape(8, 4, 2, 4), ("z", "x", "c", "kvh"))
    ctx = ("z", "x", "c")
    split = P(ctx, "kvh")
    return jax.shard_map(
        per_device,
        mesh=fine,
        in_specs=(split,) * 6 + (P(), P()),
        out_specs=split,
        check_vma=False,
    )
```

time: 671 us -> 110 us (0.16)
  waiting for transfers between devices: 487 us -> 34.3 us
  matrix products: 135 us -> 0 us
  starting transfers between devices: 0.19 us -> 33.7 us
  blocking collectives: 0 us -> 24 us
  other arithmetic: 19.4 us -> 1.84 us
  between operations: 13.6 us -> 0.22 us
  Pallas kernels: 0 us -> 12.6 us
  local copies, waits for them, and re-layouts: 11 us -> 1.45 us
    all_gather x5 -> x0, waiting for transfers between devices: 335 us -> none  [the longest x1 83 us: per_device(): lax.all_gather(query_weight, 'ctx', axis=0, tiled=True)]
    reduce_scatter x1 -> x0, waiting for transfers between devices: 149 us -> none  [per_device(): lax.psum_scatter(lax.dot_general(features_all, second_order, (((0,), (0,)...]
    dot_general x99 -> x0, matrix products: 135 us -> none  [the longest x32 40 us: scored_of(): jnp.einsum('rkgd,nkd->rkgn', query_heads, key_heads, preferred_element_ty...]
    ppermute x0 -> x24, waiting for transfers between devices: none -> 34.3 us  [the longest x17 34.3 us: shift(): lax.ppermute(value, axis, [(i, (i + step) % size) for i in range(size)])]
    ppermute x0 -> x24, starting transfers between devices: none -> 33.7 us  [the longest x17 22 us: shift(): lax.ppermute(value, axis, [(i, (i + step) % size) for i in range(size)])]
    all_to_all x0 -> x1, blocking collectives: none -> 24 us  [per_device(): shares = lax.all_to_all(partial, ('z', 'x'), 0, 0, tiled=True)]
    pallas_call x0 -> x8, Pallas kernels: none -> 12.6 us  [the longest x7 9.89 us: call(): pl.pallas_call(kernel, out_shape=out_shape, in_specs=[SMEM_SPEC] * len(sc...]
    reduce_sum x66 -> x1, other arithmetic: 11.2 us -> 0.08 us  [per_device(): summed = jnp.sum(shares.reshape(8, 4, 64, 128).astype(F32), axis=0)]
  transfers between devices with their start and end apart: 6 -> 24, of which waited for: 6 -> 8; matrix products, arithmetic and copies ran while one was open for 1% -> 0% of each run, Pallas kernels for 0% -> 3%
where the time goes in v2:
time: 110 us; the launch traced here: 108 us
  waiting for transfers between devices  34.3 us (31%)
  starting transfers between devices  33.7 us (31%)
  blocking collectives  24 us (22%)
  Pallas kernels  12.6 us (11%)
  other arithmetic  1.84 us (2%)
  local copies, waits for them, and re-layouts  1.45 us (1%)
    ppermute x17, waiting for transfers between devices, shift(): lax.ppermute(value, axis, [(i, (i + step) % size) for i in range(size)])  34.3 us
    all_to_all x1, blocking collectives, per_device(): shares = lax.all_to_all(partial, ('z', 'x'), 0, 0, tiled=True)  24 us
    ppermute x17, starting transfers between devices, shift(): lax.ppermute(value, axis, [(i, (i + step) % size) for i in range(size)])  22 us
    ppermute x7, starting transfers between devices, shift_plane(): return lax.ppermute(value, ('x', 'c', 'kvh'), pairs)  11.8 us
    pallas_call x7, Pallas kernels, call(): pl.pallas_call(kernel, out_shape=out_shape, in_specs=[SMEM_SPEC] * len(sc...  9.89 us
    pallas_call x1, Pallas kernels, prepare(): pl.pallas_call(prepare_kernel, out_shape=(pack,) * 4 + (half,) * 2, in_sp...  2.71 us
  transfers between devices with their start and end apart: 24, of which 8 were waited for; matrix products, arithmetic and copies ran while one was open for 0% of the time, Pallas kernels for 3%

profile of v2, /device:TPU:8, one launch (start us, length us, event | category | flops | bytes accessed | tf_op | source)
XLA Modules:
  0.0 108.2 jit_solution(12046236493428396083)
XLA Ops:
  0.0 0.6 pad_add_fusion.where_ref.refs_0_
  0.6 2.7 %shard_map.82 = (bf16[256,256]{1,0:T(8,128)(2,1)}, bf16[256,256]{1,0:T(8,128)(2,1)}, bf16[256,256]{1,0:T(8,128)(2,1)}, bf16[256,256]{1,0:T(8,128)(2,1)}, bf16[12...) custom-call(s32[4]{0:T(128)} %pad_add_fusion.where_ref.refs_0_, bf16[128,1024]{1,0:T(8,128)(2,1)} %hidden_hbm.1, ...), custom_call_target="tpu_custom_call" | custom-call | flops 1000000 | bytes 600000 | tf_op jit(solution)/shard_map/pallas_call | solution.py:344
  3.4 0.1 collective-permute-start
  3.5 1.5 %collective-permute-done = bf16[128,512]{1,0:T(8,128)(2,1)S(1)} collective-permute-done((bf16[128,512]{1,0:T(8,128)(2,1)}, bf16[128,512]{1,0:T(8,128)(2,1)S(1)}, u32[]{:S(2)}, u32[]{:S(2)}) %collective-permute-start) | collective-permute-done | bytes 131104 | tf_op jit(solution)/shard_map/ppermute | solution.py:401
  5.0 1.0 pad_maximum_fusion.1
  6.0 0.0 copy-done.6
  6.0 2.8 %collective-permute-start.10 = (bf16[256,256]{1,0:T(8,128)(2,1)S(1)}, bf16[256,256]{1,0:T(8,128)(2,1)S(1)}, u32[]{:S(2)}, u32[]{:S(2)}) collective-permute-start(bf16[256,256]{1,0:T(8,128)(2,1)S(1)} %copy-done.6), channel_id=1, source_target_pairs={{0,24},{8,0},{16,8},{24,16},{1,25},{9,1},{17,9},{25,17},{2,26},{10... | collective-permute-start | bytes 393224 | tf_op jit(solution)/shard_map/ppermute | solution.py:401
  8.9 1.6 %collective-permute-start.1 = (bf16[256,512]{1,0:T(8,128)(2,1)S(1)}, bf16[256,512]{1,0:T(8,128)(2,1)S(1)}, u32[]{:S(2)}, u32[]{:S(2)}) collective-permute-start(bf16[256,512]{1,0:T(8,128)(2,1)S(1)} %pad_maximum_fusion.1), channel_id=1, source_target_pairs={{0,1},{1,2},{2,3},{3,0},{4,12},{5,13},{6,14},{7,15},{8,9},{9,10},{... | collective-permute-start | bytes 786440 | tf_op jit(solution)/shard_map/ppermute | solution.py:416
  10.4 0.9 collective-permute-start.2
  11.4 2.4 %collective-permute-start.3 = (bf16[256,512]{1,0:T(8,128)(2,1)S(1)}, bf16[256,512]{1,0:T(8,128)(2,1)S(1)}, u32[]{:S(2)}, u32[]{:S(2)}) collective-permute-start(bf16[256,512]{1,0:T(8,128)(2,1)S(1)} %pad_maximum_fusion.1), channel_id=1, source_target_pairs={{0,3},{1,0},{2,1},{3,2},{4,28},{5,29},{6,30},{7,31},{8,11},{9,8},{... | collective-permute-start | bytes 786440 | tf_op jit(solution)/shard_map/ppermute | solution.py:416
  13.8 0.0 collective-permute-start.8
  13.8 0.0 collective-permute-done.10.refs_3_
  13.8 2.3 %collective-permute-start.9 = (bf16[256,256]{1,0:T(8,128)(2,1)S(1)}, bf16[256,256]{1,0:T(8,128)(2,1)S(1)}, u32[]{:S(2)}, u32[]{:S(2)}) collective-permute-start(bf16[256,256]{1,0:T(8,128)(2,1)S(1)} %copy-done.4), channel_id=1, source_target_pairs={{0,16},{8,24},{16,0},{24,8},{1,17},{9,25},{17,1},{25,9},{2,18},{10... | collective-permute-start | bytes 393224 | tf_op jit(solution)/shard_map/ppermute | solution.py:401
  16.1 7.7 %collective-permute-done.8.refs_1_ = bf16[256,256]{1,0:T(8,128)(2,1)S(1)} collective-permute-done((bf16[256,256]{1,0:T(8,128)(2,1)S(1)}, bf16[256,256]{1,0:T(8,128)(2,1)S(1)}, u32[]{:S(2)}, u32[]{:S(2)}) %collective-permute-start.8) | collective-permute-done | bytes 131104 | tf_op jit(solution)/shard_map/ppermute | solution.py:401
  23.8 0.0 collective-permute-done.9.refs_2_
  23.8 2.0 %collective-permute-start.11 = (bf16[768,256]{1,0:T(8,128)(2,1)S(1)}, bf16[768,256]{1,0:T(8,128)(2,1)S(1)}, u32[]{:S(2)}, u32[]{:S(2)}) collective-permute-start(bf16[768,256]{1,0:T(8,128)(2,1)S(1)} %get-tuple-element.35.refs_6_.refs_0_.refs_5_), channel_id=1, source_target_pairs={{0,32},{32,64},{64,96},{96,128},{128,160},{160,192},{192,224},{224... | collective-permute-start | bytes 1179656 | tf_op jit(solution)/shard_map/ppermute | solution.py:401
  25.8 4.0 %collective-permute-start.12 = (bf16[768,256]{1,0:T(8,128)(2,1)S(1)}, bf16[768,256]{1,0:T(8,128)(2,1)S(1)}, u32[]{:S(2)}, u32[]{:S(2)}) collective-permute-start(bf16[768,256]{1,0:T(8,128)(2,1)S(1)} %get-tuple-element.35.refs_6_.refs_0_.refs_5_), channel_id=1, source_target_pairs={{0,224},{32,0},{64,32},{96,64},{128,96},{160,128},{192,160},{224,1... | collective-permute-start | bytes 1179656 | tf_op jit(solution)/shard_map/ppermute | solution.py:401
  29.8 0.0 collective-permute-done.1
  29.8 0.0 collective-permute-done.2
  29.8 0.0 collective-permute-done.3
  29.9 0.1 pad_maximum_fusion.refs_1_
  30.0 0.1 collective-permute-start.4
  30.1 3.2 %collective-permute-start.5 = (bf16[4,256,512]{2,1,0:T(8,128)(2,1)S(1)}, bf16[4,256,512]{2,1,0:T(8,128)(2,1)S(1)}, u32[]{:S(2)}, u32[]{:S(2)}) collective-permute-start(bf16[4,256,512]{2,1,0:T(8,128)(2,1)S(1)} %pad_maximum_fusion.refs_1_), channel_id=1, source_target_pairs={{0,24},{1,25},{2,26},{3,27},{4,7},{5,4},{6,5},{7,6},{8,0},{9,1},{1... | collective-permute-start | bytes 3145736 | tf_op jit(solution)/shard_map/ppermute | solution.py:416
  33.3 5.3 %collective-permute-done.11.refs_7_.refs_1_.refs_6_ = bf16[768,256]{1,0:T(8,128)(2,1)S(1)} collective-permute-done((bf16[768,256]{1,0:T(8,128)(2,1)S(1)}, bf16[768,256]{1,0:T(8,128)(2,1)S(1)}, u32[]{:S(2)}, u32[]{:S(2)}) %collective-permute-start.11) | collective-permute-done | bytes 393248 | tf_op jit(solution)/shard_map/ppermute | solution.py:401
  38.7 0.0 collective-permute-done.12.refs_8_.refs_2_.refs_7_
  38.7 0.0 collective-permute-start.13
  38.7 3.2 %collective-permute-start.14 = (bf16[768,256]{1,0:T(8,128)(2,1)S(1)}, bf16[768,256]{1,0:T(8,128)(2,1)S(1)}, u32[]{:S(2)}, u32[]{:S(2)}) collective-permute-start(bf16[768,256]{1,0:T(8,128)(2,1)S(1)} %collective-permute-done.12.refs_8_.refs_2_.refs_7_), channel_id=1, source_target_pairs={{0,224},{32,0},{64,32},{96,64},{128,96},{160,128},{192,160},{224,1... | collective-permute-start | bytes 1179656 | tf_op jit(solution)/shard_map/ppermute | solution.py:401
  41.9 8.0 %collective-permute-done.13.refs_9_.refs_0_.refs_8_ = bf16[768,256]{1,0:T(8,128)(2,1)S(1)} collective-permute-done((bf16[768,256]{1,0:T(8,128)(2,1)S(1)}, bf16[768,256]{1,0:T(8,128)(2,1)S(1)}, u32[]{:S(2)}, u32[]{:S(2)}) %collective-permute-start.13) | collective-permute-done | bytes 393248 | tf_op jit(solution)/shard_map/ppermute | solution.py:401
  49.9 0.0 collective-permute-start.15
  49.9 0.0 collective-permute-done.14.refs_10_.refs_1_.refs_9_
  49.9 3.2 %collective-permute-start.16 = (bf16[768,256]{1,0:T(8,128)(2,1)S(1)}, bf16[768,256]{1,0:T(8,128)(2,1)S(1)}, u32[]{:S(2)}, u32[]{:S(2)}) collective-permute-start(bf16[768,256]{1,0:T(8,128)(2,1)S(1)} %collective-permute-done.14.refs_10_.refs_1_.refs_9_), channel_id=1, source_target_pairs={{0,224},{32,0},{64,32},{96,64},{128,96},{160,128},{192,160},{224,1... | collective-permute-start | bytes 1179656 | tf_op jit(solution)/shard_map/ppermute | solution.py:401
  53.2 0.0 collective-permute-done.4.refs_2_
  53.2 0.3 collective-permute-start.6
  53.5 0.0 collective-permute-done.5.refs_3_
  53.5 3.3 %collective-permute-start.7 = (bf16[2,256,512]{2,1,0:T(8,128)(2,1)S(1)}, bf16[2,256,512]{2,1,0:T(8,128)(2,1)S(1)}, u32[]{:S(2)}, u32[]{:S(2)}) collective-permute-start(bf16[2,256,512]{2,1,0:T(8,128)(2,1)S(1)} %slice.17), channel_id=1, source_target_pairs={{0,24},{1,25},{2,26},{3,27},{4,7},{5,4},{6,5},{7,6},{8,0},{9,1},{1... | collective-permute-start | bytes 1572872 | tf_op jit(solution)/shard_map/ppermute | solution.py:416
  56.8 3.5 %collective-permute-done.15.refs_11_.refs_2_.refs_10_ = bf16[768,256]{1,0:T(8,128)(2,1)S(1)} collective-permute-done((bf16[768,256]{1,0:T(8,128)(2,1)S(1)}, bf16[768,256]{1,0:T(8,128)(2,1)S(1)}, u32[]{:S(2)}, u32[]{:S(2)}) %collective-permute-start.15) | collective-permute-done | bytes 393248 | tf_op jit(solution)/shard_map/ppermute | solution.py:401
  60.3 0.0 collective-permute-done.16.refs_12_.refs_3_.refs_11_
  60.3 0.1 shard_map.86
  60.4 0.1 collective-permute-start.21
  60.5 0.1 collective-permute-start.17
  60.6 0.0 copy-start.1
  60.6 3.3 %collective-permute-start.18 = (bf16[384,256]{1,0:T(8,128)(2,1)S(1)}, bf16[384,256]{1,0:T(8,128)(2,1)S(1)}, u32[]{:S(2)}, u32[]{:S(2)}) collective-permute-start(bf16[384,256]{1,0:T(8,128)(2,1)S(1)} %slice.15), channel_id=1, source_target_pairs={{0,224},{32,0},{64,32},{96,64},{128,96},{160,128},{192,160},{224,1... | collective-permute-start | bytes 589832 | tf_op jit(solution)/shard_map/ppermute | solution.py:401
  63.9 0.1 shard_map.85
  64.0 5.1 %collective-permute-done.17.refs_13_.refs_0_.refs_12_ = bf16[384,256]{1,0:T(8,128)(2,1)S(1)} collective-permute-done((bf16[384,256]{1,0:T(8,128)(2,1)S(1)}, bf16[384,256]{1,0:T(8,128)(2,1)S(1)}, u32[]{:S(2)}, u32[]{:S(2)}) %collective-permute-start.17) | collective-permute-done | bytes 196640 | tf_op jit(solution)/shard_map/ppermute | solution.py:401
  69.1 0.0 collective-permute-start.20
  69.1 0.0 collective-permute-done.18.refs_14_.refs_1_.refs_13_
  69.1 0.0 collective-permute-done.6.refs_4_
  69.1 0.0 collective-permute-done.7.refs_5_
  69.1 2.6 %shard_map.84 = (f32[4,128,256]{2,1,0:T(8,128)S(1)}, f32[4,128,256]{2,1,0:T(8,128)S(1)}) custom-call(s32[4]{0:T(128)S(1)} %copy-done.1, bf16[4,256,512]{2,1,0:T(8,128)(2,1)S(1)} %pad_maximum_fusion.refs_1_, bf16[4,256,512]{2,1,0:T(8,128)(2,1)S(1)} %collective-permute-done.4.refs_2_, bf16[4,256,512]{2,1,0:T(8,128)(2,1)S(1)} %collective-permute-done.5.refs_3_, ...), custom_call_target="tpu_custom_call" | custom-call | flops 1000000000 | bytes 8000000 | tf_op jit(solution)/shard_map/pallas_call | solution.py:329
  71.7 0.5 collective-permute-start.19
  72.3 0.1 collective-permute-start.22
  72.4 0.0 collective-permute-done.20.refs_14_
  72.4 1.8 %collective-permute-done.22.refs_16_ = bf16[512,256]{1,0:T(8,128)(2,1)S(1)} collective-permute-done((bf16[512,256]{1,0:T(8,128)(2,1)S(1)}, bf16[512,256]{1,0:T(8,128)(2,1)S(1)}, u32[]{:S(2)}, u32[]{:S(2)}) %collective-permute-start.22) | collective-permute-done | bytes 262176 | tf_op jit(solution)/shard_map/ppermute | solution.py:401
  74.2 0.0 collective-permute-done.21.refs_15_
  74.2 0.0 collective-permute-done.19.refs_4_
  74.2 0.6 copy-done.2
  74.8 0.0 copy-done.3
  74.8 5.4 %shard_map.88.refs_6_ = bf16[512,128]{1,0:T(8,128)(2,1)S(1)} custom-call(s32[4]{0:T(128)S(1)} %copy-done.1, s32[128]{0:T(128)S(1)} %copy-done.2, s32[16]{0:T(128)S(1)} %copy-done.3, f32[4,128,256]{2,1,0:T(8,128)S(1)} %get-tuple-element.40.refs_3_, f32[4,128,256]{2,1,0:T(8,128)S(1)} %collective-permute-done.19.refs_4_, ...), custom_call_target="tpu_custom_call" | custom-call | flops 2000000000 | bytes 8000000 | tf_op jit(solution)/shard_map/pallas_call | solution.py:329
  80.2 0.1 collective-permute-start.23
  80.3 1.3 %collective-permute-done.23.refs_7_ = bf16[512,128]{1,0:T(8,128)(2,1)S(1)} collective-permute-done((bf16[512,128]{1,0:T(8,128)(2,1)S(1)}, bf16[512,128]{1,0:T(8,128)(2,1)S(1)}, u32[]{:S(2)}, u32[]{:S(2)}) %collective-permute-start.23) | collective-permute-done | bytes 131104 | tf_op jit(solution)/shard_map/ppermute | solution.py:401
  81.6 1.8 %shard_map.89 = bf16[2048,128]{1,0:T(8,128)(2,1)S(1)} custom-call(s32[4]{0:T(128)S(1)} %copy-done.1, bf16[4,256,512]{2,1,0:T(8,128)(2,1)S(1)} %pad_maximum_fusion.refs_1_, bf16[4,256,512]{2,1,0:T(8,128)(2,1)S(1)} %collective-permute-done.4.refs_2_, bf16[4,256,512]{2,1,0:T(8,128)(2,1)S(1)} %collective-permute-done.5.refs_3_, ...), custom_call_target="tpu_custom_call" | custom-call | flops 600000000 | bytes 8000000 | tf_op jit(solution)/shard_map/pallas_call | solution.py:329
  83.4 24.0 %all_to_all.9 = bf16[32,64,128]{2,1,0:T(8,128)(2,1)S(1)} all-to-all(bf16[32,64,128]{2,1,0:T(8,128)(2,1)S(1)} %bitcast.17), channel_id=1, replica_groups=mesh['z'=8,'x'=4,'c'=2,'kvh'=4] {'z','x'}, dimensions={0} | all-to-all | bytes 1048576 | tf_op jit(solution)/shard_map/all_to_all | solution.py:474
  107.4 0.1 convert_reduce_fusion
  107.5 0.7 copy_bitcast_fusion
  (16 shorter events, 0.2 us)
Async XLA Ops:
  3.4 1.6 %collective-permute-start = (bf16[128,512]{1,0:T(8,128)(2,1)}, bf16[128,512]{1,0:T(8,128)(2,1)S(1)}, u32[]{:S(2)}, u32[]{:S(2)}) collective-permute-start(bf16[128,512]{1,0:T(8,128)(2,1)} %get-tuple-element.29), channel_id=1, source_target_pairs={{0,4},{4,0},{1,5},{5,1},{2,6},{6,2},{3,7},{7,3},{8,12},{12,8},{9,1... | collective-permute-start | bytes 393224 | tf_op jit(solution)/shard_map/ppermute | solution.py:401
  5.0 1.0 copy-start.6
  5.0 8.8 %copy-start.5 = (bf16[256,256]{1,0:T(8,128)(2,1)S(1)}, bf16[256,256]{1,0:T(8,128)(2,1)}, u32[]{:S(2)}) copy-start(bf16[256,256]{1,0:T(8,128)(2,1)} %get-tuple-element.32) | copy-start | bytes 393220
  5.0 8.8 %copy-start.4 = (bf16[256,256]{1,0:T(8,128)(2,1)S(1)}, bf16[256,256]{1,0:T(8,128)(2,1)}, u32[]{:S(2)}) copy-start(bf16[256,256]{1,0:T(8,128)(2,1)} %get-tuple-element.33) | copy-start | bytes 393220
  5.0 18.7 %copy-start = (bf16[256,256]{1,0:T(8,128)(2,1)S(1)}, bf16[256,256]{1,0:T(8,128)(2,1)}, u32[]{:S(2)}) copy-start(bf16[256,256]{1,0:T(8,128)(2,1)} %get-tuple-element.31.refs_0_) | copy-start | bytes 393220
  6.0 7.8 %collective-permute-start.10 = (bf16[256,256]{1,0:T(8,128)(2,1)S(1)}, bf16[256,256]{1,0:T(8,128)(2,1)S(1)}, u32[]{:S(2)}, u32[]{:S(2)}) collective-permute-start(bf16[256,256]{1,0:T(8,128)(2,1)S(1)} %copy-done.6), channel_id=1, source_target_pairs={{0,24},{8,0},{16,8},{24,16},{1,25},{9,1},{17,9},{25,17},{2,26},{10... | collective-permute-start | bytes 393224 | tf_op jit(solution)/shard_map/ppermute | solution.py:401
  8.9 21.0 %collective-permute-start.1 = (bf16[256,512]{1,0:T(8,128)(2,1)S(1)}, bf16[256,512]{1,0:T(8,128)(2,1)S(1)}, u32[]{:S(2)}, u32[]{:S(2)}) collective-permute-start(bf16[256,512]{1,0:T(8,128)(2,1)S(1)} %pad_maximum_fusion.1), channel_id=1, source_target_pairs={{0,1},{1,2},{2,3},{3,0},{4,12},{5,13},{6,14},{7,15},{8,9},{9,10},{... | collective-permute-start | bytes 786440 | tf_op jit(solution)/shard_map/ppermute | solution.py:416
  10.4 19.4 %collective-permute-start.2 = (bf16[256,512]{1,0:T(8,128)(2,1)S(1)}, bf16[256,512]{1,0:T(8,128)(2,1)S(1)}, u32[]{:S(2)}, u32[]{:S(2)}) collective-permute-start(bf16[256,512]{1,0:T(8,128)(2,1)S(1)} %pad_maximum_fusion.1), channel_id=1, source_target_pairs={{0,2},{1,3},{2,0},{3,1},{4,20},{5,21},{6,22},{7,23},{8,10},{9,11},... | collective-permute-start | bytes 786440 | tf_op jit(solution)/shard_map/ppermute | solution.py:416
  11.4 18.5 %collective-permute-start.3 = (bf16[256,512]{1,0:T(8,128)(2,1)S(1)}, bf16[256,512]{1,0:T(8,128)(2,1)S(1)}, u32[]{:S(2)}, u32[]{:S(2)}) collective-permute-start(bf16[256,512]{1,0:T(8,128)(2,1)S(1)} %pad_maximum_fusion.1), channel_id=1, source_target_pairs={{0,3},{1,0},{2,1},{3,2},{4,28},{5,29},{6,30},{7,31},{8,11},{9,8},{... | collective-permute-start | bytes 786440 | tf_op jit(solution)/shard_map/ppermute | solution.py:416
  13.8 10.0 %collective-permute-start.8 = (bf16[256,256]{1,0:T(8,128)(2,1)S(1)}, bf16[256,256]{1,0:T(8,128)(2,1)S(1)}, u32[]{:S(2)}, u32[]{:S(2)}) collective-permute-start(bf16[256,256]{1,0:T(8,128)(2,1)S(1)} %copy-done.5), channel_id=1, source_target_pairs={{0,8},{8,16},{16,24},{24,0},{1,9},{9,17},{17,25},{25,1},{2,10},{10... | collective-permute-start | bytes 393224 | tf_op jit(solution)/shard_map/ppermute | solution.py:401
  13.8 10.0 %collective-permute-start.9 = (bf16[256,256]{1,0:T(8,128)(2,1)S(1)}, bf16[256,256]{1,0:T(8,128)(2,1)S(1)}, u32[]{:S(2)}, u32[]{:S(2)}) collective-permute-start(bf16[256,256]{1,0:T(8,128)(2,1)S(1)} %copy-done.4), channel_id=1, source_target_pairs={{0,16},{8,24},{16,0},{24,8},{1,17},{9,25},{17,1},{25,9},{2,18},{10... | collective-permute-start | bytes 393224 | tf_op jit(solution)/shard_map/ppermute | solution.py:401
  23.8 14.8 %collective-permute-start.11 = (bf16[768,256]{1,0:T(8,128)(2,1)S(1)}, bf16[768,256]{1,0:T(8,128)(2,1)S(1)}, u32[]{:S(2)}, u32[]{:S(2)}) collective-permute-start(bf16[768,256]{1,0:T(8,128)(2,1)S(1)} %get-tuple-element.35.refs_6_.refs_0_.refs_5_), channel_id=1, source_target_pairs={{0,32},{32,64},{64,96},{96,128},{128,160},{160,192},{192,224},{224... | collective-permute-start | bytes 1179656 | tf_op jit(solution)/shard_map/ppermute | solution.py:401
  25.8 12.8 %collective-permute-start.12 = (bf16[768,256]{1,0:T(8,128)(2,1)S(1)}, bf16[768,256]{1,0:T(8,128)(2,1)S(1)}, u32[]{:S(2)}, u32[]{:S(2)}) collective-permute-start(bf16[768,256]{1,0:T(8,128)(2,1)S(1)} %get-tuple-element.35.refs_6_.refs_0_.refs_5_), channel_id=1, source_target_pairs={{0,224},{32,0},{64,32},{96,64},{128,96},{160,128},{192,160},{224,1... | collective-permute-start | bytes 1179656 | tf_op jit(solution)/shard_map/ppermute | solution.py:401
  30.0 23.2 %collective-permute-start.4 = (bf16[4,256,512]{2,1,0:T(8,128)(2,1)S(1)}, bf16[4,256,512]{2,1,0:T(8,128)(2,1)S(1)}, u32[]{:S(2)}, u32[]{:S(2)}) collective-permute-start(bf16[4,256,512]{2,1,0:T(8,128)(2,1)S(1)} %pad_maximum_fusion.refs_1_), channel_id=1, source_target_pairs={{0,8},{1,9},{2,10},{3,11},{4,5},{5,6},{6,7},{7,4},{8,16},{9,17},{1... | collective-permute-start | bytes 3145736 | tf_op jit(solution)/shard_map/ppermute | solution.py:416
  30.1 23.4 %collective-permute-start.5 = (bf16[4,256,512]{2,1,0:T(8,128)(2,1)S(1)}, bf16[4,256,512]{2,1,0:T(8,128)(2,1)S(1)}, u32[]{:S(2)}, u32[]{:S(2)}) collective-permute-start(bf16[4,256,512]{2,1,0:T(8,128)(2,1)S(1)} %pad_maximum_fusion.refs_1_), channel_id=1, source_target_pairs={{0,24},{1,25},{2,26},{3,27},{4,7},{5,4},{6,5},{7,6},{8,0},{9,1},{1... | collective-permute-start | bytes 3145736 | tf_op jit(solution)/shard_map/ppermute | solution.py:416
  38.7 11.3 %collective-permute-start.13 = (bf16[768,256]{1,0:T(8,128)(2,1)S(1)}, bf16[768,256]{1,0:T(8,128)(2,1)S(1)}, u32[]{:S(2)}, u32[]{:S(2)}) collective-permute-start(bf16[768,256]{1,0:T(8,128)(2,1)S(1)} %collective-permute-done.11.refs_7_.refs_1_.refs_6_), channel_id=1, source_target_pairs={{0,32},{32,64},{64,96},{96,128},{128,160},{160,192},{192,224},{224... | collective-permute-start | bytes 1179656 | tf_op jit(solution)/shard_map/ppermute | solution.py:401
  38.7 11.3 %collective-permute-start.14 = (bf16[768,256]{1,0:T(8,128)(2,1)S(1)}, bf16[768,256]{1,0:T(8,128)(2,1)S(1)}, u32[]{:S(2)}, u32[]{:S(2)}) collective-permute-start(bf16[768,256]{1,0:T(8,128)(2,1)S(1)} %collective-permute-done.12.refs_8_.refs_2_.refs_7_), channel_id=1, source_target_pairs={{0,224},{32,0},{64,32},{96,64},{128,96},{160,128},{192,160},{224,1... | collective-permute-start | bytes 1179656 | tf_op jit(solution)/shard_map/ppermute | solution.py:401
  49.9 10.4 %collective-permute-start.15 = (bf16[768,256]{1,0:T(8,128)(2,1)S(1)}, bf16[768,256]{1,0:T(8,128)(2,1)S(1)}, u32[]{:S(2)}, u32[]{:S(2)}) collective-permute-start(bf16[768,256]{1,0:T(8,128)(2,1)S(1)} %collective-permute-done.13.refs_9_.refs_0_.refs_8_), channel_id=1, source_target_pairs={{0,32},{32,64},{64,96},{96,128},{128,160},{160,192},{192,224},{224... | collective-permute-start | bytes 1179656 | tf_op jit(solution)/shard_map/ppermute | solution.py:401
  49.9 10.4 %collective-permute-start.16 = (bf16[768,256]{1,0:T(8,128)(2,1)S(1)}, bf16[768,256]{1,0:T(8,128)(2,1)S(1)}, u32[]{:S(2)}, u32[]{:S(2)}) collective-permute-start(bf16[768,256]{1,0:T(8,128)(2,1)S(1)} %collective-permute-done.14.refs_10_.refs_1_.refs_9_), channel_id=1, source_target_pairs={{0,224},{32,0},{64,32},{96,64},{128,96},{160,128},{192,160},{224,1... | collective-permute-start | bytes 1179656 | tf_op jit(solution)/shard_map/ppermute | solution.py:401
  53.2 15.9 %collective-permute-start.6 = (bf16[2,256,512]{2,1,0:T(8,128)(2,1)S(1)}, bf16[2,256,512]{2,1,0:T(8,128)(2,1)S(1)}, u32[]{:S(2)}, u32[]{:S(2)}) collective-permute-start(bf16[2,256,512]{2,1,0:T(8,128)(2,1)S(1)} %slice.16), channel_id=1, source_target_pairs={{0,8},{1,9},{2,10},{3,11},{4,5},{5,6},{6,7},{7,4},{8,16},{9,17},{1... | collective-permute-start | bytes 1572872 | tf_op jit(solution)/shard_map/ppermute | solution.py:416
  53.5 15.6 %collective-permute-start.7 = (bf16[2,256,512]{2,1,0:T(8,128)(2,1)S(1)}, bf16[2,256,512]{2,1,0:T(8,128)(2,1)S(1)}, u32[]{:S(2)}, u32[]{:S(2)}) collective-permute-start(bf16[2,256,512]{2,1,0:T(8,128)(2,1)S(1)} %slice.17), channel_id=1, source_target_pairs={{0,24},{1,25},{2,26},{3,27},{4,7},{5,4},{6,5},{7,6},{8,0},{9,1},{1... | collective-permute-start | bytes 1572872 | tf_op jit(solution)/shard_map/ppermute | solution.py:416
  60.4 13.8 %collective-permute-start.21 = (bf16[2048,256]{1,0:T(8,128)(2,1)S(1)}, bf16[2048,256]{1,0:T(8,128)(2,1)S(1)}, u32[]{:S(2)}, u32[]{:S(2)}) collective-permute-start(bf16[2048,256]{1,0:T(8,128)(2,1)S(1)} %shard_map.86), channel_id=1, source_target_pairs={{0,4},{4,0},{1,5},{5,1},{2,6},{6,2},{3,7},{7,3},{8,12},{12,8},{9,1... | collective-permute-start | bytes 3145736 | tf_op jit(solution)/shard_map/ppermute | solution.py:401
  60.5 8.6 %collective-permute-start.17 = (bf16[384,256]{1,0:T(8,128)(2,1)S(1)}, bf16[384,256]{1,0:T(8,128)(2,1)S(1)}, u32[]{:S(2)}, u32[]{:S(2)}) collective-permute-start(bf16[384,256]{1,0:T(8,128)(2,1)S(1)} %slice.14), channel_id=1, source_target_pairs={{0,32},{32,64},{64,96},{96,128},{128,160},{160,192},{192,224},{224... | collective-permute-start | bytes 589832 | tf_op jit(solution)/shard_map/ppermute | solution.py:401
  60.6 8.5 %copy-start.1 = (s32[4]{0:T(128)S(1)}, s32[4]{0:T(128)}, u32[]{:S(2)}) copy-start(s32[4]{0:T(128)} %pad_add_fusion.where_ref.refs_0_) | copy-start | bytes 52
  60.6 8.5 %collective-permute-start.18 = (bf16[384,256]{1,0:T(8,128)(2,1)S(1)}, bf16[384,256]{1,0:T(8,128)(2,1)S(1)}, u32[]{:S(2)}, u32[]{:S(2)}) collective-permute-start(bf16[384,256]{1,0:T(8,128)(2,1)S(1)} %slice.15), channel_id=1, source_target_pairs={{0,224},{32,0},{64,32},{96,64},{128,96},{160,128},{192,160},{224,1... | collective-permute-start | bytes 589832 | tf_op jit(solution)/shard_map/ppermute | solution.py:401
  69.1 3.3 %collective-permute-start.20 = (bf16[1536,256]{1,0:T(8,128)(2,1)S(1)}, bf16[1536,256]{1,0:T(8,128)(2,1)S(1)}, u32[]{:S(2)}, u32[]{:S(2)}) collective-permute-start(bf16[1536,256]{1,0:T(8,128)(2,1)S(1)} %shard_map.85), channel_id=1, source_target_pairs={{0,4},{4,0},{1,5},{5,1},{2,6},{6,2},{3,7},{7,3},{8,12},{12,8},{9,1... | collective-permute-start | bytes 2359304 | tf_op jit(solution)/shard_map/ppermute | solution.py:401
  71.7 2.5 %collective-permute-start.19 = (f32[4,128,256]{2,1,0:T(8,128)S(1)}, f32[4,128,256]{2,1,0:T(8,128)S(1)}, u32[]{:S(2)}, u32[]{:S(2)}) collective-permute-start(f32[4,128,256]{2,1,0:T(8,128)S(1)} %get-tuple-element.41), channel_id=1, source_target_pairs={{0,4},{4,0},{1,5},{5,1},{2,6},{6,2},{3,7},{7,3},{8,12},{12,8},{9,1... | collective-permute-start | bytes 1572872 | tf_op jit(solution)/shard_map/ppermute | solution.py:401
  72.3 1.9 %collective-permute-start.22 = (bf16[512,256]{1,0:T(8,128)(2,1)S(1)}, bf16[512,256]{1,0:T(8,128)(2,1)S(1)}, u32[]{:S(2)}, u32[]{:S(2)}) collective-permute-start(bf16[512,256]{1,0:T(8,128)(2,1)S(1)} %shard_map.87), channel_id=1, source_target_pairs={{0,4},{4,0},{1,5},{5,1},{2,6},{6,2},{3,7},{7,3},{8,12},{12,8},{9,1... | collective-permute-start | bytes 786440 | tf_op jit(solution)/shard_map/ppermute | solution.py:401
  74.2 0.7 copy-start.2
  74.2 0.7 copy-start.3
  80.2 1.4 %collective-permute-start.23 = (bf16[512,128]{1,0:T(8,128)(2,1)S(1)}, bf16[512,128]{1,0:T(8,128)(2,1)S(1)}, u32[]{:S(2)}, u32[]{:S(2)}) collective-permute-start(bf16[512,128]{1,0:T(8,128)(2,1)S(1)} %shard_map.88.refs_6_), channel_id=1, source_target_pairs={{0,4},{4,0},{1,5},{5,1},{2,6},{6,2},{3,7},{7,3},{8,12},{12,8},{9,1... | collective-permute-start | bytes 393224 | tf_op jit(solution)/shard_map/ppermute | solution.py:401

commit v3 on v2

--- a/solution.py
+++ b/solution.py
@@ -14,6 +14,9 @@
 LANES = 128
 ROW_BLOCKS = 8
 MOST_EXTRA = ROW_BLOCKS * 4
+TOGETHER = 4
+ORDER = 4
+LENGTHS = ORDER + 128
 SCALE = 1.0 / math.sqrt(HD)
 LOG2E = 1.4426950408889634
 TOKENS = 8192
@@ -83,16 +86,13 @@
 
 
 def hidden_piece(refs, r, s):
-    stack, right, left, far_a, far_b = refs
-    if r == 2:
-        return far_a[s] if s < 2 else far_b[s - 2]
-    return (stack, right, None, left)[r][s]
+    return refs[r][s]
 
 
 def project_kernel(*refs):
-    where_ref, hidden = refs[0], refs[1:6]
-    packs, far_r, far_l = refs[6:13], refs[13], refs[14]
-    keep_ref, send_ref, weights, total = refs[15:]
+    where_ref, hidden = refs[0], refs[1:5]
+    packs, far_r, far_l = refs[5:12], refs[12], refs[13]
+    keep_ref, send_ref, weights, total = refs[14:]
     z, x, c, y = where_ref[0], where_ref[1], where_ref[2], where_ref[3]
 
     def place(pack, dz, places=(0, 1, 2, 3)):
@@ -119,24 +119,22 @@
 
 
 def attend_kernel(*refs):
-    where_ref, order_ref, lengths_ref, qt_keep, qt_received = refs[:5]
-    packs, far_r, far_l = refs[5:12], refs[12], refs[13]
-    swap_a, swap_b, swap_c = refs[14:17]
-    upstream_ref, second_ref = refs[17:19]
+    where_ref, qt_keep, qt_received = refs[:3]
+    packs, far_r, far_l = refs[3:10], refs[10], refs[11]
+    swap_a, swap_b, swap_c = refs[12:15]
+    upstream_ref, second_ref = refs[15:17]
     (
         keys_values,
         query_tangent,
         starts,
-        exp_buf,
-        tan_buf,
-        val_buf,
+        scores,
         sums,
         stats,
         second,
         ends,
         extra_block,
         extra_row,
-    ) = refs[19:]
+    ) = refs[17:]
     z, x, c = where_ref[0], where_ref[1], where_ref[2]
 
     keys_values[0:CHUNK, :] = jnp.zeros((CHUNK, 256), BF16)
@@ -146,7 +144,7 @@
         for i, dx in enumerate(places):
             block = ((zz * 4 + lax.rem(x - dx + 4, 4)) * 2 + cc) * 2
             for b in range(2):
-                target = pl.multiple_of(CHUNK + order_ref[block + b] * BLK, BLK)
+                target = pl.multiple_of(CHUNK + where_ref[ORDER + block + b] * BLK, BLK)
                 row = first_row + i * step + b * 64
                 keys_values[pl.ds(target, BLK), :] = src[row : row + 64, :]
 
@@ -168,7 +166,7 @@
 
     total = jnp.int32(0)
     for d in range(NDOC):
-        total = total + lengths_ref[d]
+        total = total + where_ref[LENGTHS + d]
         ends[d] = total
     packed_block = []
     extras = jnp.int32(0)
@@ -176,7 +174,7 @@
     lane = lax.broadcasted_iota(I32, (BLK, LANES), 1)
     for rb in range(ROW_BLOCKS):
         xx = lax.rem(x - rb // 2 + 4, 4)
-        p = order_ref[((z * 4 + xx) * 2 + c) * 2 + rb % 2]
+        p = where_ref[ORDER + ((z * 4 + xx) * 2 + c) * 2 + rb % 2]
         packed_block.append(p)
         first = jnp.int32(0)
         start = jnp.zeros((BLK, LANES), I32)
@@ -193,8 +191,9 @@
             return at + 1
 
         extras = lax.fori_loop(0, more, note, extras)
-    extra_block[extras] = ROW_BLOCKS
-    extra_row[extras] = 0
+    for n in range(TOGETHER - 1):
+        extra_block[extras + n] = ROW_BLOCKS
+        extra_row[extras + n] = 0
     sums[ROW_BLOCKS] = jnp.zeros((4, BLK, LANES), F32)
     stats[ROW_BLOCKS] = jnp.zeros((4, BLK, LANES), F32)
     second[ROW_BLOCKS] = jnp.zeros((BLK, LANES), F32)
@@ -203,12 +202,12 @@
     def dot_t(a, b):
         return lax.dot_general(a, b, (((1,), (1,)), ((), ())), preferred_element_type=F32)
 
-    def scored(rb, source, row, slot, last_pos):
+    def scored(rb, source, row, last_pos):
         kv = keys_values[pl.ds(pl.multiple_of(row, BLK), CHUNK), :]
         st = dot_t(query_tangent[source], kv[:, 0:128])
         v = dot_t(upstream_ref[source], kv[:, 128:256])
         start = starts[rb]
-        parts = [None] * 4
+        parts = []
         for i in range(CHUNK // LANES):
             cut = slice(i * LANES, (i + 1) * LANES)
             key_pos = row - CHUNK + i * LANES + lane
@@ -216,46 +215,54 @@
             if last_pos is not None:
                 allowed = allowed & (key_pos <= last_pos)
             e = jnp.where(allowed, jnp.exp2(st[0:64, cut] * (SCALE * LOG2E)), 0.0)
-            t_i, v_i = st[64:128, cut], v[:, cut]
-            exp_buf[slot, :, cut] = e
-            tan_buf[slot, :, cut] = t_i
-            val_buf[slot, :, cut] = v_i
-            ev = e * v_i
-            for n, term in enumerate((e, ev, e * t_i, ev * t_i)):
-                parts[n] = term if parts[n] is None else parts[n] + term
+            parts.append((e, st[64:128, cut], v[:, cut]))
         return parts
 
-    def weighted(rb, row, slot):
+    def row_sums(parts):
+        out = [None] * 4
+        for e, t, v in parts:
+            ev = e * v
+            for n, term in enumerate((e, ev, e * t, ev * t)):
+                out[n] = term if out[n] is None else out[n] + term
+        return out
+
+    def keep_scores(slot, parts):
+        for i, part in enumerate(parts):
+            for n in range(3):
+                scores[slot, n, :, i * LANES : (i + 1) * LANES] = part[n]
+
+    def kept_scores(slot):
+        cuts = [slice(i * LANES, (i + 1) * LANES) for i in range(CHUNK // LANES)]
+        return [[scores[slot, n, :, cut] for n in range(3)] for cut in cuts]
+
+    def weighted(rb, row, parts):
         value_mean, tangent_mean, drift, inverse = [stats[rb, n] for n in range(4)]
         pieces = []
-        for i in range(CHUNK // LANES):
-            cut = slice(i * LANES, (i + 1) * LANES)
-            w = (exp_buf[slot, :, cut] * inverse) * (
-                (tan_buf[slot, :, cut] - tangent_mean) * (val_buf[slot, :, cut] - value_mean)
-                - drift
-            )
+        for e, t, v in parts:
+            w = (e * inverse) * ((t - tangent_mean) * (v - value_mean) - drift)
             pieces.append(w.astype(BF16))
         keys = keys_values[pl.ds(pl.multiple_of(row, BLK), CHUNK), 0:128]
         return jnp.dot(jnp.concatenate(pieces, axis=1), keys, preferred_element_type=F32)
 
     for rb in range(ROW_BLOCKS):
-        row = packed_block[rb] * BLK + BLK
-        parts = scored(rb, rb, row, rb, packed_block[rb] * BLK + sub)
-        for n in range(4):
-            sums[rb, n] = parts[n]
-
-    pairs = (extras + 1) // 2
+        p = packed_block[rb]
+        parts = scored(rb, rb, p * BLK + BLK, p * BLK + sub)
+        keep_scores(rb, parts)
+        for n, total in enumerate(row_sums(parts)):
+            sums[rb, n] = total
+
+    rounds = (extras + TOGETHER - 1) // TOGETHER
 
     def extra_scores(i, carry):
-        for item in (2 * i, 2 * i + 1):
+        for item in [TOGETHER * i + n for n in range(TOGETHER)]:
             rb = extra_block[item]
-            row = extra_row[item]
-            parts = scored(rb, jnp.minimum(rb, ROW_BLOCKS - 1), row, ROW_BLOCKS + item, None)
-            for n in range(4):
-                sums[rb, n] += parts[n]
+            parts = scored(rb, jnp.minimum(rb, ROW_BLOCKS - 1), extra_row[item], None)
+            keep_scores(ROW_BLOCKS + item, parts)
+            for n, total in enumerate(row_sums(parts)):
+                sums[rb, n] += total
         return carry
 
-    lax.fori_loop(0, pairs, extra_scores, 0)
+    lax.fori_loop(0, rounds, extra_scores, 0)
 
     for rb in range(ROW_BLOCKS):
         weight_sum, value_sum, tangent_sum, joint_sum = [
@@ -268,15 +275,16 @@
         for n, stat in enumerate((value_mean, tangent_mean, drift, inverse)):
             stats[rb, n] = jnp.broadcast_to(stat, (BLK, LANES))
     for rb in range(ROW_BLOCKS):
-        second[rb] = weighted(rb, packed_block[rb] * BLK + BLK, rb)
+        second[rb] = weighted(rb, packed_block[rb] * BLK + BLK, kept_scores(rb))
 
     def extra_weights(i, carry):
-        for item in (2 * i, 2 * i + 1):
+        for item in [TOGETHER * i + n for n in range(TOGETHER)]:
             rb = extra_block[item]
-            second[rb] += weighted(rb, extra_row[item], ROW_BLOCKS + item)
+            row = extra_row[item]
+            second[rb] += weighted(rb, row, kept_scores(ROW_BLOCKS + item))
         return carry
 
-    lax.fori_loop(0, pairs, extra_weights, 0)
+    lax.fori_loop(0, rounds, extra_weights, 0)
 
     second_ref[...] = (
         second[0:ROW_BLOCKS].reshape(512, 128) * (SCALE * SCALE)
@@ -284,8 +292,8 @@
 
 
 def curvature_kernel(*refs):
-    where_ref, hidden = refs[0], refs[1:6]
-    second_own, second_other, out_ref, second_t, total = refs[6:]
+    where_ref, hidden = refs[0], refs[1:5]
+    second_own, second_other, out_ref, second_t, total = refs[5:]
     c, y = where_ref[2], where_ref[3]
     for dx in range(4):
         rows = slice(dx * 128, dx * 128 + 128)
@@ -305,7 +313,7 @@
 
 
 def gather_kernel(*refs):
-    packs, (mine_ref, upstream_ref) = refs[:4], refs[4:]
+    packs, (mine_ref, upstream_ref) = refs[1:5], refs[5:]
     for dx, pack in enumerate(packs):
         mine_ref[dx * 192 : dx * 192 + 192, :] = pack[0:192, :]
         upstream_ref[2 * dx] = pack[192:256, 0:128]
@@ -348,22 +356,22 @@
         out_specs=(VMEM_SPEC,) * 6,
         scratch_shapes=[pltpu.VMEM(a.shape, BF16) for a in arrays]
         + [pltpu.SemaphoreType.DMA((6,))],
-        compiler_params=pltpu.CompilerParams(vmem_limit_bytes=60 * 1024 * 1024),
+        compiler_params=pltpu.CompilerParams(vmem_limit_bytes=2 * 1024 * 1024),
         cost_estimate=pl.CostEstimate(flops=1_000_000, bytes_accessed=600_000, transcendentals=0),
     )(where, *arrays)
 
 
-def gather(packs):
+def gather(scalars, packs):
     shapes = (
         jax.ShapeDtypeStruct((768, 256), BF16),
         jax.ShapeDtypeStruct((ROW_BLOCKS, BLK, HD), BF16),
     )
-    return call(gather_kernel, (), packs, shapes, [], 2, 100_000)
-
-
-def keys_of(packs):
+    return call(gather_kernel, (scalars,), packs, shapes, [], 2, 100_000)
+
+
+def keys_of(packs, flops=100_000):
     rows = sum(p.shape[0] // 192 * 128 for p in packs)
-    return call(keys_kernel, (), packs, jax.ShapeDtypeStruct((rows, 256), BF16), [], 2, 100_000)
+    return call(keys_kernel, (), packs, jax.ShapeDtypeStruct((rows, 256), BF16), [], 2, flops)
 
 
 def project(where, arrays):
@@ -377,18 +385,16 @@
         pltpu.VMEM((CHUNK + TOKENS, 256), BF16),
         pltpu.VMEM((ROW_BLOCKS, 128, 128), BF16),
         pltpu.VMEM((ROW_BLOCKS + 1, BLK, LANES), I32),
-        pltpu.VMEM((ROW_BLOCKS + MOST_EXTRA + 1, BLK, CHUNK), F32),
-        pltpu.VMEM((ROW_BLOCKS + MOST_EXTRA + 1, BLK, CHUNK), F32),
-        pltpu.VMEM((ROW_BLOCKS + MOST_EXTRA + 1, BLK, CHUNK), F32),
+        pltpu.VMEM((ROW_BLOCKS + MOST_EXTRA, 3, BLK, CHUNK), F32),
         pltpu.VMEM((ROW_BLOCKS + 1, 4, BLK, LANES), F32),
         pltpu.VMEM((ROW_BLOCKS + 1, 4, BLK, LANES), F32),
         pltpu.VMEM((ROW_BLOCKS + 1, BLK, LANES), F32),
         pltpu.SMEM((NDOC,), I32),
-        pltpu.SMEM((MOST_EXTRA + 1,), I32),
-        pltpu.SMEM((MOST_EXTRA + 1,), I32),
+        pltpu.SMEM((MOST_EXTRA + TOGETHER,), I32),
+        pltpu.SMEM((MOST_EXTRA + TOGETHER,), I32),
     ]
     shape = jax.ShapeDtypeStruct((512, 128), BF16)
-    return call(attend_kernel, scalars, arrays, shape, scratch, 26, 2_000_000_000)
+    return call(attend_kernel, scalars, arrays, shape, scratch, 27, 2_000_000_000)
 
 
 def curvature(where, arrays):
@@ -424,39 +430,39 @@
     c = lax.axis_index("c")
     y = lax.axis_index("kvh")
     where = jnp.stack([z, x, c, y]).astype(I32)
+    scalars = jnp.concatenate([where, block_order, lengths])
 
     *packs, keep, send = prepare(
-        where, (hidden, query_weight, probe_vector, key_rows, value_rows, upstream)
+        where,
+        tuple(
+            pltpu.with_memory_space_constraint(a, pltpu.HBM)
+            for a in (hidden, query_weight, probe_vector, key_rows, value_rows, upstream)
+        ),
     )
     base = jnp.concatenate([keep, swap(send)], axis=0)
-    *packs, base = lax.optimization_barrier((*packs, base))
     packs = [packs[0]] + [shift(packs[dx], "x", 4, dx) for dx in (1, 2, 3)]
-    mine, upstream_rows = gather(packs)
+    base, *packs = lax.optimization_barrier((base, *packs))
+    mine, upstream_rows = gather(scalars, packs)
     right_1, left_1 = shift(mine, "z", 8, 1), shift(mine, "z", 8, 7)
 
     stack = jnp.stack([base] + [shift_plane(base, s, True) for s in (1, 2, 3)])
-    hid_right = shift_plane(stack, 1, False)
-    hid_left = shift_plane(stack, 3, False)
-
-    right_1, left_1, _ = lax.optimization_barrier((right_1, left_1, stack))
+    hid_right, hid_far, hid_left = [shift_plane(stack, n, False) for n in (1, 2, 3)]
     right_2, left_2 = shift(right_1, "z", 8, 1), shift(left_1, "z", 8, 7)
 
     right_3, left_3 = shift(right_2, "z", 8, 1), shift(left_2, "z", 8, 7)
     swap_a = swap(keys_of((mine, right_1, left_1)))
 
-    hid_far_a = shift_plane(hid_right[:2], 1, False)
-    hid_far_b = shift_plane(hid_left[2:], 3, False)
-    right_3, left_3, _ = lax.optimization_barrier((right_3, left_3, hid_right))
     far_r, far_l = shift(right_3[:384], "z", 8, 1), shift(left_3[384:], "z", 8, 7)
-    swap_b = swap(keys_of((right_2, left_2, right_3, left_3)))
-    pieces = (stack, hid_right, hid_left, hid_far_a, hid_far_b)
+    *late, hid_right = lax.optimization_barrier((right_2, left_2, right_3, left_3, hid_right))
+    swap_b = swap(keys_of(late))
+    pieces = (stack, hid_right, hid_far, hid_left)
 
     ring = (mine, right_1, left_1, right_2, left_2, right_3, left_3)
     qt_keep, qt_send = project(where, (*pieces, *ring, far_r, far_l))
     qt_received = swap(qt_send)
-    swap_c = swap(keys_of((far_r, far_l)))
+    swap_c = swap(keys_of((far_r, far_l), 20000000000))
     second_own = attend(
-        (where, block_order, lengths),
+        (scalars,),
         (
             qt_keep,
             qt_received,

time: 110 us -> 102 us (0.927)
  waiting for transfers between devices: 34.3 us -> 27 us
  blocking collectives: 24 us -> 27.8 us
  other arithmetic: 1.84 us -> 0.3 us
  Pallas kernels: 12.6 us -> 11.3 us
    ppermute x17, waiting for transfers between devices: 34.3 us -> 26.4 us  [shift(): lax.ppermute(value, axis, [(i, (i + step) % size) for i in range(size)])]
    all_to_all x1, blocking collectives: 24 us -> 27.8 us  [per_device(): shares = lax.all_to_all(partial, ('z', 'x'), 0, 0, tiled=True)]
    ppermute x7 -> x6, starting transfers between devices: 11.8 us -> 9.7 us  [shift_plane(): return lax.ppermute(value, ('x', 'c', 'kvh'), pairs)]
    ppermute x17, starting transfers between devices: 22 us -> 23.7 us  [shift(): lax.ppermute(value, axis, [(i, (i + step) % size) for i in range(size)])]
  transfers between devices with their start and end apart: 24 -> 23, of which waited for: 8 -> 9; matrix products, arithmetic and copies ran while one was open for 0% -> 0% of each run, Pallas kernels for 3% -> 3%
where the time goes in v3:
time: 102 us; the launch traced here: 101 us
  starting transfers between devices  33.3 us (33%)
  blocking collectives  27.8 us (27%)
  waiting for transfers between devices  27 us (26%)
  Pallas kernels  11.3 us (11%)
    all_to_all x1, blocking collectives, per_device(): shares = lax.all_to_all(partial, ('z', 'x'), 0, 0, tiled=True)  27.8 us
    ppermute x17, waiting for transfers between devices, shift(): lax.ppermute(value, axis, [(i, (i + step) % size) for i in range(size)])  26.4 us
    ppermute x17, starting transfers between devices, shift(): lax.ppermute(value, axis, [(i, (i + step) % size) for i in range(size)])  23.7 us
    ppermute x6, starting transfers between devices, shift_plane(): return lax.ppermute(value, ('x', 'c', 'kvh'), pairs)  9.7 us
    pallas_call x7, Pallas kernels, call(): pl.pallas_call(kernel, out_shape=out_shape, in_specs=[SMEM_SPEC] * len(sc...  9.43 us
  transfers between devices with their start and end apart: 23, of which 9 were waited for; matrix products, arithmetic and copies ran while one was open for 0% of the time, Pallas kernels for 3%

profile of v3, /device:TPU:8, one launch (start us, length us, event | category | flops | bytes accessed | tf_op | source)
XLA Modules:
  0.0 100.7 jit_solution(3623613132300964934)
XLA Ops:
  0.0 0.1 pad_add_fusion.where_ref.refs_0_
  0.1 1.9 %shard_map.82 = (bf16[256,256]{1,0:T(8,128)(2,1)S(1)}, bf16[256,256]{1,0:T(8,128)(2,1)S(1)}, bf16[256,256]{1,0:T(8,128)(2,1)S(1)}, bf16[256,256]{1,0:T(8,128)(2,...) custom-call(s32[4]{0:T(128)S(1)} %pad_add_fusion.where_ref.refs_0_, bf16[128,1024]{1,0:T(8,128)(2,1)} %hidden_hbm.1, ...), custom_call_target="tpu_custom_call" | custom-call | flops 1000000 | bytes 600000 | tf_op jit(solution)/shard_map/pallas_call | solution.py:352
  2.0 0.1 collective-permute-start
  2.1 1.6 %collective-permute-start.1 = (bf16[256,256]{1,0:T(8,128)(2,1)S(1)}, bf16[256,256]{1,0:T(8,128)(2,1)S(1)}, u32[]{:S(2)}, u32[]{:S(2)}) collective-permute-start(bf16[256,256]{1,0:T(8,128)(2,1)S(1)} %get-tuple-element.28), channel_id=1, source_target_pairs={{0,8},{8,16},{16,24},{24,0},{1,9},{9,17},{17,25},{25,1},{2,10},{10... | collective-permute-start | bytes 393224 | tf_op jit(solution)/shard_map/ppermute | solution.py:407
  3.6 2.7 %collective-permute-start.2 = (bf16[256,256]{1,0:T(8,128)(2,1)S(1)}, bf16[256,256]{1,0:T(8,128)(2,1)S(1)}, u32[]{:S(2)}, u32[]{:S(2)}) collective-permute-start(bf16[256,256]{1,0:T(8,128)(2,1)S(1)} %get-tuple-element.29), channel_id=1, source_target_pairs={{0,16},{8,24},{16,0},{24,8},{1,17},{9,25},{17,1},{25,9},{2,18},{10... | collective-permute-start | bytes 393224 | tf_op jit(solution)/shard_map/ppermute | solution.py:407
  6.4 1.4 %collective-permute-start.3 = (bf16[256,256]{1,0:T(8,128)(2,1)S(1)}, bf16[256,256]{1,0:T(8,128)(2,1)S(1)}, u32[]{:S(2)}, u32[]{:S(2)}) collective-permute-start(bf16[256,256]{1,0:T(8,128)(2,1)S(1)} %get-tuple-element.30), channel_id=1, source_target_pairs={{0,24},{8,0},{16,8},{24,16},{1,25},{9,1},{17,9},{25,17},{2,26},{10... | collective-permute-start | bytes 393224 | tf_op jit(solution)/shard_map/ppermute | solution.py:407
  7.8 0.0 collective-permute-done
  7.8 0.0 copy-start
  7.8 0.0 copy-start.1
  7.8 1.3 %collective-permute-done.1.refs_2_ = bf16[256,256]{1,0:T(8,128)(2,1)S(1)} collective-permute-done((bf16[256,256]{1,0:T(8,128)(2,1)S(1)}, bf16[256,256]{1,0:T(8,128)(2,1)S(1)}, u32[]{:S(2)}, u32[]{:S(2)}) %collective-permute-start.1) | collective-permute-done | bytes 131104 | tf_op jit(solution)/shard_map/ppermute | solution.py:407
  9.2 3.8 %collective-permute-done.2.refs_3_ = bf16[256,256]{1,0:T(8,128)(2,1)S(1)} collective-permute-done((bf16[256,256]{1,0:T(8,128)(2,1)S(1)}, bf16[256,256]{1,0:T(8,128)(2,1)S(1)}, u32[]{:S(2)}, u32[]{:S(2)}) %collective-permute-start.2) | collective-permute-done | bytes 131104 | tf_op jit(solution)/shard_map/ppermute | solution.py:407
  13.0 0.0 collective-permute-done.3.refs_4_
  13.0 1.6 %collective-permute-start.4 = (bf16[256,512]{1,0:T(8,128)(2,1)S(1)}, bf16[256,512]{1,0:T(8,128)(2,1)S(1)}, u32[]{:S(2)}, u32[]{:S(2)}) collective-permute-start(bf16[256,512]{1,0:T(8,128)(2,1)S(1)} %pad_maximum_fusion.1), channel_id=1, source_target_pairs={{0,1},{1,2},{2,3},{3,0},{4,12},{5,13},{6,14},{7,15},{8,9},{9,10},{... | collective-permute-start | bytes 786440 | tf_op jit(solution)/shard_map/ppermute | solution.py:422
  14.6 2.3 %collective-permute-start.5 = (bf16[256,512]{1,0:T(8,128)(2,1)S(1)}, bf16[256,512]{1,0:T(8,128)(2,1)S(1)}, u32[]{:S(2)}, u32[]{:S(2)}) collective-permute-start(bf16[256,512]{1,0:T(8,128)(2,1)S(1)} %pad_maximum_fusion.1), channel_id=1, source_target_pairs={{0,2},{1,3},{2,0},{3,1},{4,20},{5,21},{6,22},{7,23},{8,10},{9,11},... | collective-permute-start | bytes 786440 | tf_op jit(solution)/shard_map/ppermute | solution.py:422
  16.9 1.0 %collective-permute-start.6 = (bf16[256,512]{1,0:T(8,128)(2,1)S(1)}, bf16[256,512]{1,0:T(8,128)(2,1)S(1)}, u32[]{:S(2)}, u32[]{:S(2)}) collective-permute-start(bf16[256,512]{1,0:T(8,128)(2,1)S(1)} %pad_maximum_fusion.1), channel_id=1, source_target_pairs={{0,3},{1,0},{2,1},{3,2},{4,28},{5,29},{6,30},{7,31},{8,11},{9,8},{... | collective-permute-start | bytes 786440 | tf_op jit(solution)/shard_map/ppermute | solution.py:422
  17.9 0.0 copy-done
  17.9 0.0 copy-done.1
  17.9 0.1 concatenate.8.refs_0_
  18.0 0.6 shard_map.83
  18.6 2.0 %collective-permute-start.7 = (bf16[768,256]{1,0:T(8,128)(2,1)S(1)}, bf16[768,256]{1,0:T(8,128)(2,1)S(1)}, u32[]{:S(2)}, u32[]{:S(2)}) collective-permute-start(bf16[768,256]{1,0:T(8,128)(2,1)S(1)} %get-tuple-element.36.refs_5_.refs_0_.refs_3_), channel_id=1, source_target_pairs={{0,32},{32,64},{64,96},{96,128},{128,160},{160,192},{192,224},{224... | collective-permute-start | bytes 1179656 | tf_op jit(solution)/shard_map/ppermute | solution.py:407
  20.6 4.0 %collective-permute-start.9 = (bf16[768,256]{1,0:T(8,128)(2,1)S(1)}, bf16[768,256]{1,0:T(8,128)(2,1)S(1)}, u32[]{:S(2)}, u32[]{:S(2)}) collective-permute-start(bf16[768,256]{1,0:T(8,128)(2,1)S(1)} %get-tuple-element.36.refs_5_.refs_0_.refs_3_), channel_id=1, source_target_pairs={{0,224},{32,0},{64,32},{96,64},{128,96},{160,128},{192,160},{224,1... | collective-permute-start | bytes 1179656 | tf_op jit(solution)/shard_map/ppermute | solution.py:407
  24.6 0.0 collective-permute-done.4
  24.6 0.0 collective-permute-done.5
  24.6 0.6 collective-permute-done.6
  25.2 0.1 pad_maximum_fusion.refs_1_
  25.4 1.4 %collective-permute-start.13 = (bf16[4,256,512]{2,1,0:T(8,128)(2,1)S(1)}, bf16[4,256,512]{2,1,0:T(8,128)(2,1)S(1)}, u32[]{:S(2)}, u32[]{:S(2)}) collective-permute-start(bf16[4,256,512]{2,1,0:T(8,128)(2,1)S(1)} %pad_maximum_fusion.refs_1_), channel_id=1, source_target_pairs={{0,8},{1,9},{2,10},{3,11},{4,5},{5,6},{6,7},{7,4},{8,16},{9,17},{1... | collective-permute-start | bytes 3145736 | tf_op jit(solution)/shard_map/ppermute | solution.py:422
  26.8 2.4 %collective-permute-start.14 = (bf16[4,256,512]{2,1,0:T(8,128)(2,1)S(1)}, bf16[4,256,512]{2,1,0:T(8,128)(2,1)S(1)}, u32[]{:S(2)}, u32[]{:S(2)}) collective-permute-start(bf16[4,256,512]{2,1,0:T(8,128)(2,1)S(1)} %pad_maximum_fusion.refs_1_), channel_id=1, source_target_pairs={{0,16},{1,17},{2,18},{3,19},{4,6},{5,7},{6,4},{7,5},{8,24},{9,25},... | collective-permute-start | bytes 3145736 | tf_op jit(solution)/shard_map/ppermute | solution.py:422
  29.2 1.0 collective-permute-start.15
  30.1 2.5 %collective-permute-done.7.refs_6_.refs_1_.refs_4_ = bf16[768,256]{1,0:T(8,128)(2,1)S(1)} collective-permute-done((bf16[768,256]{1,0:T(8,128)(2,1)S(1)}, bf16[768,256]{1,0:T(8,128)(2,1)S(1)}, u32[]{:S(2)}, u32[]{:S(2)}) %collective-permute-start.7) | collective-permute-done | bytes 393248 | tf_op jit(solution)/shard_map/ppermute | solution.py:407
  32.7 0.0 collective-permute-start.8
  32.7 0.0 collective-permute-done.9.refs_7_.refs_2_.refs_5_
  32.7 3.5 %collective-permute-start.10 = (bf16[768,256]{1,0:T(8,128)(2,1)S(1)}, bf16[768,256]{1,0:T(8,128)(2,1)S(1)}, u32[]{:S(2)}, u32[]{:S(2)}) collective-permute-start(bf16[768,256]{1,0:T(8,128)(2,1)S(1)} %collective-permute-done.9.refs_7_.refs_2_.refs_5_), channel_id=1, source_target_pairs={{0,224},{32,0},{64,32},{96,64},{128,96},{160,128},{192,160},{224,1... | collective-permute-start | bytes 1179656 | tf_op jit(solution)/shard_map/ppermute | solution.py:407
  36.1 7.0 %collective-permute-done.8.refs_8_.refs_0_.refs_6_ = bf16[768,256]{1,0:T(8,128)(2,1)S(1)} collective-permute-done((bf16[768,256]{1,0:T(8,128)(2,1)S(1)}, bf16[768,256]{1,0:T(8,128)(2,1)S(1)}, u32[]{:S(2)}, u32[]{:S(2)}) %collective-permute-start.8) | collective-permute-done | bytes 393248 | tf_op jit(solution)/shard_map/ppermute | solution.py:407
  43.1 0.0 collective-permute-start.11
  43.1 0.0 collective-permute-done.10.refs_9_.refs_1_.refs_7_
  43.1 3.2 %collective-permute-start.12 = (bf16[768,256]{1,0:T(8,128)(2,1)S(1)}, bf16[768,256]{1,0:T(8,128)(2,1)S(1)}, u32[]{:S(2)}, u32[]{:S(2)}) collective-permute-start(bf16[768,256]{1,0:T(8,128)(2,1)S(1)} %collective-permute-done.10.refs_9_.refs_1_.refs_7_), channel_id=1, source_target_pairs={{0,224},{32,0},{64,32},{96,64},{128,96},{160,128},{192,160},{224,1... | collective-permute-start | bytes 1179656 | tf_op jit(solution)/shard_map/ppermute | solution.py:407
  46.3 6.1 %collective-permute-done.11.refs_10_.refs_2_.refs_8_ = bf16[768,256]{1,0:T(8,128)(2,1)S(1)} collective-permute-done((bf16[768,256]{1,0:T(8,128)(2,1)S(1)}, bf16[768,256]{1,0:T(8,128)(2,1)S(1)}, u32[]{:S(2)}, u32[]{:S(2)}) %collective-permute-start.11) | collective-permute-done | bytes 393248 | tf_op jit(solution)/shard_map/ppermute | solution.py:407
  52.5 0.3 collective-permute-start.16
  52.8 0.0 collective-permute-done.12.refs_11_.refs_3_.refs_9_
  52.8 3.3 %collective-permute-start.17 = (bf16[384,256]{1,0:T(8,128)(2,1)S(1)}, bf16[384,256]{1,0:T(8,128)(2,1)S(1)}, u32[]{:S(2)}, u32[]{:S(2)}) collective-permute-start(bf16[384,256]{1,0:T(8,128)(2,1)S(1)} %slice.9), channel_id=1, source_target_pairs={{0,224},{32,0},{64,32},{96,64},{128,96},{160,128},{192,160},{224,1... | collective-permute-start | bytes 589832 | tf_op jit(solution)/shard_map/ppermute | solution.py:407
  56.1 0.1 shard_map.85
  56.1 0.0 collective-permute-done.13.refs_2_
  56.1 0.1 collective-permute-start.19
  56.2 0.1 shard_map.86
  56.3 0.0 collective-permute-done.14.refs_3_
  56.3 0.6 collective-permute-start.20
  56.9 0.0 collective-permute-done.15.refs_4_
  56.9 2.7 %collective-permute-done.16.refs_12_.refs_0_.refs_10_ = bf16[384,256]{1,0:T(8,128)(2,1)S(1)} collective-permute-done((bf16[384,256]{1,0:T(8,128)(2,1)S(1)}, bf16[384,256]{1,0:T(8,128)(2,1)S(1)}, u32[]{:S(2)}, u32[]{:S(2)}) %collective-permute-start.16) | collective-permute-done | bytes 196640 | tf_op jit(solution)/shard_map/ppermute | solution.py:407
  59.6 0.0 collective-permute-done.17.refs_13_.refs_1_.refs_11_
  59.6 2.6 %shard_map.84 = (f32[4,128,256]{2,1,0:T(8,128)S(1)}, f32[4,128,256]{2,1,0:T(8,128)S(1)}) custom-call(s32[4]{0:T(128)S(1)} %pad_add_fusion.where_ref.refs_0_, bf16[4,256,512]{2,1,0:T(8,128)(2,1)S(1)} %pad_maximum_fusion.refs_1_, bf16[4,256,512]{2,1,0:T(8,128)(2,1)S(1)} %collective-permute-done.13.refs_2_, ...), custom_call_target="tpu_custom_call" | custom-call | flops 1000000000 | bytes 8000000 | tf_op jit(solution)/shard_map/pallas_call | solution.py:337
  62.2 0.1 collective-permute-start.18
  62.3 0.6 collective-permute-start.21
  62.9 0.0 collective-permute-done.19.refs_12_
  62.9 1.7 %collective-permute-done.21.refs_14_ = bf16[512,256]{1,0:T(8,128)(2,1)S(1)} collective-permute-done((bf16[512,256]{1,0:T(8,128)(2,1)S(1)}, bf16[512,256]{1,0:T(8,128)(2,1)S(1)}, u32[]{:S(2)}, u32[]{:S(2)}) %collective-permute-start.21) | collective-permute-done | bytes 262176 | tf_op jit(solution)/shard_map/ppermute | solution.py:407
  64.6 0.0 collective-permute-done.18.refs_2_
  64.6 0.0 collective-permute-done.20.refs_13_
  64.6 4.4 %shard_map.88.refs_5_ = bf16[512,128]{1,0:T(8,128)(2,1)S(1)} custom-call(s32[148]{0:T(256)S(1)} %concatenate.8.refs_0_, f32[4,128,256]{2,1,0:T(8,128)S(1)} %get-tuple-element.38.refs_1_, f32[4,128,256]{2,1,0:T(8,128)S(1)} %collective-permute-done.18.refs_2_, bf16[768,256]{1,0:T(8,128)(2,1)S(1)} %get-tuple-element.36.refs_5_.refs_0_.refs_3_, ...), custom_call_target="tpu_custom_call" | custom-call | flops 2000000000 | bytes 8000000 | tf_op jit(solution)/shard_map/pallas_call | solution.py:337
  68.9 0.2 collective-permute-start.22
  69.2 1.2 %collective-permute-done.22.refs_6_ = bf16[512,128]{1,0:T(8,128)(2,1)S(1)} collective-permute-done((bf16[512,128]{1,0:T(8,128)(2,1)S(1)}, bf16[512,128]{1,0:T(8,128)(2,1)S(1)}, u32[]{:S(2)}, u32[]{:S(2)}) %collective-permute-start.22) | collective-permute-done | bytes 131104 | tf_op jit(solution)/shard_map/ppermute | solution.py:407
  70.4 1.8 %shard_map.89 = bf16[2048,128]{1,0:T(8,128)(2,1)S(1)} custom-call(s32[4]{0:T(128)S(1)} %pad_add_fusion.where_ref.refs_0_, bf16[4,256,512]{2,1,0:T(8,128)(2,1)S(1)} %pad_maximum_fusion.refs_1_, bf16[4,256,512]{2,1,0:T(8,128)(2,1)S(1)} %collective-permute-done.13.refs_2_, bf16[4,256,512]{2,1,0:T(8,128)(2,1)S(1)} %collective-permute-done.14.refs_3_, ...), custom_call_target="tpu_custom_call" | custom-call | flops 600000000 | bytes 8000000 | tf_op jit(solution)/shard_map/pallas_call | solution.py:337
  72.2 27.8 %all_to_all.9 = bf16[32,64,128]{2,1,0:T(8,128)(2,1)S(1)} all-to-all(bf16[32,64,128]{2,1,0:T(8,128)(2,1)S(1)} %bitcast.17), channel_id=1, replica_groups=mesh['z'=8,'x'=4,'c'=2,'kvh'=4] {'z','x'}, dimensions={0} | all-to-all | bytes 1048576 | tf_op jit(solution)/shard_map/all_to_all | solution.py:480
  99.9 0.1 convert_reduce_fusion
  100.0 0.7 copy_bitcast_fusion
  (4 shorter events, 0.1 us)
Async XLA Ops:
  2.0 5.8 %collective-permute-start = (bf16[128,512]{1,0:T(8,128)(2,1)S(1)}, bf16[128,512]{1,0:T(8,128)(2,1)S(1)}, u32[]{:S(2)}, u32[]{:S(2)}) collective-permute-start(bf16[128,512]{1,0:T(8,128)(2,1)S(1)} %get-tuple-element.26), channel_id=1, source_target_pairs={{0,4},{4,0},{1,5},{5,1},{2,6},{6,2},{3,7},{7,3},{8,12},{12,8},{9,1... | collective-permute-start | bytes 393224 | tf_op jit(solution)/shard_map/ppermute | solution.py:407
  2.1 7.1 %collective-permute-start.1 = (bf16[256,256]{1,0:T(8,128)(2,1)S(1)}, bf16[256,256]{1,0:T(8,128)(2,1)S(1)}, u32[]{:S(2)}, u32[]{:S(2)}) collective-permute-start(bf16[256,256]{1,0:T(8,128)(2,1)S(1)} %get-tuple-element.28), channel_id=1, source_target_pairs={{0,8},{8,16},{16,24},{24,0},{1,9},{9,17},{17,25},{25,1},{2,10},{10... | collective-permute-start | bytes 393224 | tf_op jit(solution)/shard_map/ppermute | solution.py:407
  3.6 9.3 %collective-permute-start.2 = (bf16[256,256]{1,0:T(8,128)(2,1)S(1)}, bf16[256,256]{1,0:T(8,128)(2,1)S(1)}, u32[]{:S(2)}, u32[]{:S(2)}) collective-permute-start(bf16[256,256]{1,0:T(8,128)(2,1)S(1)} %get-tuple-element.29), channel_id=1, source_target_pairs={{0,16},{8,24},{16,0},{24,8},{1,17},{9,25},{17,1},{25,9},{2,18},{10... | collective-permute-start | bytes 393224 | tf_op jit(solution)/shard_map/ppermute | solution.py:407
  6.4 6.6 %collective-permute-start.3 = (bf16[256,256]{1,0:T(8,128)(2,1)S(1)}, bf16[256,256]{1,0:T(8,128)(2,1)S(1)}, u32[]{:S(2)}, u32[]{:S(2)}) collective-permute-start(bf16[256,256]{1,0:T(8,128)(2,1)S(1)} %get-tuple-element.30), channel_id=1, source_target_pairs={{0,24},{8,0},{16,8},{24,16},{1,25},{9,1},{17,9},{25,17},{2,26},{10... | collective-permute-start | bytes 393224 | tf_op jit(solution)/shard_map/ppermute | solution.py:407
  7.8 10.1 %copy-start = (s32[128]{0:T(128)S(1)}, s32[128]{0:T(128)}, u32[]{:S(2)}) copy-start(s32[128]{0:T(128)} %param.15) | copy-start | bytes 1540
  7.8 10.1 %copy-start.1 = (s32[16]{0:T(128)S(1)}, s32[16]{0:T(128)}, u32[]{:S(2)}) copy-start(s32[16]{0:T(128)} %param.14) | copy-start | bytes 196
  13.0 11.6 %collective-permute-start.4 = (bf16[256,512]{1,0:T(8,128)(2,1)S(1)}, bf16[256,512]{1,0:T(8,128)(2,1)S(1)}, u32[]{:S(2)}, u32[]{:S(2)}) collective-permute-start(bf16[256,512]{1,0:T(8,128)(2,1)S(1)} %pad_maximum_fusion.1), channel_id=1, source_target_pairs={{0,1},{1,2},{2,3},{3,0},{4,12},{5,13},{6,14},{7,15},{8,9},{9,10},{... | collective-permute-start | bytes 786440 | tf_op jit(solution)/shard_map/ppermute | solution.py:422
  14.6 10.1 %collective-permute-start.5 = (bf16[256,512]{1,0:T(8,128)(2,1)S(1)}, bf16[256,512]{1,0:T(8,128)(2,1)S(1)}, u32[]{:S(2)}, u32[]{:S(2)}) collective-permute-start(bf16[256,512]{1,0:T(8,128)(2,1)S(1)} %pad_maximum_fusion.1), channel_id=1, source_target_pairs={{0,2},{1,3},{2,0},{3,1},{4,20},{5,21},{6,22},{7,23},{8,10},{9,11},... | collective-permute-start | bytes 786440 | tf_op jit(solution)/shard_map/ppermute | solution.py:422
  16.9 8.4 %collective-permute-start.6 = (bf16[256,512]{1,0:T(8,128)(2,1)S(1)}, bf16[256,512]{1,0:T(8,128)(2,1)S(1)}, u32[]{:S(2)}, u32[]{:S(2)}) collective-permute-start(bf16[256,512]{1,0:T(8,128)(2,1)S(1)} %pad_maximum_fusion.1), channel_id=1, source_target_pairs={{0,3},{1,0},{2,1},{3,2},{4,28},{5,29},{6,30},{7,31},{8,11},{9,8},{... | collective-permute-start | bytes 786440 | tf_op jit(solution)/shard_map/ppermute | solution.py:422
  18.6 14.1 %collective-permute-start.7 = (bf16[768,256]{1,0:T(8,128)(2,1)S(1)}, bf16[768,256]{1,0:T(8,128)(2,1)S(1)}, u32[]{:S(2)}, u32[]{:S(2)}) collective-permute-start(bf16[768,256]{1,0:T(8,128)(2,1)S(1)} %get-tuple-element.36.refs_5_.refs_0_.refs_3_), channel_id=1, source_target_pairs={{0,32},{32,64},{64,96},{96,128},{128,160},{160,192},{192,224},{224... | collective-permute-start | bytes 1179656 | tf_op jit(solution)/shard_map/ppermute | solution.py:407
  20.6 12.1 %collective-permute-start.9 = (bf16[768,256]{1,0:T(8,128)(2,1)S(1)}, bf16[768,256]{1,0:T(8,128)(2,1)S(1)}, u32[]{:S(2)}, u32[]{:S(2)}) collective-permute-start(bf16[768,256]{1,0:T(8,128)(2,1)S(1)} %get-tuple-element.36.refs_5_.refs_0_.refs_3_), channel_id=1, source_target_pairs={{0,224},{32,0},{64,32},{96,64},{128,96},{160,128},{192,160},{224,1... | collective-permute-start | bytes 1179656 | tf_op jit(solution)/shard_map/ppermute | solution.py:407
  25.4 30.8 %collective-permute-start.13 = (bf16[4,256,512]{2,1,0:T(8,128)(2,1)S(1)}, bf16[4,256,512]{2,1,0:T(8,128)(2,1)S(1)}, u32[]{:S(2)}, u32[]{:S(2)}) collective-permute-start(bf16[4,256,512]{2,1,0:T(8,128)(2,1)S(1)} %pad_maximum_fusion.refs_1_), channel_id=1, source_target_pairs={{0,8},{1,9},{2,10},{3,11},{4,5},{5,6},{6,7},{7,4},{8,16},{9,17},{1... | collective-permute-start | bytes 3145736 | tf_op jit(solution)/shard_map/ppermute | solution.py:422
  26.8 29.5 %collective-permute-start.14 = (bf16[4,256,512]{2,1,0:T(8,128)(2,1)S(1)}, bf16[4,256,512]{2,1,0:T(8,128)(2,1)S(1)}, u32[]{:S(2)}, u32[]{:S(2)}) collective-permute-start(bf16[4,256,512]{2,1,0:T(8,128)(2,1)S(1)} %pad_maximum_fusion.refs_1_), channel_id=1, source_target_pairs={{0,16},{1,17},{2,18},{3,19},{4,6},{5,7},{6,4},{7,5},{8,24},{9,25},... | collective-permute-start | bytes 3145736 | tf_op jit(solution)/shard_map/ppermute | solution.py:422
  29.2 27.7 %collective-permute-start.15 = (bf16[4,256,512]{2,1,0:T(8,128)(2,1)S(1)}, bf16[4,256,512]{2,1,0:T(8,128)(2,1)S(1)}, u32[]{:S(2)}, u32[]{:S(2)}) collective-permute-start(bf16[4,256,512]{2,1,0:T(8,128)(2,1)S(1)} %pad_maximum_fusion.refs_1_), channel_id=1, source_target_pairs={{0,24},{1,25},{2,26},{3,27},{4,7},{5,4},{6,5},{7,6},{8,0},{9,1},{1... | collective-permute-start | bytes 3145736 | tf_op jit(solution)/shard_map/ppermute | solution.py:422
  32.7 10.4 %collective-permute-start.8 = (bf16[768,256]{1,0:T(8,128)(2,1)S(1)}, bf16[768,256]{1,0:T(8,128)(2,1)S(1)}, u32[]{:S(2)}, u32[]{:S(2)}) collective-permute-start(bf16[768,256]{1,0:T(8,128)(2,1)S(1)} %collective-permute-done.7.refs_6_.refs_1_.refs_4_), channel_id=1, source_target_pairs={{0,32},{32,64},{64,96},{96,128},{128,160},{160,192},{192,224},{224... | collective-permute-start | bytes 1179656 | tf_op jit(solution)/shard_map/ppermute | solution.py:407
  32.7 10.4 %collective-permute-start.10 = (bf16[768,256]{1,0:T(8,128)(2,1)S(1)}, bf16[768,256]{1,0:T(8,128)(2,1)S(1)}, u32[]{:S(2)}, u32[]{:S(2)}) collective-permute-start(bf16[768,256]{1,0:T(8,128)(2,1)S(1)} %collective-permute-done.9.refs_7_.refs_2_.refs_5_), channel_id=1, source_target_pairs={{0,224},{32,0},{64,32},{96,64},{128,96},{160,128},{192,160},{224,1... | collective-permute-start | bytes 1179656 | tf_op jit(solution)/shard_map/ppermute | solution.py:407
  43.1 9.4 %collective-permute-start.11 = (bf16[768,256]{1,0:T(8,128)(2,1)S(1)}, bf16[768,256]{1,0:T(8,128)(2,1)S(1)}, u32[]{:S(2)}, u32[]{:S(2)}) collective-permute-start(bf16[768,256]{1,0:T(8,128)(2,1)S(1)} %collective-permute-done.8.refs_8_.refs_0_.refs_6_), channel_id=1, source_target_pairs={{0,32},{32,64},{64,96},{96,128},{128,160},{160,192},{192,224},{224... | collective-permute-start | bytes 1179656 | tf_op jit(solution)/shard_map/ppermute | solution.py:407
  43.1 9.7 %collective-permute-start.12 = (bf16[768,256]{1,0:T(8,128)(2,1)S(1)}, bf16[768,256]{1,0:T(8,128)(2,1)S(1)}, u32[]{:S(2)}, u32[]{:S(2)}) collective-permute-start(bf16[768,256]{1,0:T(8,128)(2,1)S(1)} %collective-permute-done.10.refs_9_.refs_1_.refs_7_), channel_id=1, source_target_pairs={{0,224},{32,0},{64,32},{96,64},{128,96},{160,128},{192,160},{224,1... | collective-permute-start | bytes 1179656 | tf_op jit(solution)/shard_map/ppermute | solution.py:407
  52.5 7.1 %collective-permute-start.16 = (bf16[384,256]{1,0:T(8,128)(2,1)S(1)}, bf16[384,256]{1,0:T(8,128)(2,1)S(1)}, u32[]{:S(2)}, u32[]{:S(2)}) collective-permute-start(bf16[384,256]{1,0:T(8,128)(2,1)S(1)} %slice.8), channel_id=1, source_target_pairs={{0,32},{32,64},{64,96},{96,128},{128,160},{160,192},{192,224},{224... | collective-permute-start | bytes 589832 | tf_op jit(solution)/shard_map/ppermute | solution.py:407
  52.8 6.8 %collective-permute-start.17 = (bf16[384,256]{1,0:T(8,128)(2,1)S(1)}, bf16[384,256]{1,0:T(8,128)(2,1)S(1)}, u32[]{:S(2)}, u32[]{:S(2)}) collective-permute-start(bf16[384,256]{1,0:T(8,128)(2,1)S(1)} %slice.9), channel_id=1, source_target_pairs={{0,224},{32,0},{64,32},{96,64},{128,96},{160,128},{192,160},{224,1... | collective-permute-start | bytes 589832 | tf_op jit(solution)/shard_map/ppermute | solution.py:407
  56.1 6.8 %collective-permute-start.19 = (bf16[1536,256]{1,0:T(8,128)(2,1)S(1)}, bf16[1536,256]{1,0:T(8,128)(2,1)S(1)}, u32[]{:S(2)}, u32[]{:S(2)}) collective-permute-start(bf16[1536,256]{1,0:T(8,128)(2,1)S(1)} %shard_map.85), channel_id=1, source_target_pairs={{0,4},{4,0},{1,5},{5,1},{2,6},{6,2},{3,7},{7,3},{8,12},{12,8},{9,1... | collective-permute-start | bytes 2359304 | tf_op jit(solution)/shard_map/ppermute | solution.py:407
  56.3 8.2 %collective-permute-start.20 = (bf16[2048,256]{1,0:T(8,128)(2,1)S(1)}, bf16[2048,256]{1,0:T(8,128)(2,1)S(1)}, u32[]{:S(2)}, u32[]{:S(2)}) collective-permute-start(bf16[2048,256]{1,0:T(8,128)(2,1)S(1)} %shard_map.86), channel_id=1, source_target_pairs={{0,4},{4,0},{1,5},{5,1},{2,6},{6,2},{3,7},{7,3},{8,12},{12,8},{9,1... | collective-permute-start | bytes 3145736 | tf_op jit(solution)/shard_map/ppermute | solution.py:407
  62.2 2.4 %collective-permute-start.18 = (f32[4,128,256]{2,1,0:T(8,128)S(1)}, f32[4,128,256]{2,1,0:T(8,128)S(1)}, u32[]{:S(2)}, u32[]{:S(2)}) collective-permute-start(f32[4,128,256]{2,1,0:T(8,128)S(1)} %get-tuple-element.39), channel_id=1, source_target_pairs={{0,4},{4,0},{1,5},{5,1},{2,6},{6,2},{3,7},{7,3},{8,12},{12,8},{9,1... | collective-permute-start | bytes 1572872 | tf_op jit(solution)/shard_map/ppermute | solution.py:407
  62.3 2.2 %collective-permute-start.21 = (bf16[512,256]{1,0:T(8,128)(2,1)S(1)}, bf16[512,256]{1,0:T(8,128)(2,1)S(1)}, u32[]{:S(2)}, u32[]{:S(2)}) collective-permute-start(bf16[512,256]{1,0:T(8,128)(2,1)S(1)} %shard_map.87), channel_id=1, source_target_pairs={{0,4},{4,0},{1,5},{5,1},{2,6},{6,2},{3,7},{7,3},{8,12},{12,8},{9,1... | collective-permute-start | bytes 786440 | tf_op jit(solution)/shard_map/ppermute | solution.py:407
  68.9 1.4 %collective-permute-start.22 = (bf16[512,128]{1,0:T(8,128)(2,1)S(1)}, bf16[512,128]{1,0:T(8,128)(2,1)S(1)}, u32[]{:S(2)}, u32[]{:S(2)}) collective-permute-start(bf16[512,128]{1,0:T(8,128)(2,1)S(1)} %shard_map.88.refs_5_), channel_id=1, source_target_pairs={{0,4},{4,0},{1,5},{5,1},{2,6},{6,2},{3,7},{7,3},{8,12},{12,8},{9,1... | collective-permute-start | bytes 393224 | tf_op jit(solution)/shard_map/ppermute | solution.py:407

commit v4 on v3

--- a/solution.py
+++ b/solution.py
@@ -85,8 +85,11 @@
         send_ref[:, cut] = jnp.where(c == 0, second, first).astype(BF16)
 
 
+PLACE = (0, 2, 3, 1)
+
+
 def hidden_piece(refs, r, s):
-    return refs[r][s]
+    return refs[PLACE[r]][PLACE[s]]
 
 
 def project_kernel(*refs):
@@ -445,22 +448,25 @@
     mine, upstream_rows = gather(scalars, packs)
     right_1, left_1 = shift(mine, "z", 8, 1), shift(mine, "z", 8, 7)
 
-    stack = jnp.stack([base] + [shift_plane(base, s, True) for s in (1, 2, 3)])
-    hid_right, hid_far, hid_left = [shift_plane(stack, n, False) for n in (1, 2, 3)]
+    stack = [base] + [shift_plane(base, s, True) for s in (3, 1, 2)]
+    right_b, left_b, *stack = lax.optimization_barrier((right_1, left_1, *stack))
+    stack = jnp.stack(stack)
+    hid_left, hid_right, hid_far = [shift_plane(stack, n, False) for n in (3, 1, 2)]
     right_2, left_2 = shift(right_1, "z", 8, 1), shift(left_1, "z", 8, 7)
 
     right_3, left_3 = shift(right_2, "z", 8, 1), shift(left_2, "z", 8, 7)
-    swap_a = swap(keys_of((mine, right_1, left_1)))
+    swap_a = swap(keys_of((mine, right_b, left_b), 100000))
 
     far_r, far_l = shift(right_3[:384], "z", 8, 1), shift(left_3[384:], "z", 8, 7)
-    *late, hid_right = lax.optimization_barrier((right_2, left_2, right_3, left_3, hid_right))
-    swap_b = swap(keys_of(late))
-    pieces = (stack, hid_right, hid_far, hid_left)
+    swap_b = swap(keys_of((right_2, left_2, right_3, left_3)))
+    pieces = (stack, hid_left, hid_right, hid_far)
 
     ring = (mine, right_1, left_1, right_2, left_2, right_3, left_3)
+    keys_c = keys_of((far_r, far_l), 4000000000)
+    far_r, far_l, keys_c = lax.optimization_barrier((far_r, far_l, keys_c))
+    swap_c = swap(keys_c)
     qt_keep, qt_send = project(where, (*pieces, *ring, far_r, far_l))
     qt_received = swap(qt_send)
-    swap_c = swap(keys_of((far_r, far_l), 20000000000))
     second_own = attend(
         (scalars,),
         (

time: 102 us -> 97.5 us (0.956); the launches traced: 101 us -> 97.7 us
  blocking collectives: 27.8 us -> 24.6 us
    all_to_all x1, blocking collectives: 27.8 us -> 24.6 us  [per_device(): shares = lax.all_to_all(partial, ('z', 'x'), 0, 0, tiled=True)]
where the time goes in v4:
time: 97.5 us; the launch traced here: 97.7 us
  starting transfers between devices  34.3 us (35%)
  waiting for transfers between devices  26.3 us (27%)
  blocking collectives  24.6 us (25%)
  Pallas kernels  11.3 us (12%)
    ppermute x17, waiting for transfers between devices, shift(): lax.ppermute(value, axis, [(i, (i + step) % size) for i in range(size)])  26.3 us
    all_to_all x1, blocking collectives, per_device(): shares = lax.all_to_all(partial, ('z', 'x'), 0, 0, tiled=True)  24.6 us
    ppermute x17, starting transfers between devices, shift(): lax.ppermute(value, axis, [(i, (i + step) % size) for i in range(size)])  24.3 us
    ppermute x6, starting transfers between devices, shift_plane(): return lax.ppermute(value, ('x', 'c', 'kvh'), pairs)  9.99 us
    pallas_call x7, Pallas kernels, call(): pl.pallas_call(kernel, out_shape=out_shape, in_specs=[SMEM_SPEC] * len(sc...  9.41 us
  transfers between devices with their start and end apart: 23, of which 9 were waited for; matrix products, arithmetic and copies ran while one was open for 0% of the time, Pallas kernels for 3%

profile of v4, /device:TPU:8, one launch (start us, length us, event | category | flops | bytes accessed | tf_op | source)
XLA Modules:
  0.0 97.7 jit_solution(7631003391388217325)
XLA Ops:
  0.0 0.1 pad_add_fusion.where_ref.refs_0_
  0.1 1.9 %shard_map.82 = (bf16[256,256]{1,0:T(8,128)(2,1)S(1)}, bf16[256,256]{1,0:T(8,128)(2,1)S(1)}, bf16[256,256]{1,0:T(8,128)(2,1)S(1)}, bf16[256,256]{1,0:T(8,128)(2,...) custom-call(s32[4]{0:T(128)S(1)} %pad_add_fusion.where_ref.refs_0_, bf16[128,1024]{1,0:T(8,128)(2,1)} %hidden_hbm.1, ...), custom_call_target="tpu_custom_call" | custom-call | flops 1000000 | bytes 600000 | tf_op jit(solution)/shard_map/pallas_call | solution.py:355
  2.0 0.1 collective-permute-start
  2.1 1.6 %collective-permute-start.1 = (bf16[256,256]{1,0:T(8,128)(2,1)S(1)}, bf16[256,256]{1,0:T(8,128)(2,1)S(1)}, u32[]{:S(2)}, u32[]{:S(2)}) collective-permute-start(bf16[256,256]{1,0:T(8,128)(2,1)S(1)} %get-tuple-element.32), channel_id=1, source_target_pairs={{0,8},{8,16},{16,24},{24,0},{1,9},{9,17},{17,25},{25,1},{2,10},{10... | collective-permute-start | bytes 393224 | tf_op jit(solution)/shard_map/ppermute | solution.py:410
  3.6 0.0 copy-start
  3.6 0.0 copy-start.1
  3.6 2.7 %collective-permute-start.2 = (bf16[256,256]{1,0:T(8,128)(2,1)S(1)}, bf16[256,256]{1,0:T(8,128)(2,1)S(1)}, u32[]{:S(2)}, u32[]{:S(2)}) collective-permute-start(bf16[256,256]{1,0:T(8,128)(2,1)S(1)} %get-tuple-element.33), channel_id=1, source_target_pairs={{0,16},{8,24},{16,0},{24,8},{1,17},{9,25},{17,1},{25,9},{2,18},{10... | collective-permute-start | bytes 393224 | tf_op jit(solution)/shard_map/ppermute | solution.py:410
  6.4 1.4 %collective-permute-start.3 = (bf16[256,256]{1,0:T(8,128)(2,1)S(1)}, bf16[256,256]{1,0:T(8,128)(2,1)S(1)}, u32[]{:S(2)}, u32[]{:S(2)}) collective-permute-start(bf16[256,256]{1,0:T(8,128)(2,1)S(1)} %get-tuple-element.34), channel_id=1, source_target_pairs={{0,24},{8,0},{16,8},{24,16},{1,25},{9,1},{17,9},{25,17},{2,26},{10... | collective-permute-start | bytes 393224 | tf_op jit(solution)/shard_map/ppermute | solution.py:410
  7.8 0.0 copy-done
  7.8 0.0 copy-done.1
  7.8 0.1 concatenate.7.refs_0_
  7.9 0.0 collective-permute-done
  7.9 1.3 %collective-permute-done.1.refs_2_ = bf16[256,256]{1,0:T(8,128)(2,1)S(1)} collective-permute-done((bf16[256,256]{1,0:T(8,128)(2,1)S(1)}, bf16[256,256]{1,0:T(8,128)(2,1)S(1)}, u32[]{:S(2)}, u32[]{:S(2)}) %collective-permute-start.1) | collective-permute-done | bytes 131104 | tf_op jit(solution)/shard_map/ppermute | solution.py:410
  9.2 3.8 %collective-permute-done.2.refs_3_ = bf16[256,256]{1,0:T(8,128)(2,1)S(1)} collective-permute-done((bf16[256,256]{1,0:T(8,128)(2,1)S(1)}, bf16[256,256]{1,0:T(8,128)(2,1)S(1)}, u32[]{:S(2)}, u32[]{:S(2)}) %collective-permute-start.2) | collective-permute-done | bytes 131104 | tf_op jit(solution)/shard_map/ppermute | solution.py:410
  13.0 0.0 collective-permute-done.3.refs_4_
  13.0 0.6 shard_map.83
  13.6 5.9 %collective-permute-start.5 = (bf16[768,256]{1,0:T(8,128)(2,1)S(1)}, bf16[768,256]{1,0:T(8,128)(2,1)S(1)}, u32[]{:S(2)}, u32[]{:S(2)}) collective-permute-start(bf16[768,256]{1,0:T(8,128)(2,1)S(1)} %get-tuple-element.39.refs_5_.refs_0_.refs_3_), channel_id=1, source_target_pairs={{0,224},{32,0},{64,32},{96,64},{128,96},{160,128},{192,160},{224,1... | collective-permute-start | bytes 1179656 | tf_op jit(solution)/shard_map/ppermute | solution.py:410
  19.5 0.0 collective-permute-start.4
  19.5 2.3 %collective-permute-start.8 = (bf16[256,512]{1,0:T(8,128)(2,1)S(1)}, bf16[256,512]{1,0:T(8,128)(2,1)S(1)}, u32[]{:S(2)}, u32[]{:S(2)}) collective-permute-start(bf16[256,512]{1,0:T(8,128)(2,1)S(1)} %pad_maximum_fusion.1), channel_id=1, source_target_pairs={{0,2},{1,3},{2,0},{3,1},{4,20},{5,21},{6,22},{7,23},{8,10},{9,11},... | collective-permute-start | bytes 786440 | tf_op jit(solution)/shard_map/ppermute | solution.py:425
  21.8 0.0 collective-permute-start.7
  21.8 2.0 %collective-permute-start.6 = (bf16[256,512]{1,0:T(8,128)(2,1)S(1)}, bf16[256,512]{1,0:T(8,128)(2,1)S(1)}, u32[]{:S(2)}, u32[]{:S(2)}) collective-permute-start(bf16[256,512]{1,0:T(8,128)(2,1)S(1)} %pad_maximum_fusion.1), channel_id=1, source_target_pairs={{0,3},{1,0},{2,1},{3,2},{4,28},{5,29},{6,30},{7,31},{8,11},{9,8},{... | collective-permute-start | bytes 786440 | tf_op jit(solution)/shard_map/ppermute | solution.py:425
  23.8 3.9 %collective-permute-done.5.refs_7_.refs_2_.refs_5_ = bf16[768,256]{1,0:T(8,128)(2,1)S(1)} collective-permute-done((bf16[768,256]{1,0:T(8,128)(2,1)S(1)}, bf16[768,256]{1,0:T(8,128)(2,1)S(1)}, u32[]{:S(2)}, u32[]{:S(2)}) %collective-permute-start.5) | collective-permute-done | bytes 393248 | tf_op jit(solution)/shard_map/ppermute | solution.py:410
  27.7 3.7 %collective-permute-start.13 = (bf16[768,256]{1,0:T(8,128)(2,1)S(1)}, bf16[768,256]{1,0:T(8,128)(2,1)S(1)}, u32[]{:S(2)}, u32[]{:S(2)}) collective-permute-start(bf16[768,256]{1,0:T(8,128)(2,1)S(1)} %collective-permute-done.5.refs_7_.refs_2_.refs_5_), channel_id=1, source_target_pairs={{0,224},{32,0},{64,32},{96,64},{128,96},{160,128},{192,160},{224,1... | collective-permute-start | bytes 1179656 | tf_op jit(solution)/shard_map/ppermute | solution.py:410
  31.4 0.0 collective-permute-done.4.refs_6_.refs_1_.refs_4_
  31.4 0.0 collective-permute-start.12
  31.4 0.0 collective-permute-done.8
  31.4 0.0 collective-permute-done.7
  31.4 0.0 collective-permute-done.6
  31.4 0.1 pad_maximum_fusion.refs_1_
  31.6 2.4 %collective-permute-start.11 = (bf16[4,256,512]{2,1,0:T(8,128)(2,1)S(1)}, bf16[4,256,512]{2,1,0:T(8,128)(2,1)S(1)}, u32[]{:S(2)}, u32[]{:S(2)}) collective-permute-start(bf16[4,256,512]{2,1,0:T(8,128)(2,1)S(1)} %pad_maximum_fusion.refs_1_), channel_id=1, source_target_pairs={{0,16},{1,17},{2,18},{3,19},{4,6},{5,7},{6,4},{7,5},{8,24},{9,25},... | collective-permute-start | bytes 3145736 | tf_op jit(solution)/shard_map/ppermute | solution.py:425
  34.0 0.8 collective-permute-start.10
  34.8 2.5 %collective-permute-start.9 = (bf16[4,256,512]{2,1,0:T(8,128)(2,1)S(1)}, bf16[4,256,512]{2,1,0:T(8,128)(2,1)S(1)}, u32[]{:S(2)}, u32[]{:S(2)}) collective-permute-start(bf16[4,256,512]{2,1,0:T(8,128)(2,1)S(1)} %pad_maximum_fusion.refs_1_), channel_id=1, source_target_pairs={{0,24},{1,25},{2,26},{3,27},{4,7},{5,4},{6,5},{7,6},{8,0},{9,1},{1... | collective-permute-start | bytes 3145736 | tf_op jit(solution)/shard_map/ppermute | solution.py:425
  37.2 1.4 %collective-permute-done.13.refs_9_.refs_1_.refs_7_ = bf16[768,256]{1,0:T(8,128)(2,1)S(1)} collective-permute-done((bf16[768,256]{1,0:T(8,128)(2,1)S(1)}, bf16[768,256]{1,0:T(8,128)(2,1)S(1)}, u32[]{:S(2)}, u32[]{:S(2)}) %collective-permute-start.13) | collective-permute-done | bytes 393248 | tf_op jit(solution)/shard_map/ppermute | solution.py:410
  38.7 3.7 %collective-permute-start.15 = (bf16[768,256]{1,0:T(8,128)(2,1)S(1)}, bf16[768,256]{1,0:T(8,128)(2,1)S(1)}, u32[]{:S(2)}, u32[]{:S(2)}) collective-permute-start(bf16[768,256]{1,0:T(8,128)(2,1)S(1)} %collective-permute-done.13.refs_9_.refs_1_.refs_7_), channel_id=1, source_target_pairs={{0,224},{32,0},{64,32},{96,64},{128,96},{160,128},{192,160},{224,1... | collective-permute-start | bytes 1179656 | tf_op jit(solution)/shard_map/ppermute | solution.py:410
  42.4 0.0 collective-permute-done.12.refs_8_.refs_0_.refs_6_
  42.4 0.0 collective-permute-start.14
  42.4 6.4 %collective-permute-done.15.refs_11_.refs_3_.refs_9_ = bf16[768,256]{1,0:T(8,128)(2,1)S(1)} collective-permute-done((bf16[768,256]{1,0:T(8,128)(2,1)S(1)}, bf16[768,256]{1,0:T(8,128)(2,1)S(1)}, u32[]{:S(2)}, u32[]{:S(2)}) %collective-permute-start.15) | collective-permute-done | bytes 393248 | tf_op jit(solution)/shard_map/ppermute | solution.py:410
  48.7 3.9 %collective-permute-start.17 = (bf16[384,256]{1,0:T(8,128)(2,1)S(1)}, bf16[384,256]{1,0:T(8,128)(2,1)S(1)}, u32[]{:S(2)}, u32[]{:S(2)}) collective-permute-start(bf16[384,256]{1,0:T(8,128)(2,1)S(1)} %slice.9), channel_id=1, source_target_pairs={{0,224},{32,0},{64,32},{96,64},{128,96},{160,128},{192,160},{224,1... | collective-permute-start | bytes 589832 | tf_op jit(solution)/shard_map/ppermute | solution.py:410
  52.7 0.0 collective-permute-done.14.refs_10_.refs_2_.refs_8_
  52.7 0.1 collective-permute-start.16
  52.8 0.1 shard_map.87
  52.9 3.0 %collective-permute-done.17.refs_1_.refs_13_.refs_11_ = bf16[384,256]{1,0:T(8,128)(2,1)S(1)} collective-permute-done((bf16[384,256]{1,0:T(8,128)(2,1)S(1)}, bf16[384,256]{1,0:T(8,128)(2,1)S(1)}, u32[]{:S(2)}, u32[]{:S(2)}) %collective-permute-start.17) | collective-permute-done | bytes 196640 | tf_op jit(solution)/shard_map/ppermute | solution.py:410
  55.9 0.0 collective-permute-start.20
  55.9 0.1 shard_map.86
  55.9 3.7 %collective-permute-done.16.refs_0_.refs_12_.refs_10_ = bf16[384,256]{1,0:T(8,128)(2,1)S(1)} collective-permute-done((bf16[384,256]{1,0:T(8,128)(2,1)S(1)}, bf16[384,256]{1,0:T(8,128)(2,1)S(1)}, u32[]{:S(2)}, u32[]{:S(2)}) %collective-permute-start.16) | collective-permute-done | bytes 196640 | tf_op jit(solution)/shard_map/ppermute | solution.py:410
  59.7 0.0 collective-permute-start.19
  59.7 0.0 collective-permute-done.11.refs_4_
  59.7 0.0 collective-permute-done.10.refs_3_
  59.7 0.0 collective-permute-done.9.refs_2_
  59.7 2.6 %shard_map.85 = (f32[4,128,256]{2,1,0:T(8,128)S(1)}, f32[4,128,256]{2,1,0:T(8,128)S(1)}) custom-call(s32[4]{0:T(128)S(1)} %pad_add_fusion.where_ref.refs_0_, bf16[4,256,512]{2,1,0:T(8,128)(2,1)S(1)} %pad_maximum_fusion.refs_1_, bf16[4,256,512]{2,1,0:T(8,128)(2,1)S(1)} %collective-permute-done.9.refs_2_, ...), custom_call_target="tpu_custom_call" | custom-call | flops 1000000000 | bytes 8000000 | tf_op jit(solution)/shard_map/pallas_call | solution.py:340
  62.3 0.6 collective-permute-start.18
  62.9 0.1 collective-permute-start.21
  63.0 0.0 collective-permute-done.19.refs_12_
  63.0 1.8 %collective-permute-done.21.refs_14_ = bf16[512,256]{1,0:T(8,128)(2,1)S(1)} collective-permute-done((bf16[512,256]{1,0:T(8,128)(2,1)S(1)}, bf16[512,256]{1,0:T(8,128)(2,1)S(1)}, u32[]{:S(2)}, u32[]{:S(2)}) %collective-permute-start.21) | collective-permute-done | bytes 262176 | tf_op jit(solution)/shard_map/ppermute | solution.py:410
  64.8 0.0 collective-permute-done.18.refs_2_
  64.8 0.0 collective-permute-done.20.refs_13_
  64.8 4.3 %shard_map.88.refs_5_ = bf16[512,128]{1,0:T(8,128)(2,1)S(1)} custom-call(s32[148]{0:T(256)S(1)} %concatenate.7.refs_0_, f32[4,128,256]{2,1,0:T(8,128)S(1)} %get-tuple-element.47.refs_1_, f32[4,128,256]{2,1,0:T(8,128)S(1)} %collective-permute-done.18.refs_2_, bf16[768,256]{1,0:T(8,128)(2,1)S(1)} %get-tuple-element.39.refs_5_.refs_0_.refs_3_, ...), custom_call_target="tpu_custom_call" | custom-call | flops 2000000000 | bytes 8000000 | tf_op jit(solution)/shard_map/pallas_call | solution.py:340
  69.1 0.5 collective-permute-start.22
  69.6 1.0 %collective-permute-done.22.refs_6_ = bf16[512,128]{1,0:T(8,128)(2,1)S(1)} collective-permute-done((bf16[512,128]{1,0:T(8,128)(2,1)S(1)}, bf16[512,128]{1,0:T(8,128)(2,1)S(1)}, u32[]{:S(2)}, u32[]{:S(2)}) %collective-permute-start.22) | collective-permute-done | bytes 131104 | tf_op jit(solution)/shard_map/ppermute | solution.py:410
  70.6 1.8 %shard_map.89 = bf16[2048,128]{1,0:T(8,128)(2,1)S(1)} custom-call(s32[4]{0:T(128)S(1)} %pad_add_fusion.where_ref.refs_0_, bf16[4,256,512]{2,1,0:T(8,128)(2,1)S(1)} %pad_maximum_fusion.refs_1_, bf16[4,256,512]{2,1,0:T(8,128)(2,1)S(1)} %collective-permute-done.9.refs_2_, bf16[4,256,512]{2,1,0:T(8,128)(2,1)S(1)} %collective-permute-done.10.refs_3_, ...), custom_call_target="tpu_custom_call" | custom-call | flops 600000000 | bytes 8000000 | tf_op jit(solution)/shard_map/pallas_call | solution.py:340
  72.3 24.6 %all_to_all.9 = bf16[32,64,128]{2,1,0:T(8,128)(2,1)S(1)} all-to-all(bf16[32,64,128]{2,1,0:T(8,128)(2,1)S(1)} %bitcast.17), channel_id=1, replica_groups=mesh['z'=8,'x'=4,'c'=2,'kvh'=4] {'z','x'}, dimensions={0} | all-to-all | bytes 1048576 | tf_op jit(solution)/shard_map/all_to_all | solution.py:486
  97.0 0.1 convert_reduce_fusion
  97.1 0.7 copy_bitcast_fusion
  (4 shorter events, 0.1 us)
Async XLA Ops:
  2.0 5.9 %collective-permute-start = (bf16[128,512]{1,0:T(8,128)(2,1)S(1)}, bf16[128,512]{1,0:T(8,128)(2,1)S(1)}, u32[]{:S(2)}, u32[]{:S(2)}) collective-permute-start(bf16[128,512]{1,0:T(8,128)(2,1)S(1)} %get-tuple-element.30), channel_id=1, source_target_pairs={{0,4},{4,0},{1,5},{5,1},{2,6},{6,2},{3,7},{7,3},{8,12},{12,8},{9,1... | collective-permute-start | bytes 393224 | tf_op jit(solution)/shard_map/ppermute | solution.py:410
  2.1 7.1 %collective-permute-start.1 = (bf16[256,256]{1,0:T(8,128)(2,1)S(1)}, bf16[256,256]{1,0:T(8,128)(2,1)S(1)}, u32[]{:S(2)}, u32[]{:S(2)}) collective-permute-start(bf16[256,256]{1,0:T(8,128)(2,1)S(1)} %get-tuple-element.32), channel_id=1, source_target_pairs={{0,8},{8,16},{16,24},{24,0},{1,9},{9,17},{17,25},{25,1},{2,10},{10... | collective-permute-start | bytes 393224 | tf_op jit(solution)/shard_map/ppermute | solution.py:410
  3.6 4.2 %copy-start = (s32[128]{0:T(128)S(1)}, s32[128]{0:T(128)}, u32[]{:S(2)}) copy-start(s32[128]{0:T(128)} %param.15) | copy-start | bytes 1540
  3.6 4.2 %copy-start.1 = (s32[16]{0:T(128)S(1)}, s32[16]{0:T(128)}, u32[]{:S(2)}) copy-start(s32[16]{0:T(128)} %param.14) | copy-start | bytes 196
  3.6 9.3 %collective-permute-start.2 = (bf16[256,256]{1,0:T(8,128)(2,1)S(1)}, bf16[256,256]{1,0:T(8,128)(2,1)S(1)}, u32[]{:S(2)}, u32[]{:S(2)}) collective-permute-start(bf16[256,256]{1,0:T(8,128)(2,1)S(1)} %get-tuple-element.33), channel_id=1, source_target_pairs={{0,16},{8,24},{16,0},{24,8},{1,17},{9,25},{17,1},{25,9},{2,18},{10... | collective-permute-start | bytes 393224 | tf_op jit(solution)/shard_map/ppermute | solution.py:410
  6.4 6.6 %collective-permute-start.3 = (bf16[256,256]{1,0:T(8,128)(2,1)S(1)}, bf16[256,256]{1,0:T(8,128)(2,1)S(1)}, u32[]{:S(2)}, u32[]{:S(2)}) collective-permute-start(bf16[256,256]{1,0:T(8,128)(2,1)S(1)} %get-tuple-element.34), channel_id=1, source_target_pairs={{0,24},{8,0},{16,8},{24,16},{1,25},{9,1},{17,9},{25,17},{2,26},{10... | collective-permute-start | bytes 393224 | tf_op jit(solution)/shard_map/ppermute | solution.py:410
  13.6 14.1 %collective-permute-start.5 = (bf16[768,256]{1,0:T(8,128)(2,1)S(1)}, bf16[768,256]{1,0:T(8,128)(2,1)S(1)}, u32[]{:S(2)}, u32[]{:S(2)}) collective-permute-start(bf16[768,256]{1,0:T(8,128)(2,1)S(1)} %get-tuple-element.39.refs_5_.refs_0_.refs_3_), channel_id=1, source_target_pairs={{0,224},{32,0},{64,32},{96,64},{128,96},{160,128},{192,160},{224,1... | collective-permute-start | bytes 1179656 | tf_op jit(solution)/shard_map/ppermute | solution.py:410
  19.5 11.9 %collective-permute-start.4 = (bf16[768,256]{1,0:T(8,128)(2,1)S(1)}, bf16[768,256]{1,0:T(8,128)(2,1)S(1)}, u32[]{:S(2)}, u32[]{:S(2)}) collective-permute-start(bf16[768,256]{1,0:T(8,128)(2,1)S(1)} %get-tuple-element.39.refs_5_.refs_0_.refs_3_), channel_id=1, source_target_pairs={{0,32},{32,64},{64,96},{96,128},{128,160},{160,192},{192,224},{224... | collective-permute-start | bytes 1179656 | tf_op jit(solution)/shard_map/ppermute | solution.py:410
  19.5 11.9 %collective-permute-start.8 = (bf16[256,512]{1,0:T(8,128)(2,1)S(1)}, bf16[256,512]{1,0:T(8,128)(2,1)S(1)}, u32[]{:S(2)}, u32[]{:S(2)}) collective-permute-start(bf16[256,512]{1,0:T(8,128)(2,1)S(1)} %pad_maximum_fusion.1), channel_id=1, source_target_pairs={{0,2},{1,3},{2,0},{3,1},{4,20},{5,21},{6,22},{7,23},{8,10},{9,11},... | collective-permute-start | bytes 786440 | tf_op jit(solution)/shard_map/ppermute | solution.py:425
  21.8 9.6 %collective-permute-start.7 = (bf16[256,512]{1,0:T(8,128)(2,1)S(1)}, bf16[256,512]{1,0:T(8,128)(2,1)S(1)}, u32[]{:S(2)}, u32[]{:S(2)}) collective-permute-start(bf16[256,512]{1,0:T(8,128)(2,1)S(1)} %pad_maximum_fusion.1), channel_id=1, source_target_pairs={{0,1},{1,2},{2,3},{3,0},{4,12},{5,13},{6,14},{7,15},{8,9},{9,10},{... | collective-permute-start | bytes 786440 | tf_op jit(solution)/shard_map/ppermute | solution.py:425
  21.8 9.6 %collective-permute-start.6 = (bf16[256,512]{1,0:T(8,128)(2,1)S(1)}, bf16[256,512]{1,0:T(8,128)(2,1)S(1)}, u32[]{:S(2)}, u32[]{:S(2)}) collective-permute-start(bf16[256,512]{1,0:T(8,128)(2,1)S(1)} %pad_maximum_fusion.1), channel_id=1, source_target_pairs={{0,3},{1,0},{2,1},{3,2},{4,28},{5,29},{6,30},{7,31},{8,11},{9,8},{... | collective-permute-start | bytes 786440 | tf_op jit(solution)/shard_map/ppermute | solution.py:425
  27.7 11.0 %collective-permute-start.13 = (bf16[768,256]{1,0:T(8,128)(2,1)S(1)}, bf16[768,256]{1,0:T(8,128)(2,1)S(1)}, u32[]{:S(2)}, u32[]{:S(2)}) collective-permute-start(bf16[768,256]{1,0:T(8,128)(2,1)S(1)} %collective-permute-done.5.refs_7_.refs_2_.refs_5_), channel_id=1, source_target_pairs={{0,224},{32,0},{64,32},{96,64},{128,96},{160,128},{192,160},{224,1... | collective-permute-start | bytes 1179656 | tf_op jit(solution)/shard_map/ppermute | solution.py:410
  31.4 11.0 %collective-permute-start.12 = (bf16[768,256]{1,0:T(8,128)(2,1)S(1)}, bf16[768,256]{1,0:T(8,128)(2,1)S(1)}, u32[]{:S(2)}, u32[]{:S(2)}) collective-permute-start(bf16[768,256]{1,0:T(8,128)(2,1)S(1)} %collective-permute-done.4.refs_6_.refs_1_.refs_4_), channel_id=1, source_target_pairs={{0,32},{32,64},{64,96},{96,128},{128,160},{160,192},{192,224},{224... | collective-permute-start | bytes 1179656 | tf_op jit(solution)/shard_map/ppermute | solution.py:410
  31.6 28.1 %collective-permute-start.11 = (bf16[4,256,512]{2,1,0:T(8,128)(2,1)S(1)}, bf16[4,256,512]{2,1,0:T(8,128)(2,1)S(1)}, u32[]{:S(2)}, u32[]{:S(2)}) collective-permute-start(bf16[4,256,512]{2,1,0:T(8,128)(2,1)S(1)} %pad_maximum_fusion.refs_1_), channel_id=1, source_target_pairs={{0,16},{1,17},{2,18},{3,19},{4,6},{5,7},{6,4},{7,5},{8,24},{9,25},... | collective-permute-start | bytes 3145736 | tf_op jit(solution)/shard_map/ppermute | solution.py:425
  34.0 25.7 %collective-permute-start.10 = (bf16[4,256,512]{2,1,0:T(8,128)(2,1)S(1)}, bf16[4,256,512]{2,1,0:T(8,128)(2,1)S(1)}, u32[]{:S(2)}, u32[]{:S(2)}) collective-permute-start(bf16[4,256,512]{2,1,0:T(8,128)(2,1)S(1)} %pad_maximum_fusion.refs_1_), channel_id=1, source_target_pairs={{0,8},{1,9},{2,10},{3,11},{4,5},{5,6},{6,7},{7,4},{8,16},{9,17},{1... | collective-permute-start | bytes 3145736 | tf_op jit(solution)/shard_map/ppermute | solution.py:425
  34.8 24.9 %collective-permute-start.9 = (bf16[4,256,512]{2,1,0:T(8,128)(2,1)S(1)}, bf16[4,256,512]{2,1,0:T(8,128)(2,1)S(1)}, u32[]{:S(2)}, u32[]{:S(2)}) collective-permute-start(bf16[4,256,512]{2,1,0:T(8,128)(2,1)S(1)} %pad_maximum_fusion.refs_1_), channel_id=1, source_target_pairs={{0,24},{1,25},{2,26},{3,27},{4,7},{5,4},{6,5},{7,6},{8,0},{9,1},{1... | collective-permute-start | bytes 3145736 | tf_op jit(solution)/shard_map/ppermute | solution.py:425
  38.7 10.1 %collective-permute-start.15 = (bf16[768,256]{1,0:T(8,128)(2,1)S(1)}, bf16[768,256]{1,0:T(8,128)(2,1)S(1)}, u32[]{:S(2)}, u32[]{:S(2)}) collective-permute-start(bf16[768,256]{1,0:T(8,128)(2,1)S(1)} %collective-permute-done.13.refs_9_.refs_1_.refs_7_), channel_id=1, source_target_pairs={{0,224},{32,0},{64,32},{96,64},{128,96},{160,128},{192,160},{224,1... | collective-permute-start | bytes 1179656 | tf_op jit(solution)/shard_map/ppermute | solution.py:410
  42.4 10.3 %collective-permute-start.14 = (bf16[768,256]{1,0:T(8,128)(2,1)S(1)}, bf16[768,256]{1,0:T(8,128)(2,1)S(1)}, u32[]{:S(2)}, u32[]{:S(2)}) collective-permute-start(bf16[768,256]{1,0:T(8,128)(2,1)S(1)} %collective-permute-done.12.refs_8_.refs_0_.refs_6_), channel_id=1, source_target_pairs={{0,32},{32,64},{64,96},{96,128},{128,160},{160,192},{192,224},{224... | collective-permute-start | bytes 1179656 | tf_op jit(solution)/shard_map/ppermute | solution.py:410
  48.7 7.1 %collective-permute-start.17 = (bf16[384,256]{1,0:T(8,128)(2,1)S(1)}, bf16[384,256]{1,0:T(8,128)(2,1)S(1)}, u32[]{:S(2)}, u32[]{:S(2)}) collective-permute-start(bf16[384,256]{1,0:T(8,128)(2,1)S(1)} %slice.9), channel_id=1, source_target_pairs={{0,224},{32,0},{64,32},{96,64},{128,96},{160,128},{192,160},{224,1... | collective-permute-start | bytes 589832 | tf_op jit(solution)/shard_map/ppermute | solution.py:410
  52.7 7.0 %collective-permute-start.16 = (bf16[384,256]{1,0:T(8,128)(2,1)S(1)}, bf16[384,256]{1,0:T(8,128)(2,1)S(1)}, u32[]{:S(2)}, u32[]{:S(2)}) collective-permute-start(bf16[384,256]{1,0:T(8,128)(2,1)S(1)} %slice.8), channel_id=1, source_target_pairs={{0,32},{32,64},{64,96},{96,128},{128,160},{160,192},{192,224},{224... | collective-permute-start | bytes 589832 | tf_op jit(solution)/shard_map/ppermute | solution.py:410
  55.9 8.9 %collective-permute-start.20 = (bf16[2048,256]{1,0:T(8,128)(2,1)S(1)}, bf16[2048,256]{1,0:T(8,128)(2,1)S(1)}, u32[]{:S(2)}, u32[]{:S(2)}) collective-permute-start(bf16[2048,256]{1,0:T(8,128)(2,1)S(1)} %shard_map.87), channel_id=1, source_target_pairs={{0,4},{4,0},{1,5},{5,1},{2,6},{6,2},{3,7},{7,3},{8,12},{12,8},{9,1... | collective-permute-start | bytes 3145736 | tf_op jit(solution)/shard_map/ppermute | solution.py:410
  59.7 3.3 %collective-permute-start.19 = (bf16[1536,256]{1,0:T(8,128)(2,1)S(1)}, bf16[1536,256]{1,0:T(8,128)(2,1)S(1)}, u32[]{:S(2)}, u32[]{:S(2)}) collective-permute-start(bf16[1536,256]{1,0:T(8,128)(2,1)S(1)} %shard_map.86), channel_id=1, source_target_pairs={{0,4},{4,0},{1,5},{5,1},{2,6},{6,2},{3,7},{7,3},{8,12},{12,8},{9,1... | collective-permute-start | bytes 2359304 | tf_op jit(solution)/shard_map/ppermute | solution.py:410
  62.3 2.5 %collective-permute-start.18 = (f32[4,128,256]{2,1,0:T(8,128)S(1)}, f32[4,128,256]{2,1,0:T(8,128)S(1)}, u32[]{:S(2)}, u32[]{:S(2)}) collective-permute-start(f32[4,128,256]{2,1,0:T(8,128)S(1)} %get-tuple-element.48), channel_id=1, source_target_pairs={{0,4},{4,0},{1,5},{5,1},{2,6},{6,2},{3,7},{7,3},{8,12},{12,8},{9,1... | collective-permute-start | bytes 1572872 | tf_op jit(solution)/shard_map/ppermute | solution.py:410
  62.9 1.9 %collective-permute-start.21 = (bf16[512,256]{1,0:T(8,128)(2,1)S(1)}, bf16[512,256]{1,0:T(8,128)(2,1)S(1)}, u32[]{:S(2)}, u32[]{:S(2)}) collective-permute-start(bf16[512,256]{1,0:T(8,128)(2,1)S(1)} %shard_map.84), channel_id=1, source_target_pairs={{0,4},{4,0},{1,5},{5,1},{2,6},{6,2},{3,7},{7,3},{8,12},{12,8},{9,1... | collective-permute-start | bytes 786440 | tf_op jit(solution)/shard_map/ppermute | solution.py:410
  69.1 1.4 %collective-permute-start.22 = (bf16[512,128]{1,0:T(8,128)(2,1)S(1)}, bf16[512,128]{1,0:T(8,128)(2,1)S(1)}, u32[]{:S(2)}, u32[]{:S(2)}) collective-permute-start(bf16[512,128]{1,0:T(8,128)(2,1)S(1)} %shard_map.88.refs_5_), channel_id=1, source_target_pairs={{0,4},{4,0},{1,5},{5,1},{2,6},{6,2},{3,7},{7,3},{8,12},{12,8},{9,1... | collective-permute-start | bytes 393224 | tf_op jit(solution)/shard_map/ppermute | solution.py:410

commit v5 on v4

--- a/solution.py
+++ b/solution.py
@@ -27,7 +27,6 @@
 
 def prepare_kernel(
     where_ref,
-    hidden_hbm,
     query_hbm,
     probe_hbm,
     key_hbm,
@@ -37,9 +36,6 @@
     pack1_ref,
     pack2_ref,
     pack3_ref,
-    keep_ref,
-    send_ref,
-    hidden_ref,
     query_ref,
     probe_ref,
     key_ref,
@@ -47,7 +43,7 @@
     upstream_ref,
     sems,
 ):
-    x, c = where_ref[1], where_ref[2]
+    x = where_ref[1]
     copies = [
         pltpu.make_async_copy(src, dst, sems.at[i])
         for i, (src, dst) in enumerate(
@@ -57,13 +53,12 @@
                 (key_hbm, key_ref),
                 (value_hbm, value_ref),
                 (upstream_hbm, upstream_ref),
-                (hidden_hbm, hidden_ref),
             )
         )
     ]
     for copy in copies:
         copy.start()
-    for copy in copies[:5]:
+    for copy in copies:
         copy.wait()
     for dx, pack in enumerate((pack0_ref, pack1_ref, pack2_ref, pack3_ref)):
         columns = pl.ds(pl.multiple_of(lax.rem(x + dx, 4) * HD, HD), HD)
@@ -73,16 +68,18 @@
         pack[64:192, 128:256] = value_ref[...]
         pack[192:256, 0:128] = upstream_ref[0:64, columns]
         pack[192:256, 128:256] = upstream_ref[64:128, columns]
-    copies[5].wait()
+
+
+def select_kernel(where_ref, own_ref, other_ref, base_ref):
+    c = where_ref[2]
     low = lax.broadcasted_iota(I32, (128, 128), 1) < 64
-    for k in range(4):
-        a = hidden_ref[:, 256 * k : 256 * k + 128].astype(F32)
-        b = hidden_ref[:, 256 * k + 128 : 256 * k + 256].astype(F32)
-        first = jnp.where(low, a, pltpu.roll(b, 64, 1))
-        second = jnp.where(low, pltpu.roll(a, 64, 1), b)
-        cut = slice(128 * k, 128 * k + 128)
-        keep_ref[:, cut] = jnp.where(c == 0, first, second).astype(BF16)
-        send_ref[:, cut] = jnp.where(c == 0, second, first).astype(BF16)
+    for rows, ref in ((slice(0, 128), own_ref), (slice(128, 256), other_ref)):
+        for k in range(4):
+            a = ref[:, 256 * k : 256 * k + 128].astype(F32)
+            b = ref[:, 256 * k + 128 : 256 * k + 256].astype(F32)
+            first = jnp.where(low, a, pltpu.roll(b, 64, 1))
+            second = jnp.where(low, pltpu.roll(a, 64, 1), b)
+            base_ref[rows, 128 * k : 128 * k + 128] = jnp.where(c == 0, first, second).astype(BF16)
 
 
 PLACE = (0, 2, 3, 1)
@@ -95,7 +92,7 @@
 def project_kernel(*refs):
     where_ref, hidden = refs[0], refs[1:5]
     packs, far_r, far_l = refs[5:12], refs[12], refs[13]
-    keep_ref, send_ref, weights, total = refs[14:]
+    keep_ref, send_ref, weights = refs[14:]
     z, x, c, y = where_ref[0], where_ref[1], where_ref[2], where_ref[3]
 
     def place(pack, dz, places=(0, 1, 2, 3)):
@@ -109,16 +106,25 @@
     place(far_r, 4, (0, 1))
     place(far_l, 4, (2, 3))
 
-    total[...] = jnp.zeros((4, 256, 256), F32)
-    for r in range(4):
-        for s in range(4):
-            dx = jnp.where(c == 0, r, s)
-            dy = jnp.where(c == 0, s, r)
+    def products(piece):
+        rows = []
+        for dy in range(4):
             group = lax.rem(y - dy + 4, 4)
-            w = weights[pl.ds(group * 2, 2)].reshape(512, 256)
-            total[dx] += jnp.dot(hidden_piece(hidden, r, s), w, preferred_element_type=F32)
-    keep_ref[...] = total[:, 0:128, :]
-    send_ref[...] = total[:, 128:256, :]
+            rows.append(weights[pl.ds(group * 2, 2)].reshape(512, 256))
+        w = jnp.concatenate(rows, axis=0)
+        for dx in range(4):
+            tokens = jnp.concatenate([piece(dx, dy) for dy in range(4)], axis=1)
+            total = jnp.dot(tokens, w, preferred_element_type=F32)
+            keep_ref[dx] = total[0:128]
+            send_ref[dx] = total[128:256]
+
+    @pl.when(c == 0)
+    def _():
+        products(lambda dx, dy: hidden_piece(hidden, dx, dy))
+
+    @pl.when(c == 1)
+    def _():
+        products(lambda dx, dy: hidden_piece(hidden, dy, dx))
 
 
 def attend_kernel(*refs):
@@ -296,28 +302,32 @@
 
 def curvature_kernel(*refs):
     where_ref, hidden = refs[0], refs[1:5]
-    second_own, second_other, out_ref, second_t, total = refs[5:]
+    second_own, second_other, out_ref, second_t = refs[5:]
     c, y = where_ref[2], where_ref[3]
     for dx in range(4):
         rows = slice(dx * 128, dx * 128 + 128)
         both = jnp.concatenate([second_own[rows, :], second_other[rows, :]], axis=0)
-        second_t[dx] = both.astype(F32).T.astype(BF16)
-    total[...] = jnp.zeros((4, 128, 512), F32)
-    for r in range(4):
-        for s in range(4):
-            dx = jnp.where(c == 0, r, s)
-            dy = jnp.where(c == 0, s, r)
-            group = lax.rem(y - dy + 4, 4)
-            total[group] += jnp.dot(
-                second_t[dx], hidden_piece(hidden, r, s), preferred_element_type=F32
-            )
-    for g in range(4):
-        out_ref[g * 512 : g * 512 + 512, :] = total[g].T.astype(BF16)
+        second_t[:, dx * 256 : dx * 256 + 256] = both.astype(F32).T.astype(BF16)
+
+    def products(piece):
+        for dy in range(4):
+            tokens = jnp.concatenate([piece(dx, dy) for dx in range(4)], axis=0)
+            out = jnp.dot(second_t[...], tokens, preferred_element_type=F32)
+            first = pl.multiple_of(lax.rem(y - dy + 4, 4) * 512, 512)
+            out_ref[pl.ds(first, 512), :] = out.T.astype(BF16)
+
+    @pl.when(c == 0)
+    def _():
+        products(lambda dx, dy: hidden_piece(hidden, dx, dy))
+
+    @pl.when(c == 1)
+    def _():
+        products(lambda dx, dy: hidden_piece(hidden, dy, dx))
 
 
 def gather_kernel(*refs):
     packs, (mine_ref, upstream_ref) = refs[1:5], refs[5:]
-    for dx, pack in enumerate(packs):
+    for dx, pack in zip((0, 2, 1, 3), packs):
         mine_ref[dx * 192 : dx * 192 + 192, :] = pack[0:192, :]
         upstream_ref[2 * dx] = pack[192:256, 0:128]
         upstream_ref[2 * dx + 1] = pack[192:256, 128:256]
@@ -351,14 +361,13 @@
 def prepare(where, arrays):
     any_spec = pl.BlockSpec(memory_space=pl.ANY)
     pack = jax.ShapeDtypeStruct((256, 256), BF16)
-    half = jax.ShapeDtypeStruct((128, 512), BF16)
     return pl.pallas_call(
         prepare_kernel,
-        out_shape=(pack,) * 4 + (half,) * 2,
-        in_specs=[SMEM_SPEC] + [any_spec] * 6,
-        out_specs=(VMEM_SPEC,) * 6,
+        out_shape=(pack,) * 4,
+        in_specs=[SMEM_SPEC] + [any_spec] * 5,
+        out_specs=(VMEM_SPEC,) * 4,
         scratch_shapes=[pltpu.VMEM(a.shape, BF16) for a in arrays]
-        + [pltpu.SemaphoreType.DMA((6,))],
+        + [pltpu.SemaphoreType.DMA((5,))],
         compiler_params=pltpu.CompilerParams(vmem_limit_bytes=2 * 1024 * 1024),
         cost_estimate=pl.CostEstimate(flops=1_000_000, bytes_accessed=600_000, transcendentals=0),
     )(where, *arrays)
@@ -377,10 +386,15 @@
     return call(keys_kernel, (), packs, jax.ShapeDtypeStruct((rows, 256), BF16), [], 2, flops)
 
 
+def select(where, arrays):
+    shape = jax.ShapeDtypeStruct((256, 512), BF16)
+    return call(select_kernel, (where,), arrays, shape, [], 2, 1_000_000)
+
+
 def project(where, arrays):
     shape = jax.ShapeDtypeStruct((4, 128, 256), F32)
-    scratch = [pltpu.VMEM((8, 4, 64, 256), BF16), pltpu.VMEM((4, 256, 256), F32)]
-    return call(project_kernel, (where,), arrays, (shape, shape), scratch, 6, 1_000_000_000)
+    scratch = [pltpu.VMEM((8, 4, 64, 256), BF16)]
+    return call(project_kernel, (where,), arrays, (shape, shape), scratch, 8, 1_000_000_000)
 
 
 def attend(scalars, arrays):
@@ -402,8 +416,8 @@
 
 def curvature(where, arrays):
     shape = jax.ShapeDtypeStruct((2048, 128), BF16)
-    scratch = [pltpu.VMEM((4, 128, 256), BF16), pltpu.VMEM((4, 128, 512), F32)]
-    return call(curvature_kernel, (where,), arrays, shape, scratch, 6, 600_000_000)
+    scratch = [pltpu.VMEM((128, 1024), BF16)]
+    return call(curvature_kernel, (where,), arrays, shape, scratch, 8, 600_000_000)
 
 
 def shift(value, axis, size, step):
@@ -435,15 +449,16 @@
     where = jnp.stack([z, x, c, y]).astype(I32)
     scalars = jnp.concatenate([where, block_order, lengths])
 
-    *packs, keep, send = prepare(
+    hidden_other = swap(hidden)
+    packs = prepare(
         where,
         tuple(
             pltpu.with_memory_space_constraint(a, pltpu.HBM)
-            for a in (hidden, query_weight, probe_vector, key_rows, value_rows, upstream)
+            for a in (query_weight, probe_vector, key_rows, value_rows, upstream)
         ),
     )
-    base = jnp.concatenate([keep, swap(send)], axis=0)
-    packs = [packs[0]] + [shift(packs[dx], "x", 4, dx) for dx in (1, 2, 3)]
+    base = select(where, (hidden, hidden_other))
+    packs = [packs[0]] + [shift(packs[dx], "x", 4, dx) for dx in (2, 1, 3)]
     base, *packs = lax.optimization_barrier((base, *packs))
     mine, upstream_rows = gather(scalars, packs)
     right_1, left_1 = shift(mine, "z", 8, 1), shift(mine, "z", 8, 7)

time: 97.5 us -> 95.6 us (0.981)
  waiting for transfers between devices: 26.3 us -> 25.3 us
    ppermute x17, waiting for transfers between devices: 26.3 us -> 25.2 us  [shift(): lax.ppermute(value, axis, [(i, (i + step) % size) for i in range(size)])]
    pallas_call x7 -> x8, Pallas kernels: 9.41 us -> 9.28 us  [call(): pl.pallas_call(kernel, out_shape=out_shape, in_specs=[SMEM_SPEC] * len(sc...]
  transfers between devices with their start and end apart: 23 -> 23, of which waited for: 9 -> 10; matrix products, arithmetic and copies ran while one was open for 0% -> 0% of each run, Pallas kernels for 3% -> 5%
where the time goes in v5:
time: 95.6 us; the launch traced here: 95.5 us
  starting transfers between devices  34.2 us (36%)
  waiting for transfers between devices  25.3 us (26%)
  blocking collectives  23.8 us (25%)
  Pallas kernels  11 us (12%)
    ppermute x17, waiting for transfers between devices, shift(): lax.ppermute(value, axis, [(i, (i + step) % size) for i in range(size)])  25.2 us
    ppermute x17, starting transfers between devices, shift(): lax.ppermute(value, axis, [(i, (i + step) % size) for i in range(size)])  24.5 us
    all_to_all x1, blocking collectives, per_device(): shares = lax.all_to_all(partial, ('z', 'x'), 0, 0, tiled=True)  23.8 us
    ppermute x6, starting transfers between devices, shift_plane(): return lax.ppermute(value, ('x', 'c', 'kvh'), pairs)  9.72 us
    pallas_call x8, Pallas kernels, call(): pl.pallas_call(kernel, out_shape=out_shape, in_specs=[SMEM_SPEC] * len(sc...  9.28 us
  transfers between devices with their start and end apart: 23, of which 10 were waited for; matrix products, arithmetic and copies ran while one was open for 0% of the time, Pallas kernels for 5%

profile of v5, /device:TPU:8, one launch (start us, length us, event | category | flops | bytes accessed | tf_op | source)
XLA Modules:
  0.0 95.5 jit_solution(16421979058732799979)
XLA Ops:
  0.0 0.0 copy-start
  0.0 0.0 collective-permute-start
  0.0 0.1 pad_add_fusion.where_ref.refs_0_
  0.1 1.7 %shard_map.83 = (bf16[256,256]{1,0:T(8,128)(2,1)S(1)}, bf16[256,256]{1,0:T(8,128)(2,1)S(1)}, bf16[256,256]{1,0:T(8,128)(2,1)S(1)}, bf16[256,256]{1,0:T(8,128)(2,1)S(1)}) custom-call(s32[4]{0:T(128)S(1)} %pad_add_fusion.where_ref.refs_0_, bf16[64,512]{1,0:T(8,128)(2,1)} %query_hbm.1, bf16[64,512]{1,0:T(8,128)(2,1)} %probe_hbm.1, bf16[128,128]{1,0:T(8,128)(2,1)} %key_hbm.1, ...), custom_call_target="tpu_custom_call" | custom-call | flops 1000000 | bytes 600000 | tf_op jit(solution)/shard_map/pallas_call | solution.py:364
  1.8 3.1 %collective-permute-start.1 = (bf16[256,256]{1,0:T(8,128)(2,1)S(1)}, bf16[256,256]{1,0:T(8,128)(2,1)S(1)}, u32[]{:S(2)}, u32[]{:S(2)}) collective-permute-start(bf16[256,256]{1,0:T(8,128)(2,1)S(1)} %get-tuple-element.28), channel_id=1, source_target_pairs={{0,16},{8,24},{16,0},{24,8},{1,17},{9,25},{17,1},{25,9},{2,18},{10... | collective-permute-start | bytes 393224 | tf_op jit(solution)/shard_map/ppermute | solution.py:424
  4.9 0.6 collective-permute-start.2
  5.5 2.6 %collective-permute-start.3 = (bf16[256,256]{1,0:T(8,128)(2,1)S(1)}, bf16[256,256]{1,0:T(8,128)(2,1)S(1)}, u32[]{:S(2)}, u32[]{:S(2)}) collective-permute-start(bf16[256,256]{1,0:T(8,128)(2,1)S(1)} %get-tuple-element.30), channel_id=1, source_target_pairs={{0,24},{8,0},{16,8},{24,16},{1,25},{9,1},{17,9},{25,17},{2,26},{10... | collective-permute-start | bytes 393224 | tf_op jit(solution)/shard_map/ppermute | solution.py:424
  8.1 0.0 copy-done.1
  8.1 0.0 copy-done.2
  8.1 0.1 concatenate.4.refs_0_
  8.2 0.0 collective-permute-done.other_ref
  8.2 0.0 copy-done
  8.2 0.8 shard_map.82
  9.0 0.7 collective-permute-done.1.refs_2_
  9.7 2.4 %collective-permute-done.2.refs_3_ = bf16[256,256]{1,0:T(8,128)(2,1)S(1)} collective-permute-done((bf16[256,256]{1,0:T(8,128)(2,1)S(1)}, bf16[256,256]{1,0:T(8,128)(2,1)S(1)}, u32[]{:S(2)}, u32[]{:S(2)}) %collective-permute-start.2) | collective-permute-done | bytes 131104 | tf_op jit(solution)/shard_map/ppermute | solution.py:424
  12.1 0.1 collective-permute-done.3.refs_4_
  12.2 0.6 shard_map.84
  12.8 5.9 %collective-permute-start.5 = (bf16[768,256]{1,0:T(8,128)(2,1)S(1)}, bf16[768,256]{1,0:T(8,128)(2,1)S(1)}, u32[]{:S(2)}, u32[]{:S(2)}) collective-permute-start(bf16[768,256]{1,0:T(8,128)(2,1)S(1)} %get-tuple-element.35.refs_5_.refs_0_.refs_3_), channel_id=1, source_target_pairs={{0,224},{32,0},{64,32},{96,64},{128,96},{160,128},{192,160},{224,1... | collective-permute-start | bytes 1179656 | tf_op jit(solution)/shard_map/ppermute | solution.py:424
  18.7 0.0 collective-permute-start.4
  18.7 2.3 %collective-permute-start.8 = (bf16[256,512]{1,0:T(8,128)(2,1)S(1)}, bf16[256,512]{1,0:T(8,128)(2,1)S(1)}, u32[]{:S(2)}, u32[]{:S(2)}) collective-permute-start(bf16[256,512]{1,0:T(8,128)(2,1)S(1)} %shard_map.82), channel_id=1, source_target_pairs={{0,2},{1,3},{2,0},{3,1},{4,20},{5,21},{6,22},{7,23},{8,10},{9,11},... | collective-permute-start | bytes 786440 | tf_op jit(solution)/shard_map/ppermute | solution.py:439
  21.0 0.0 collective-permute-start.7
  21.0 2.0 %collective-permute-start.6 = (bf16[256,512]{1,0:T(8,128)(2,1)S(1)}, bf16[256,512]{1,0:T(8,128)(2,1)S(1)}, u32[]{:S(2)}, u32[]{:S(2)}) collective-permute-start(bf16[256,512]{1,0:T(8,128)(2,1)S(1)} %shard_map.82), channel_id=1, source_target_pairs={{0,3},{1,0},{2,1},{3,2},{4,28},{5,29},{6,30},{7,31},{8,11},{9,8},{... | collective-permute-start | bytes 786440 | tf_op jit(solution)/shard_map/ppermute | solution.py:439
  23.0 3.9 %collective-permute-done.5.refs_7_.refs_2_.refs_5_ = bf16[768,256]{1,0:T(8,128)(2,1)S(1)} collective-permute-done((bf16[768,256]{1,0:T(8,128)(2,1)S(1)}, bf16[768,256]{1,0:T(8,128)(2,1)S(1)}, u32[]{:S(2)}, u32[]{:S(2)}) %collective-permute-start.5) | collective-permute-done | bytes 393248 | tf_op jit(solution)/shard_map/ppermute | solution.py:424
  27.0 3.7 %collective-permute-start.13 = (bf16[768,256]{1,0:T(8,128)(2,1)S(1)}, bf16[768,256]{1,0:T(8,128)(2,1)S(1)}, u32[]{:S(2)}, u32[]{:S(2)}) collective-permute-start(bf16[768,256]{1,0:T(8,128)(2,1)S(1)} %collective-permute-done.5.refs_7_.refs_2_.refs_5_), channel_id=1, source_target_pairs={{0,224},{32,0},{64,32},{96,64},{128,96},{160,128},{192,160},{224,1... | collective-permute-start | bytes 1179656 | tf_op jit(solution)/shard_map/ppermute | solution.py:424
  30.7 0.0 collective-permute-done.4.refs_6_.refs_1_.refs_4_
  30.7 0.0 collective-permute-start.12
  30.7 0.0 collective-permute-done.8
  30.7 0.0 collective-permute-done.7
  30.7 0.0 collective-permute-done.6
  30.7 0.1 pad_maximum_fusion.refs_1_
  30.8 2.2 %collective-permute-start.11 = (bf16[4,256,512]{2,1,0:T(8,128)(2,1)S(1)}, bf16[4,256,512]{2,1,0:T(8,128)(2,1)S(1)}, u32[]{:S(2)}, u32[]{:S(2)}) collective-permute-start(bf16[4,256,512]{2,1,0:T(8,128)(2,1)S(1)} %pad_maximum_fusion.refs_1_), channel_id=1, source_target_pairs={{0,16},{1,17},{2,18},{3,19},{4,6},{5,7},{6,4},{7,5},{8,24},{9,25},... | collective-permute-start | bytes 3145736 | tf_op jit(solution)/shard_map/ppermute | solution.py:439
  33.0 1.2 %collective-permute-start.10 = (bf16[4,256,512]{2,1,0:T(8,128)(2,1)S(1)}, bf16[4,256,512]{2,1,0:T(8,128)(2,1)S(1)}, u32[]{:S(2)}, u32[]{:S(2)}) collective-permute-start(bf16[4,256,512]{2,1,0:T(8,128)(2,1)S(1)} %pad_maximum_fusion.refs_1_), channel_id=1, source_target_pairs={{0,8},{1,9},{2,10},{3,11},{4,5},{5,6},{6,7},{7,4},{8,16},{9,17},{1... | collective-permute-start | bytes 3145736 | tf_op jit(solution)/shard_map/ppermute | solution.py:439
  34.2 2.0 %collective-permute-start.9 = (bf16[4,256,512]{2,1,0:T(8,128)(2,1)S(1)}, bf16[4,256,512]{2,1,0:T(8,128)(2,1)S(1)}, u32[]{:S(2)}, u32[]{:S(2)}) collective-permute-start(bf16[4,256,512]{2,1,0:T(8,128)(2,1)S(1)} %pad_maximum_fusion.refs_1_), channel_id=1, source_target_pairs={{0,24},{1,25},{2,26},{3,27},{4,7},{5,4},{6,5},{7,6},{8,0},{9,1},{1... | collective-permute-start | bytes 3145736 | tf_op jit(solution)/shard_map/ppermute | solution.py:439
  36.2 1.8 %collective-permute-done.13.refs_9_.refs_1_.refs_7_ = bf16[768,256]{1,0:T(8,128)(2,1)S(1)} collective-permute-done((bf16[768,256]{1,0:T(8,128)(2,1)S(1)}, bf16[768,256]{1,0:T(8,128)(2,1)S(1)}, u32[]{:S(2)}, u32[]{:S(2)}) %collective-permute-start.13) | collective-permute-done | bytes 393248 | tf_op jit(solution)/shard_map/ppermute | solution.py:424
  38.0 3.7 %collective-permute-start.15 = (bf16[768,256]{1,0:T(8,128)(2,1)S(1)}, bf16[768,256]{1,0:T(8,128)(2,1)S(1)}, u32[]{:S(2)}, u32[]{:S(2)}) collective-permute-start(bf16[768,256]{1,0:T(8,128)(2,1)S(1)} %collective-permute-done.13.refs_9_.refs_1_.refs_7_), channel_id=1, source_target_pairs={{0,224},{32,0},{64,32},{96,64},{128,96},{160,128},{192,160},{224,1... | collective-permute-start | bytes 1179656 | tf_op jit(solution)/shard_map/ppermute | solution.py:424
  41.7 0.0 collective-permute-done.12.refs_8_.refs_0_.refs_6_
  41.7 0.0 collective-permute-start.14
  41.7 6.4 %collective-permute-done.15.refs_11_.refs_3_.refs_9_ = bf16[768,256]{1,0:T(8,128)(2,1)S(1)} collective-permute-done((bf16[768,256]{1,0:T(8,128)(2,1)S(1)}, bf16[768,256]{1,0:T(8,128)(2,1)S(1)}, u32[]{:S(2)}, u32[]{:S(2)}) %collective-permute-start.15) | collective-permute-done | bytes 393248 | tf_op jit(solution)/shard_map/ppermute | solution.py:424
  48.2 3.9 %collective-permute-start.17 = (bf16[384,256]{1,0:T(8,128)(2,1)S(1)}, bf16[384,256]{1,0:T(8,128)(2,1)S(1)}, u32[]{:S(2)}, u32[]{:S(2)}) collective-permute-start(bf16[384,256]{1,0:T(8,128)(2,1)S(1)} %slice.9), channel_id=1, source_target_pairs={{0,224},{32,0},{64,32},{96,64},{128,96},{160,128},{192,160},{224,1... | collective-permute-start | bytes 589832 | tf_op jit(solution)/shard_map/ppermute | solution.py:424
  52.1 0.0 collective-permute-done.14.refs_10_.refs_2_.refs_8_
  52.2 0.1 collective-permute-start.16
  52.3 0.1 shard_map.88
  52.3 3.0 %collective-permute-done.17.refs_1_.refs_13_.refs_11_ = bf16[384,256]{1,0:T(8,128)(2,1)S(1)} collective-permute-done((bf16[384,256]{1,0:T(8,128)(2,1)S(1)}, bf16[384,256]{1,0:T(8,128)(2,1)S(1)}, u32[]{:S(2)}, u32[]{:S(2)}) %collective-permute-start.17) | collective-permute-done | bytes 196640 | tf_op jit(solution)/shard_map/ppermute | solution.py:424
  55.3 0.0 collective-permute-start.20
  55.3 0.1 shard_map.87
  55.4 3.7 %collective-permute-done.16.refs_0_.refs_12_.refs_10_ = bf16[384,256]{1,0:T(8,128)(2,1)S(1)} collective-permute-done((bf16[384,256]{1,0:T(8,128)(2,1)S(1)}, bf16[384,256]{1,0:T(8,128)(2,1)S(1)}, u32[]{:S(2)}, u32[]{:S(2)}) %collective-permute-start.16) | collective-permute-done | bytes 196640 | tf_op jit(solution)/shard_map/ppermute | solution.py:424
  59.1 0.0 collective-permute-start.19
  59.1 0.0 collective-permute-done.11.refs_4_
  59.2 0.0 collective-permute-done.10.refs_3_
  59.2 0.0 collective-permute-done.9.refs_2_
  59.2 1.9 %shard_map.86 = (f32[4,128,256]{2,1,0:T(8,128)S(1)}, f32[4,128,256]{2,1,0:T(8,128)S(1)}) custom-call(s32[4]{0:T(128)S(1)} %pad_add_fusion.where_ref.refs_0_, bf16[4,256,512]{2,1,0:T(8,128)(2,1)S(1)} %pad_maximum_fusion.refs_1_, bf16[4,256,512]{2,1,0:T(8,128)(2,1)S(1)} %collective-permute-done.9.refs_2_, ...), custom_call_target="tpu_custom_call" | custom-call | flops 1000000000 | bytes 8000000 | tf_op jit(solution)/shard_map/pallas_call | solution.py:350
  61.1 0.6 collective-permute-start.18
  61.7 0.1 collective-permute-start.21
  61.8 0.0 collective-permute-done.19.refs_12_
  61.8 1.8 %collective-permute-done.21.refs_14_ = bf16[512,256]{1,0:T(8,128)(2,1)S(1)} collective-permute-done((bf16[512,256]{1,0:T(8,128)(2,1)S(1)}, bf16[512,256]{1,0:T(8,128)(2,1)S(1)}, u32[]{:S(2)}, u32[]{:S(2)}) %collective-permute-start.21) | collective-permute-done | bytes 262176 | tf_op jit(solution)/shard_map/ppermute | solution.py:424
  63.6 0.0 collective-permute-done.18.refs_2_
  63.6 0.0 collective-permute-done.20.refs_13_
  63.6 4.4 %shard_map.89.refs_5_ = bf16[512,128]{1,0:T(8,128)(2,1)S(1)} custom-call(s32[148]{0:T(256)S(1)} %concatenate.4.refs_0_, f32[4,128,256]{2,1,0:T(8,128)S(1)} %get-tuple-element.43.refs_1_, f32[4,128,256]{2,1,0:T(8,128)S(1)} %collective-permute-done.18.refs_2_, bf16[768,256]{1,0:T(8,128)(2,1)S(1)} %get-tuple-element.35.refs_5_.refs_0_.refs_3_, ...), custom_call_target="tpu_custom_call" | custom-call | flops 2000000000 | bytes 8000000 | tf_op jit(solution)/shard_map/pallas_call | solution.py:350
  68.0 0.1 collective-permute-start.22
  68.1 1.3 %collective-permute-done.22.refs_6_ = bf16[512,128]{1,0:T(8,128)(2,1)S(1)} collective-permute-done((bf16[512,128]{1,0:T(8,128)(2,1)S(1)}, bf16[512,128]{1,0:T(8,128)(2,1)S(1)}, u32[]{:S(2)}, u32[]{:S(2)}) %collective-permute-start.22) | collective-permute-done | bytes 131104 | tf_op jit(solution)/shard_map/ppermute | solution.py:424
  69.4 1.5 %shard_map.90 = bf16[2048,128]{1,0:T(8,128)(2,1)S(1)} custom-call(s32[4]{0:T(128)S(1)} %pad_add_fusion.where_ref.refs_0_, bf16[4,256,512]{2,1,0:T(8,128)(2,1)S(1)} %pad_maximum_fusion.refs_1_, bf16[4,256,512]{2,1,0:T(8,128)(2,1)S(1)} %collective-permute-done.9.refs_2_, bf16[4,256,512]{2,1,0:T(8,128)(2,1)S(1)} %collective-permute-done.10.refs_3_, ...), custom_call_target="tpu_custom_call" | custom-call | flops 600000000 | bytes 8000000 | tf_op jit(solution)/shard_map/pallas_call | solution.py:350
  70.9 23.8 %all_to_all.9 = bf16[32,64,128]{2,1,0:T(8,128)(2,1)S(1)} all-to-all(bf16[32,64,128]{2,1,0:T(8,128)(2,1)S(1)} %bitcast.17), channel_id=1, replica_groups=mesh['z'=8,'x'=4,'c'=2,'kvh'=4] {'z','x'}, dimensions={0} | all-to-all | bytes 1048576 | tf_op jit(solution)/shard_map/all_to_all | solution.py:501
  94.7 0.1 convert_reduce_fusion
  94.8 0.7 copy_bitcast_fusion
  (5 shorter events, 0.0 us)
Async XLA Ops:
  0.0 8.2 %copy-start = (bf16[128,1024]{1,0:T(8,128)(2,1)S(1)}, bf16[128,1024]{1,0:T(8,128)(2,1)}, u32[]{:S(2)}) copy-start(bf16[128,1024]{1,0:T(8,128)(2,1)} %own_ref.1) | copy-start | bytes 786436
  0.0 8.2 %collective-permute-start = (bf16[128,1024]{1,0:T(8,128)(2,1)}, bf16[128,1024]{1,0:T(8,128)(2,1)S(1)}, u32[]{:S(2)}, u32[]{:S(2)}) collective-permute-start(bf16[128,1024]{1,0:T(8,128)(2,1)} %own_ref.1), channel_id=1, source_target_pairs={{0,4},{4,0},{1,5},{5,1},{2,6},{6,2},{3,7},{7,3},{8,12},{12,8},{9,1... | collective-permute-start | bytes 786440 | tf_op jit(solution)/shard_map/ppermute | solution.py:424
  1.8 7.9 %collective-permute-start.1 = (bf16[256,256]{1,0:T(8,128)(2,1)S(1)}, bf16[256,256]{1,0:T(8,128)(2,1)S(1)}, u32[]{:S(2)}, u32[]{:S(2)}) collective-permute-start(bf16[256,256]{1,0:T(8,128)(2,1)S(1)} %get-tuple-element.28), channel_id=1, source_target_pairs={{0,16},{8,24},{16,0},{24,8},{1,17},{9,25},{17,1},{25,9},{2,18},{10... | collective-permute-start | bytes 393224 | tf_op jit(solution)/shard_map/ppermute | solution.py:424
  4.9 3.2 %copy-start.1 = (s32[128]{0:T(128)S(1)}, s32[128]{0:T(128)}, u32[]{:S(2)}) copy-start(s32[128]{0:T(128)} %param.15) | copy-start | bytes 1540
  4.9 3.2 %copy-start.2 = (s32[16]{0:T(128)S(1)}, s32[16]{0:T(128)}, u32[]{:S(2)}) copy-start(s32[16]{0:T(128)} %param.14) | copy-start | bytes 196
  4.9 7.2 %collective-permute-start.2 = (bf16[256,256]{1,0:T(8,128)(2,1)S(1)}, bf16[256,256]{1,0:T(8,128)(2,1)S(1)}, u32[]{:S(2)}, u32[]{:S(2)}) collective-permute-start(bf16[256,256]{1,0:T(8,128)(2,1)S(1)} %get-tuple-element.29), channel_id=1, source_target_pairs={{0,8},{8,16},{16,24},{24,0},{1,9},{9,17},{17,25},{25,1},{2,10},{10... | collective-permute-start | bytes 393224 | tf_op jit(solution)/shard_map/ppermute | solution.py:424
  5.5 6.7 %collective-permute-start.3 = (bf16[256,256]{1,0:T(8,128)(2,1)S(1)}, bf16[256,256]{1,0:T(8,128)(2,1)S(1)}, u32[]{:S(2)}, u32[]{:S(2)}) collective-permute-start(bf16[256,256]{1,0:T(8,128)(2,1)S(1)} %get-tuple-element.30), channel_id=1, source_target_pairs={{0,24},{8,0},{16,8},{24,16},{1,25},{9,1},{17,9},{25,17},{2,26},{10... | collective-permute-start | bytes 393224 | tf_op jit(solution)/shard_map/ppermute | solution.py:424
  12.8 14.2 %collective-permute-start.5 = (bf16[768,256]{1,0:T(8,128)(2,1)S(1)}, bf16[768,256]{1,0:T(8,128)(2,1)S(1)}, u32[]{:S(2)}, u32[]{:S(2)}) collective-permute-start(bf16[768,256]{1,0:T(8,128)(2,1)S(1)} %get-tuple-element.35.refs_5_.refs_0_.refs_3_), channel_id=1, source_target_pairs={{0,224},{32,0},{64,32},{96,64},{128,96},{160,128},{192,160},{224,1... | collective-permute-start | bytes 1179656 | tf_op jit(solution)/shard_map/ppermute | solution.py:424
  18.7 12.0 %collective-permute-start.4 = (bf16[768,256]{1,0:T(8,128)(2,1)S(1)}, bf16[768,256]{1,0:T(8,128)(2,1)S(1)}, u32[]{:S(2)}, u32[]{:S(2)}) collective-permute-start(bf16[768,256]{1,0:T(8,128)(2,1)S(1)} %get-tuple-element.35.refs_5_.refs_0_.refs_3_), channel_id=1, source_target_pairs={{0,32},{32,64},{64,96},{96,128},{128,160},{160,192},{192,224},{224... | collective-permute-start | bytes 1179656 | tf_op jit(solution)/shard_map/ppermute | solution.py:424
  18.7 12.0 %collective-permute-start.8 = (bf16[256,512]{1,0:T(8,128)(2,1)S(1)}, bf16[256,512]{1,0:T(8,128)(2,1)S(1)}, u32[]{:S(2)}, u32[]{:S(2)}) collective-permute-start(bf16[256,512]{1,0:T(8,128)(2,1)S(1)} %shard_map.82), channel_id=1, source_target_pairs={{0,2},{1,3},{2,0},{3,1},{4,20},{5,21},{6,22},{7,23},{8,10},{9,11},... | collective-permute-start | bytes 786440 | tf_op jit(solution)/shard_map/ppermute | solution.py:439
  21.0 9.7 %collective-permute-start.7 = (bf16[256,512]{1,0:T(8,128)(2,1)S(1)}, bf16[256,512]{1,0:T(8,128)(2,1)S(1)}, u32[]{:S(2)}, u32[]{:S(2)}) collective-permute-start(bf16[256,512]{1,0:T(8,128)(2,1)S(1)} %shard_map.82), channel_id=1, source_target_pairs={{0,1},{1,2},{2,3},{3,0},{4,12},{5,13},{6,14},{7,15},{8,9},{9,10},{... | collective-permute-start | bytes 786440 | tf_op jit(solution)/shard_map/ppermute | solution.py:439
  21.0 9.7 %collective-permute-start.6 = (bf16[256,512]{1,0:T(8,128)(2,1)S(1)}, bf16[256,512]{1,0:T(8,128)(2,1)S(1)}, u32[]{:S(2)}, u32[]{:S(2)}) collective-permute-start(bf16[256,512]{1,0:T(8,128)(2,1)S(1)} %shard_map.82), channel_id=1, source_target_pairs={{0,3},{1,0},{2,1},{3,2},{4,28},{5,29},{6,30},{7,31},{8,11},{9,8},{... | collective-permute-start | bytes 786440 | tf_op jit(solution)/shard_map/ppermute | solution.py:439
  27.0 11.1 %collective-permute-start.13 = (bf16[768,256]{1,0:T(8,128)(2,1)S(1)}, bf16[768,256]{1,0:T(8,128)(2,1)S(1)}, u32[]{:S(2)}, u32[]{:S(2)}) collective-permute-start(bf16[768,256]{1,0:T(8,128)(2,1)S(1)} %collective-permute-done.5.refs_7_.refs_2_.refs_5_), channel_id=1, source_target_pairs={{0,224},{32,0},{64,32},{96,64},{128,96},{160,128},{192,160},{224,1... | collective-permute-start | bytes 1179656 | tf_op jit(solution)/shard_map/ppermute | solution.py:424
  30.7 11.1 %collective-permute-start.12 = (bf16[768,256]{1,0:T(8,128)(2,1)S(1)}, bf16[768,256]{1,0:T(8,128)(2,1)S(1)}, u32[]{:S(2)}, u32[]{:S(2)}) collective-permute-start(bf16[768,256]{1,0:T(8,128)(2,1)S(1)} %collective-permute-done.4.refs_6_.refs_1_.refs_4_), channel_id=1, source_target_pairs={{0,32},{32,64},{64,96},{96,128},{128,160},{160,192},{192,224},{224... | collective-permute-start | bytes 1179656 | tf_op jit(solution)/shard_map/ppermute | solution.py:424
  30.8 28.3 %collective-permute-start.11 = (bf16[4,256,512]{2,1,0:T(8,128)(2,1)S(1)}, bf16[4,256,512]{2,1,0:T(8,128)(2,1)S(1)}, u32[]{:S(2)}, u32[]{:S(2)}) collective-permute-start(bf16[4,256,512]{2,1,0:T(8,128)(2,1)S(1)} %pad_maximum_fusion.refs_1_), channel_id=1, source_target_pairs={{0,16},{1,17},{2,18},{3,19},{4,6},{5,7},{6,4},{7,5},{8,24},{9,25},... | collective-permute-start | bytes 3145736 | tf_op jit(solution)/shard_map/ppermute | solution.py:439
  33.0 26.2 %collective-permute-start.10 = (bf16[4,256,512]{2,1,0:T(8,128)(2,1)S(1)}, bf16[4,256,512]{2,1,0:T(8,128)(2,1)S(1)}, u32[]{:S(2)}, u32[]{:S(2)}) collective-permute-start(bf16[4,256,512]{2,1,0:T(8,128)(2,1)S(1)} %pad_maximum_fusion.refs_1_), channel_id=1, source_target_pairs={{0,8},{1,9},{2,10},{3,11},{4,5},{5,6},{6,7},{7,4},{8,16},{9,17},{1... | collective-permute-start | bytes 3145736 | tf_op jit(solution)/shard_map/ppermute | solution.py:439
  34.2 25.0 %collective-permute-start.9 = (bf16[4,256,512]{2,1,0:T(8,128)(2,1)S(1)}, bf16[4,256,512]{2,1,0:T(8,128)(2,1)S(1)}, u32[]{:S(2)}, u32[]{:S(2)}) collective-permute-start(bf16[4,256,512]{2,1,0:T(8,128)(2,1)S(1)} %pad_maximum_fusion.refs_1_), channel_id=1, source_target_pairs={{0,24},{1,25},{2,26},{3,27},{4,7},{5,4},{6,5},{7,6},{8,0},{9,1},{1... | collective-permute-start | bytes 3145736 | tf_op jit(solution)/shard_map/ppermute | solution.py:439
  38.0 10.1 %collective-permute-start.15 = (bf16[768,256]{1,0:T(8,128)(2,1)S(1)}, bf16[768,256]{1,0:T(8,128)(2,1)S(1)}, u32[]{:S(2)}, u32[]{:S(2)}) collective-permute-start(bf16[768,256]{1,0:T(8,128)(2,1)S(1)} %collective-permute-done.13.refs_9_.refs_1_.refs_7_), channel_id=1, source_target_pairs={{0,224},{32,0},{64,32},{96,64},{128,96},{160,128},{192,160},{224,1... | collective-permute-start | bytes 1179656 | tf_op jit(solution)/shard_map/ppermute | solution.py:424
  41.7 10.4 %collective-permute-start.14 = (bf16[768,256]{1,0:T(8,128)(2,1)S(1)}, bf16[768,256]{1,0:T(8,128)(2,1)S(1)}, u32[]{:S(2)}, u32[]{:S(2)}) collective-permute-start(bf16[768,256]{1,0:T(8,128)(2,1)S(1)} %collective-permute-done.12.refs_8_.refs_0_.refs_6_), channel_id=1, source_target_pairs={{0,32},{32,64},{64,96},{96,128},{128,160},{160,192},{192,224},{224... | collective-permute-start | bytes 1179656 | tf_op jit(solution)/shard_map/ppermute | solution.py:424
  48.2 7.1 %collective-permute-start.17 = (bf16[384,256]{1,0:T(8,128)(2,1)S(1)}, bf16[384,256]{1,0:T(8,128)(2,1)S(1)}, u32[]{:S(2)}, u32[]{:S(2)}) collective-permute-start(bf16[384,256]{1,0:T(8,128)(2,1)S(1)} %slice.9), channel_id=1, source_target_pairs={{0,224},{32,0},{64,32},{96,64},{128,96},{160,128},{192,160},{224,1... | collective-permute-start | bytes 589832 | tf_op jit(solution)/shard_map/ppermute | solution.py:424
  52.2 7.0 %collective-permute-start.16 = (bf16[384,256]{1,0:T(8,128)(2,1)S(1)}, bf16[384,256]{1,0:T(8,128)(2,1)S(1)}, u32[]{:S(2)}, u32[]{:S(2)}) collective-permute-start(bf16[384,256]{1,0:T(8,128)(2,1)S(1)} %slice.8), channel_id=1, source_target_pairs={{0,32},{32,64},{64,96},{96,128},{128,160},{160,192},{192,224},{224... | collective-permute-start | bytes 589832 | tf_op jit(solution)/shard_map/ppermute | solution.py:424
  55.3 8.3 %collective-permute-start.20 = (bf16[2048,256]{1,0:T(8,128)(2,1)S(1)}, bf16[2048,256]{1,0:T(8,128)(2,1)S(1)}, u32[]{:S(2)}, u32[]{:S(2)}) collective-permute-start(bf16[2048,256]{1,0:T(8,128)(2,1)S(1)} %shard_map.88), channel_id=1, source_target_pairs={{0,4},{4,0},{1,5},{5,1},{2,6},{6,2},{3,7},{7,3},{8,12},{12,8},{9,1... | collective-permute-start | bytes 3145736 | tf_op jit(solution)/shard_map/ppermute | solution.py:424
  59.1 2.7 %collective-permute-start.19 = (bf16[1536,256]{1,0:T(8,128)(2,1)S(1)}, bf16[1536,256]{1,0:T(8,128)(2,1)S(1)}, u32[]{:S(2)}, u32[]{:S(2)}) collective-permute-start(bf16[1536,256]{1,0:T(8,128)(2,1)S(1)} %shard_map.87), channel_id=1, source_target_pairs={{0,4},{4,0},{1,5},{5,1},{2,6},{6,2},{3,7},{7,3},{8,12},{12,8},{9,1... | collective-permute-start | bytes 2359304 | tf_op jit(solution)/shard_map/ppermute | solution.py:424
  61.1 2.5 %collective-permute-start.18 = (f32[4,128,256]{2,1,0:T(8,128)S(1)}, f32[4,128,256]{2,1,0:T(8,128)S(1)}, u32[]{:S(2)}, u32[]{:S(2)}) collective-permute-start(f32[4,128,256]{2,1,0:T(8,128)S(1)} %get-tuple-element.44), channel_id=1, source_target_pairs={{0,4},{4,0},{1,5},{5,1},{2,6},{6,2},{3,7},{7,3},{8,12},{12,8},{9,1... | collective-permute-start | bytes 1572872 | tf_op jit(solution)/shard_map/ppermute | solution.py:424
  61.7 1.9 %collective-permute-start.21 = (bf16[512,256]{1,0:T(8,128)(2,1)S(1)}, bf16[512,256]{1,0:T(8,128)(2,1)S(1)}, u32[]{:S(2)}, u32[]{:S(2)}) collective-permute-start(bf16[512,256]{1,0:T(8,128)(2,1)S(1)} %shard_map.85), channel_id=1, source_target_pairs={{0,4},{4,0},{1,5},{5,1},{2,6},{6,2},{3,7},{7,3},{8,12},{12,8},{9,1... | collective-permute-start | bytes 786440 | tf_op jit(solution)/shard_map/ppermute | solution.py:424
  68.0 1.4 %collective-permute-start.22 = (bf16[512,128]{1,0:T(8,128)(2,1)S(1)}, bf16[512,128]{1,0:T(8,128)(2,1)S(1)}, u32[]{:S(2)}, u32[]{:S(2)}) collective-permute-start(bf16[512,128]{1,0:T(8,128)(2,1)S(1)} %shard_map.89.refs_5_), channel_id=1, source_target_pairs={{0,4},{4,0},{1,5},{5,1},{2,6},{6,2},{3,7},{7,3},{8,12},{12,8},{9,1... | collective-permute-start | bytes 393224 | tf_op jit(solution)/shard_map/ppermute | solution.py:424

commit v6 on v5

--- a/solution.py
+++ b/solution.py
@@ -103,8 +103,8 @@
 
     for pack, dz in zip(packs, (0, 1, 7, 2, 6, 3, 5)):
         place(pack, dz)
-    place(far_r, 4, (0, 1))
-    place(far_l, 4, (2, 3))
+    place(far_r, 4, (0, 1, 2))
+    place(far_l, 4, (3,))
 
     def products(piece):
         rows = []
@@ -127,23 +127,52 @@
         products(lambda dx, dy: hidden_piece(hidden, dy, dx))
 
 
+def plan_kernel(where_ref, starts, extra_block, extra_row, ends):
+    z, x, c = where_ref[0], where_ref[1], where_ref[2]
+    total = jnp.int32(0)
+    for d in range(NDOC):
+        total = total + where_ref[LENGTHS + d]
+        ends[d] = total
+    extras = jnp.int32(0)
+    sub = lax.broadcasted_iota(I32, (BLK, LANES), 0)
+    for rb in range(ROW_BLOCKS):
+        xx = lax.rem(x - rb // 2 + 4, 4)
+        p = where_ref[ORDER + ((z * 4 + xx) * 2 + c) * 2 + rb % 2]
+        first = jnp.int32(0)
+        start = jnp.zeros((BLK, LANES), I32)
+        for d in range(NDOC):
+            end = ends[d]
+            first = jnp.where(end <= p * BLK, end, first)
+            start = jnp.where(end <= p * BLK + sub, end, start)
+        starts[rb] = start
+        more = (p * BLK + BLK - first + CHUNK - 1) // CHUNK - 1
+
+        def note(j, at, rb=rb, p=p):
+            extra_block[at] = rb
+            extra_row[at] = p * BLK + BLK - CHUNK * (j + 1)
+            return at + 1
+
+        extras = lax.fori_loop(0, more, note, extras)
+    for n in range(TOGETHER - 1):
+        extra_block[extras + n] = ROW_BLOCKS
+        extra_row[extras + n] = 0
+    extra_block[MOST_EXTRA + TOGETHER] = extras
+    starts[ROW_BLOCKS] = jnp.zeros((BLK, LANES), I32)
+
+
 def attend_kernel(*refs):
-    where_ref, qt_keep, qt_received = refs[:3]
-    packs, far_r, far_l = refs[3:10], refs[10], refs[11]
-    swap_a, swap_b, swap_c = refs[12:15]
-    upstream_ref, second_ref = refs[15:17]
+    where_ref, extra_block, extra_row, qt_keep, qt_received = refs[:5]
+    packs, far_r, far_l = refs[5:12], refs[12], refs[13]
+    swap_a, swap_b, swap_c = refs[14:17]
+    upstream_ref, starts, second_ref = refs[17:20]
     (
         keys_values,
         query_tangent,
-        starts,
         scores,
         sums,
         stats,
         second,
-        ends,
-        extra_block,
-        extra_row,
-    ) = refs[17:]
+    ) = refs[20:]
     z, x, c = where_ref[0], where_ref[1], where_ref[2]
 
     keys_values[0:CHUNK, :] = jnp.zeros((CHUNK, 256), BF16)
@@ -159,8 +188,8 @@
 
     for pack, dz in zip(packs, (0, 1, 7, 2, 6, 3, 5)):
         place(pack, 64, 192, dz, c)
-    place(far_r, 64, 192, 4, c, (0, 1))
-    place(far_l, 64, 192, 4, c, (2, 3))
+    place(far_r, 64, 192, 4, c, (0, 1, 2))
+    place(far_l, 64, 192, 4, c, (3,))
     for i, dz in enumerate((0, 1, 7)):
         place(swap_a, i * 512, 128, dz, 1 - c)
     for i, dz in enumerate((2, 6, 3, 5)):
@@ -173,40 +202,16 @@
         query_tangent[rb, 0:64, :] = both[:, 0:128]
         query_tangent[rb, 64:128, :] = both[:, 128:256]
 
-    total = jnp.int32(0)
-    for d in range(NDOC):
-        total = total + where_ref[LENGTHS + d]
-        ends[d] = total
     packed_block = []
-    extras = jnp.int32(0)
+    for rb in range(ROW_BLOCKS):
+        xx = lax.rem(x - rb // 2 + 4, 4)
+        packed_block.append(where_ref[ORDER + ((z * 4 + xx) * 2 + c) * 2 + rb % 2])
+    extras = extra_block[MOST_EXTRA + TOGETHER]
     sub = lax.broadcasted_iota(I32, (BLK, LANES), 0)
     lane = lax.broadcasted_iota(I32, (BLK, LANES), 1)
-    for rb in range(ROW_BLOCKS):
-        xx = lax.rem(x - rb // 2 + 4, 4)
-        p = where_ref[ORDER + ((z * 4 + xx) * 2 + c) * 2 + rb % 2]
-        packed_block.append(p)
-        first = jnp.int32(0)
-        start = jnp.zeros((BLK, LANES), I32)
-        for d in range(NDOC):
-            end = ends[d]
-            first = jnp.where(end <= p * BLK, end, first)
-            start = jnp.where(end <= p * BLK + sub, end, start)
-        starts[rb] = start
-        more = (p * BLK + BLK - first + CHUNK - 1) // CHUNK - 1
-
-        def note(j, at, rb=rb, p=p):
-            extra_block[at] = rb
-            extra_row[at] = p * BLK + BLK - CHUNK * (j + 1)
-            return at + 1
-
-        extras = lax.fori_loop(0, more, note, extras)
-    for n in range(TOGETHER - 1):
-        extra_block[extras + n] = ROW_BLOCKS
-        extra_row[extras + n] = 0
     sums[ROW_BLOCKS] = jnp.zeros((4, BLK, LANES), F32)
     stats[ROW_BLOCKS] = jnp.zeros((4, BLK, LANES), F32)
     second[ROW_BLOCKS] = jnp.zeros((BLK, LANES), F32)
-    starts[ROW_BLOCKS] = jnp.zeros((BLK, LANES), I32)
 
     def dot_t(a, b):
         return lax.dot_general(a, b, (((1,), (1,)), ((), ())), preferred_element_type=F32)
@@ -326,7 +331,7 @@
 
 
 def gather_kernel(*refs):
-    packs, (mine_ref, upstream_ref) = refs[1:5], refs[5:]
+    packs, (mine_ref, upstream_ref) = refs[2:6], refs[6:]
     for dx, pack in zip((0, 2, 1, 3), packs):
         mine_ref[dx * 192 : dx * 192 + 192, :] = pack[0:192, :]
         upstream_ref[2 * dx] = pack[192:256, 0:128]
@@ -373,12 +378,12 @@
     )(where, *arrays)
 
 
-def gather(scalars, packs):
+def gather(scalars, starts, packs):
     shapes = (
         jax.ShapeDtypeStruct((768, 256), BF16),
         jax.ShapeDtypeStruct((ROW_BLOCKS, BLK, HD), BF16),
     )
-    return call(gather_kernel, (scalars,), packs, shapes, [], 2, 100_000)
+    return call(gather_kernel, (scalars,), (starts, *packs), shapes, [], 2, 100_000)
 
 
 def keys_of(packs, flops=100_000):
@@ -397,18 +402,27 @@
     return call(project_kernel, (where,), arrays, (shape, shape), scratch, 8, 1_000_000_000)
 
 
+def plan(scalars):
+    items = jax.ShapeDtypeStruct((MOST_EXTRA + TOGETHER + 1,), I32)
+    return pl.pallas_call(
+        plan_kernel,
+        out_shape=(jax.ShapeDtypeStruct((ROW_BLOCKS + 1, BLK, LANES), I32), items, items),
+        in_specs=[SMEM_SPEC],
+        out_specs=(VMEM_SPEC, SMEM_SPEC, SMEM_SPEC),
+        scratch_shapes=[pltpu.SMEM((NDOC,), I32)],
+        compiler_params=pltpu.CompilerParams(vmem_limit_bytes=2 * 1024 * 1024),
+        cost_estimate=pl.CostEstimate(flops=100_000, bytes_accessed=300_000, transcendentals=0),
+    )(scalars)
+
+
 def attend(scalars, arrays):
     scratch = [
         pltpu.VMEM((CHUNK + TOKENS, 256), BF16),
         pltpu.VMEM((ROW_BLOCKS, 128, 128), BF16),
-        pltpu.VMEM((ROW_BLOCKS + 1, BLK, LANES), I32),
         pltpu.VMEM((ROW_BLOCKS + MOST_EXTRA, 3, BLK, CHUNK), F32),
         pltpu.VMEM((ROW_BLOCKS + 1, 4, BLK, LANES), F32),
         pltpu.VMEM((ROW_BLOCKS + 1, 4, BLK, LANES), F32),
         pltpu.VMEM((ROW_BLOCKS + 1, BLK, LANES), F32),
-        pltpu.SMEM((NDOC,), I32),
-        pltpu.SMEM((MOST_EXTRA + TOGETHER,), I32),
-        pltpu.SMEM((MOST_EXTRA + TOGETHER,), I32),
     ]
     shape = jax.ShapeDtypeStruct((512, 128), BF16)
     return call(attend_kernel, scalars, arrays, shape, scratch, 27, 2_000_000_000)
@@ -460,7 +474,8 @@
     base = select(where, (hidden, hidden_other))
     packs = [packs[0]] + [shift(packs[dx], "x", 4, dx) for dx in (2, 1, 3)]
     base, *packs = lax.optimization_barrier((base, *packs))
-    mine, upstream_rows = gather(scalars, packs)
+    starts, extra_block, extra_row = plan(scalars)
+    mine, upstream_rows = gather(scalars, starts, packs)
     right_1, left_1 = shift(mine, "z", 8, 1), shift(mine, "z", 8, 7)
 
     stack = [base] + [shift_plane(base, s, True) for s in (3, 1, 2)]
@@ -472,18 +487,18 @@
     right_3, left_3 = shift(right_2, "z", 8, 1), shift(left_2, "z", 8, 7)
     swap_a = swap(keys_of((mine, right_b, left_b), 100000))
 
-    far_r, far_l = shift(right_3[:384], "z", 8, 1), shift(left_3[384:], "z", 8, 7)
+    far_r, far_l = shift(right_3[:576], "z", 8, 1), shift(left_3[576:], "z", 8, 7)
     swap_b = swap(keys_of((right_2, left_2, right_3, left_3)))
     pieces = (stack, hid_left, hid_right, hid_far)
 
     ring = (mine, right_1, left_1, right_2, left_2, right_3, left_3)
-    keys_c = keys_of((far_r, far_l), 4000000000)
+    keys_c = keys_of((far_r, far_l), 3000000000)
     far_r, far_l, keys_c = lax.optimization_barrier((far_r, far_l, keys_c))
     swap_c = swap(keys_c)
     qt_keep, qt_send = project(where, (*pieces, *ring, far_r, far_l))
     qt_received = swap(qt_send)
     second_own = attend(
-        (scalars,),
+        (scalars, extra_block, extra_row),
         (
             qt_keep,
             qt_received,
@@ -494,6 +509,7 @@
             swap_b,
             swap_c,
             upstream_rows,
+            starts,
         ),
     )
     second_other = swap(second_own)

time: 95.6 us -> 96.4 us (level)
  blocking collectives: 23.8 us -> 25.8 us
  starting transfers between devices: 34.2 us -> 32.8 us
  Pallas kernels: 11 us -> 12 us
    all_to_all x1, blocking collectives: 23.8 us -> 25.8 us  [per_device(): shares = lax.all_to_all(partial, ('z', 'x'), 0, 0, tiled=True)]
    ppermute x17, waiting for transfers between devices: 25.2 us -> 23.4 us  [shift(): lax.ppermute(value, axis, [(i, (i + step) % size) for i in range(size)])]
    pallas_call x0 -> x1, Pallas kernels: none -> 1.58 us  [plan(): pl.pallas_call(plan_kernel, out_shape=(jax.ShapeDtypeStruct((ROW_BLOCKS +...]
    ppermute x17, starting transfers between devices: 24.5 us -> 23 us  [shift(): lax.ppermute(value, axis, [(i, (i + step) % size) for i in range(size)])]
    ppermute x6, waiting for transfers between devices: 0.02 us -> 1.11 us  [shift_plane(): return lax.ppermute(value, ('x', 'c', 'kvh'), pairs)]
  transfers between devices with their start and end apart: 23 -> 23, of which waited for: 10 -> 10; matrix products, arithmetic and copies ran while one was open for 0% -> 0% of each run, Pallas kernels for 5% -> 6%
where the time goes in v6:
time: 96.4 us; the launch traced here: 96.3 us
  starting transfers between devices  32.8 us (34%)
  blocking collectives  25.8 us (27%)
  waiting for transfers between devices  24.5 us (25%)
  Pallas kernels  12 us (12%)
    all_to_all x1, blocking collectives, per_device(): shares = lax.all_to_all(partial, ('z', 'x'), 0, 0, tiled=True)  25.8 us
    ppermute x17, waiting for transfers between devices, shift(): lax.ppermute(value, axis, [(i, (i + step) % size) for i in range(size)])  23.4 us
    ppermute x17, starting transfers between devices, shift(): lax.ppermute(value, axis, [(i, (i + step) % size) for i in range(size)])  23 us
    ppermute x6, starting transfers between devices, shift_plane(): return lax.ppermute(value, ('x', 'c', 'kvh'), pairs)  9.72 us
    pallas_call x8, Pallas kernels, call(): pl.pallas_call(kernel, out_shape=out_shape, in_specs=[SMEM_SPEC] * len(sc...  8.75 us
  transfers between devices with their start and end apart: 23, of which 10 were waited for; matrix products, arithmetic and copies ran while one was open for 0% of the time, Pallas kernels for 6%

profile of v6, /device:TPU:8, one launch (start us, length us, event | category | flops | bytes accessed | tf_op | source)
XLA Modules:
  0.0 96.3 jit_solution(3024468676101602593)
XLA Ops:
  0.0 0.0 collective-permute-start
  0.0 0.1 pad_add_fusion.where_ref.refs_0_
  0.1 1.7 %shard_map.84 = (bf16[256,256]{1,0:T(8,128)(2,1)S(1)}, bf16[256,256]{1,0:T(8,128)(2,1)S(1)}, bf16[256,256]{1,0:T(8,128)(2,1)S(1)}, bf16[256,256]{1,0:T(8,128)(2,1)S(1)}) custom-call(s32[4]{0:T(128)S(1)} %pad_add_fusion.where_ref.refs_0_, bf16[64,512]{1,0:T(8,128)(2,1)} %query_hbm.1, bf16[64,512]{1,0:T(8,128)(2,1)} %probe_hbm.1, bf16[128,128]{1,0:T(8,128)(2,1)} %key_hbm.1, ...), custom_call_target="tpu_custom_call" | custom-call | flops 1000000 | bytes 600000 | tf_op jit(solution)/shard_map/pallas_call | solution.py:369
  1.8 3.1 %collective-permute-start.1 = (bf16[256,256]{1,0:T(8,128)(2,1)S(1)}, bf16[256,256]{1,0:T(8,128)(2,1)S(1)}, u32[]{:S(2)}, u32[]{:S(2)}) collective-permute-start(bf16[256,256]{1,0:T(8,128)(2,1)S(1)} %get-tuple-element.32), channel_id=1, source_target_pairs={{0,16},{8,24},{16,0},{24,8},{1,17},{9,25},{17,1},{25,9},{2,18},{10... | collective-permute-start | bytes 393224 | tf_op jit(solution)/shard_map/ppermute | solution.py:438
  4.9 0.6 collective-permute-start.2
  5.5 2.6 %collective-permute-start.3 = (bf16[256,256]{1,0:T(8,128)(2,1)S(1)}, bf16[256,256]{1,0:T(8,128)(2,1)S(1)}, u32[]{:S(2)}, u32[]{:S(2)}) collective-permute-start(bf16[256,256]{1,0:T(8,128)(2,1)S(1)} %get-tuple-element.34), channel_id=1, source_target_pairs={{0,24},{8,0},{16,8},{24,16},{1,25},{9,1},{17,9},{25,17},{2,26},{10... | collective-permute-start | bytes 393224 | tf_op jit(solution)/shard_map/ppermute | solution.py:438
  8.1 0.0 copy-done.1
  8.1 0.0 copy-done.2
  8.1 0.1 concatenate.4.where_ref.refs_0_
  8.2 1.6 %shard_map.82 = (s32[9,64,128]{2,1,0:T(8,128)S(1)}, s32[37]{0:T(128)S(1)}, s32[37]{0:T(128)S(1)}) custom-call(s32[148]{0:T(256)S(1)} %concatenate.4.where_ref.refs_0_), custom_call_target="tpu_custom_call" | custom-call | flops 100000 | bytes 300000 | tf_op jit(solution)/shard_map/pallas_call | solution.py:407
  9.8 0.0 collective-permute-done.other_ref
  9.8 0.0 copy-done
  9.8 0.8 shard_map.83
  10.6 0.0 collective-permute-done.1.refs_3_
  10.6 1.5 %collective-permute-done.2.refs_4_ = bf16[256,256]{1,0:T(8,128)(2,1)S(1)} collective-permute-done((bf16[256,256]{1,0:T(8,128)(2,1)S(1)}, bf16[256,256]{1,0:T(8,128)(2,1)S(1)}, u32[]{:S(2)}, u32[]{:S(2)}) %collective-permute-start.2) | collective-permute-done | bytes 131104 | tf_op jit(solution)/shard_map/ppermute | solution.py:438
  12.1 0.1 collective-permute-done.3.refs_5_
  12.2 0.6 shard_map.85
  12.8 2.0 %collective-permute-start.4 = (bf16[768,256]{1,0:T(8,128)(2,1)S(1)}, bf16[768,256]{1,0:T(8,128)(2,1)S(1)}, u32[]{:S(2)}, u32[]{:S(2)}) collective-permute-start(bf16[768,256]{1,0:T(8,128)(2,1)S(1)} %get-tuple-element.39.refs_5_.refs_0_), channel_id=1, source_target_pairs={{0,32},{32,64},{64,96},{96,128},{128,160},{160,192},{192,224},{224... | collective-permute-start | bytes 1179656 | tf_op jit(solution)/shard_map/ppermute | solution.py:438
  14.8 4.0 %collective-permute-start.5 = (bf16[768,256]{1,0:T(8,128)(2,1)S(1)}, bf16[768,256]{1,0:T(8,128)(2,1)S(1)}, u32[]{:S(2)}, u32[]{:S(2)}) collective-permute-start(bf16[768,256]{1,0:T(8,128)(2,1)S(1)} %get-tuple-element.39.refs_5_.refs_0_), channel_id=1, source_target_pairs={{0,224},{32,0},{64,32},{96,64},{128,96},{160,128},{192,160},{224,1... | collective-permute-start | bytes 1179656 | tf_op jit(solution)/shard_map/ppermute | solution.py:438
  18.8 2.3 %collective-permute-start.8 = (bf16[256,512]{1,0:T(8,128)(2,1)S(1)}, bf16[256,512]{1,0:T(8,128)(2,1)S(1)}, u32[]{:S(2)}, u32[]{:S(2)}) collective-permute-start(bf16[256,512]{1,0:T(8,128)(2,1)S(1)} %shard_map.83), channel_id=1, source_target_pairs={{0,2},{1,3},{2,0},{3,1},{4,20},{5,21},{6,22},{7,23},{8,10},{9,11},... | collective-permute-start | bytes 786440 | tf_op jit(solution)/shard_map/ppermute | solution.py:453
  21.1 0.0 collective-permute-start.7
  21.1 2.0 %collective-permute-start.6 = (bf16[256,512]{1,0:T(8,128)(2,1)S(1)}, bf16[256,512]{1,0:T(8,128)(2,1)S(1)}, u32[]{:S(2)}, u32[]{:S(2)}) collective-permute-start(bf16[256,512]{1,0:T(8,128)(2,1)S(1)} %shard_map.83), channel_id=1, source_target_pairs={{0,3},{1,0},{2,1},{3,2},{4,28},{5,29},{6,30},{7,31},{8,11},{9,8},{... | collective-permute-start | bytes 786440 | tf_op jit(solution)/shard_map/ppermute | solution.py:453
  23.1 4.6 %collective-permute-done.4.refs_6_.refs_1_ = bf16[768,256]{1,0:T(8,128)(2,1)S(1)} collective-permute-done((bf16[768,256]{1,0:T(8,128)(2,1)S(1)}, bf16[768,256]{1,0:T(8,128)(2,1)S(1)}, u32[]{:S(2)}, u32[]{:S(2)}) %collective-permute-start.4) | collective-permute-done | bytes 393248 | tf_op jit(solution)/shard_map/ppermute | solution.py:438
  27.7 0.0 collective-permute-start.12
  27.7 0.0 collective-permute-done.5.refs_7_.refs_2_
  27.7 3.2 %collective-permute-start.13 = (bf16[768,256]{1,0:T(8,128)(2,1)S(1)}, bf16[768,256]{1,0:T(8,128)(2,1)S(1)}, u32[]{:S(2)}, u32[]{:S(2)}) collective-permute-start(bf16[768,256]{1,0:T(8,128)(2,1)S(1)} %collective-permute-done.5.refs_7_.refs_2_), channel_id=1, source_target_pairs={{0,224},{32,0},{64,32},{96,64},{128,96},{160,128},{192,160},{224,1... | collective-permute-start | bytes 1179656 | tf_op jit(solution)/shard_map/ppermute | solution.py:438
  30.9 0.0 collective-permute-done.8
  30.9 0.0 collective-permute-done.7
  31.0 0.0 collective-permute-done.6
  31.0 0.1 pad_maximum_fusion.refs_1_
  31.1 2.2 %collective-permute-start.11 = (bf16[4,256,512]{2,1,0:T(8,128)(2,1)S(1)}, bf16[4,256,512]{2,1,0:T(8,128)(2,1)S(1)}, u32[]{:S(2)}, u32[]{:S(2)}) collective-permute-start(bf16[4,256,512]{2,1,0:T(8,128)(2,1)S(1)} %pad_maximum_fusion.refs_1_), channel_id=1, source_target_pairs={{0,16},{1,17},{2,18},{3,19},{4,6},{5,7},{6,4},{7,5},{8,24},{9,25},... | collective-permute-start | bytes 3145736 | tf_op jit(solution)/shard_map/ppermute | solution.py:453
  33.3 1.2 %collective-permute-start.10 = (bf16[4,256,512]{2,1,0:T(8,128)(2,1)S(1)}, bf16[4,256,512]{2,1,0:T(8,128)(2,1)S(1)}, u32[]{:S(2)}, u32[]{:S(2)}) collective-permute-start(bf16[4,256,512]{2,1,0:T(8,128)(2,1)S(1)} %pad_maximum_fusion.refs_1_), channel_id=1, source_target_pairs={{0,8},{1,9},{2,10},{3,11},{4,5},{5,6},{6,7},{7,4},{8,16},{9,17},{1... | collective-permute-start | bytes 3145736 | tf_op jit(solution)/shard_map/ppermute | solution.py:453
  34.5 2.0 %collective-permute-start.9 = (bf16[4,256,512]{2,1,0:T(8,128)(2,1)S(1)}, bf16[4,256,512]{2,1,0:T(8,128)(2,1)S(1)}, u32[]{:S(2)}, u32[]{:S(2)}) collective-permute-start(bf16[4,256,512]{2,1,0:T(8,128)(2,1)S(1)} %pad_maximum_fusion.refs_1_), channel_id=1, source_target_pairs={{0,24},{1,25},{2,26},{3,27},{4,7},{5,4},{6,5},{7,6},{8,0},{9,1},{1... | collective-permute-start | bytes 3145736 | tf_op jit(solution)/shard_map/ppermute | solution.py:453
  36.5 2.6 %collective-permute-done.12.refs_8_.refs_0_ = bf16[768,256]{1,0:T(8,128)(2,1)S(1)} collective-permute-done((bf16[768,256]{1,0:T(8,128)(2,1)S(1)}, bf16[768,256]{1,0:T(8,128)(2,1)S(1)}, u32[]{:S(2)}, u32[]{:S(2)}) %collective-permute-start.12) | collective-permute-done | bytes 393248 | tf_op jit(solution)/shard_map/ppermute | solution.py:438
  39.1 0.0 collective-permute-start.14
  39.1 0.0 collective-permute-done.13.refs_9_.refs_1_
  39.1 3.2 %collective-permute-start.15 = (bf16[768,256]{1,0:T(8,128)(2,1)S(1)}, bf16[768,256]{1,0:T(8,128)(2,1)S(1)}, u32[]{:S(2)}, u32[]{:S(2)}) collective-permute-start(bf16[768,256]{1,0:T(8,128)(2,1)S(1)} %collective-permute-done.13.refs_9_.refs_1_), channel_id=1, source_target_pairs={{0,224},{32,0},{64,32},{96,64},{128,96},{160,128},{192,160},{224,1... | collective-permute-start | bytes 1179656 | tf_op jit(solution)/shard_map/ppermute | solution.py:438
  42.3 7.2 %collective-permute-done.14.refs_10_.refs_2_ = bf16[768,256]{1,0:T(8,128)(2,1)S(1)} collective-permute-done((bf16[768,256]{1,0:T(8,128)(2,1)S(1)}, bf16[768,256]{1,0:T(8,128)(2,1)S(1)}, u32[]{:S(2)}, u32[]{:S(2)}) %collective-permute-start.14) | collective-permute-done | bytes 393248 | tf_op jit(solution)/shard_map/ppermute | solution.py:438
  49.6 0.1 collective-permute-start.16
  49.7 0.0 collective-permute-done.15.refs_11_.refs_3_
  49.7 3.3 %collective-permute-start.17 = (bf16[192,256]{1,0:T(8,128)(2,1)S(1)}, bf16[192,256]{1,0:T(8,128)(2,1)S(1)}, u32[]{:S(2)}, u32[]{:S(2)}) collective-permute-start(bf16[192,256]{1,0:T(8,128)(2,1)S(1)} %slice.9), channel_id=1, source_target_pairs={{0,224},{32,0},{64,32},{96,64},{128,96},{160,128},{192,160},{224,1... | collective-permute-start | bytes 294920 | tf_op jit(solution)/shard_map/ppermute | solution.py:438
  53.0 0.1 shard_map.89
  53.1 2.1 %collective-permute-done.17.refs_1_.refs_13_ = bf16[192,256]{1,0:T(8,128)(2,1)S(1)} collective-permute-done((bf16[192,256]{1,0:T(8,128)(2,1)S(1)}, bf16[192,256]{1,0:T(8,128)(2,1)S(1)}, u32[]{:S(2)}, u32[]{:S(2)}) %collective-permute-start.17) | collective-permute-done | bytes 98336 | tf_op jit(solution)/shard_map/ppermute | solution.py:438
  55.2 0.0 collective-permute-start.20
  55.2 0.1 shard_map.88
  55.3 2.3 %collective-permute-done.16.refs_0_.refs_12_ = bf16[576,256]{1,0:T(8,128)(2,1)S(1)} collective-permute-done((bf16[576,256]{1,0:T(8,128)(2,1)S(1)}, bf16[576,256]{1,0:T(8,128)(2,1)S(1)}, u32[]{:S(2)}, u32[]{:S(2)}) %collective-permute-start.16) | collective-permute-done | bytes 294944 | tf_op jit(solution)/shard_map/ppermute | solution.py:438
  57.6 0.0 collective-permute-start.19
  57.6 0.0 collective-permute-done.11.refs_4_
  57.6 1.1 %collective-permute-done.10.refs_3_ = bf16[4,256,512]{2,1,0:T(8,128)(2,1)S(1)} collective-permute-done((bf16[4,256,512]{2,1,0:T(8,128)(2,1)S(1)}, bf16[4,256,512]{2,1,0:T(8,128)(2,1)S(1)}, u32[]{:S(2)}, u32[]{:S(2)}) %collective-permute-start.10) | collective-permute-done | bytes 1048608 | tf_op jit(solution)/shard_map/ppermute | solution.py:453
  58.7 0.0 collective-permute-done.9.refs_2_
  58.7 1.9 %shard_map.87 = (f32[4,128,256]{2,1,0:T(8,128)S(1)}, f32[4,128,256]{2,1,0:T(8,128)S(1)}) custom-call(s32[4]{0:T(128)S(1)} %pad_add_fusion.where_ref.refs_0_, bf16[4,256,512]{2,1,0:T(8,128)(2,1)S(1)} %pad_maximum_fusion.refs_1_, bf16[4,256,512]{2,1,0:T(8,128)(2,1)S(1)} %collective-permute-done.9.refs_2_, ...), custom_call_target="tpu_custom_call" | custom-call | flops 1000000000 | bytes 8000000 | tf_op jit(solution)/shard_map/pallas_call | solution.py:355
  60.6 0.1 collective-permute-start.18
  60.7 0.5 collective-permute-start.21
  61.2 0.0 collective-permute-done.19.refs_14_
  61.2 1.8 %collective-permute-done.21.refs_16_ = bf16[512,256]{1,0:T(8,128)(2,1)S(1)} collective-permute-done((bf16[512,256]{1,0:T(8,128)(2,1)S(1)}, bf16[512,256]{1,0:T(8,128)(2,1)S(1)}, u32[]{:S(2)}, u32[]{:S(2)}) %collective-permute-start.21) | collective-permute-done | bytes 262176 | tf_op jit(solution)/shard_map/ppermute | solution.py:438
  63.0 0.0 collective-permute-done.18.refs_4_
  63.0 0.0 collective-permute-done.20.refs_15_
  63.0 3.8 %shard_map.90.refs_5_ = bf16[512,128]{1,0:T(8,128)(2,1)S(1)} custom-call(s32[148]{0:T(256)S(1)} %concatenate.4.where_ref.refs_0_, s32[37]{0:T(128)S(1)} %get-tuple-element.45.refs_1_, s32[37]{0:T(128)S(1)} %get-tuple-element.46.refs_2_, f32[4,128,256]{2,1,0:T(8,128)S(1)} %get-tuple-element.49.refs_3_, f32[4,128,256]{2,1,0:T(8,128)S(1)} %collective-permute-done.18.refs_4_, ...), custom_call_target="tpu_custom_call" | custom-call | flops 2000000000 | bytes 8000000 | tf_op jit(solution)/shard_map/pallas_call | solution.py:355
  66.9 0.2 collective-permute-start.22
  67.1 1.2 %collective-permute-done.22.refs_6_ = bf16[512,128]{1,0:T(8,128)(2,1)S(1)} collective-permute-done((bf16[512,128]{1,0:T(8,128)(2,1)S(1)}, bf16[512,128]{1,0:T(8,128)(2,1)S(1)}, u32[]{:S(2)}, u32[]{:S(2)}) %collective-permute-start.22) | collective-permute-done | bytes 131104 | tf_op jit(solution)/shard_map/ppermute | solution.py:438
  68.3 1.5 %shard_map.91 = bf16[2048,128]{1,0:T(8,128)(2,1)S(1)} custom-call(s32[4]{0:T(128)S(1)} %pad_add_fusion.where_ref.refs_0_, bf16[4,256,512]{2,1,0:T(8,128)(2,1)S(1)} %pad_maximum_fusion.refs_1_, bf16[4,256,512]{2,1,0:T(8,128)(2,1)S(1)} %collective-permute-done.9.refs_2_, bf16[4,256,512]{2,1,0:T(8,128)(2,1)S(1)} %collective-permute-done.10.refs_3_, ...), custom_call_target="tpu_custom_call" | custom-call | flops 600000000 | bytes 8000000 | tf_op jit(solution)/shard_map/pallas_call | solution.py:355
  69.8 25.8 %all_to_all.9 = bf16[32,64,128]{2,1,0:T(8,128)(2,1)S(1)} all-to-all(bf16[32,64,128]{2,1,0:T(8,128)(2,1)S(1)} %bitcast.17), channel_id=1, replica_groups=mesh['z'=8,'x'=4,'c'=2,'kvh'=4] {'z','x'}, dimensions={0} | all-to-all | bytes 1048576 | tf_op jit(solution)/shard_map/all_to_all | solution.py:517
  95.6 0.1 convert_reduce_fusion
  95.6 0.7 copy_bitcast_fusion
  (6 shorter events, 0.1 us)
Async XLA Ops:
  0.0 9.8 %copy-start = (bf16[128,1024]{1,0:T(8,128)(2,1)S(1)}, bf16[128,1024]{1,0:T(8,128)(2,1)}, u32[]{:S(2)}) copy-start(bf16[128,1024]{1,0:T(8,128)(2,1)} %own_ref.1) | copy-start | bytes 786436
  0.0 9.8 %collective-permute-start = (bf16[128,1024]{1,0:T(8,128)(2,1)}, bf16[128,1024]{1,0:T(8,128)(2,1)S(1)}, u32[]{:S(2)}, u32[]{:S(2)}) collective-permute-start(bf16[128,1024]{1,0:T(8,128)(2,1)} %own_ref.1), channel_id=1, source_target_pairs={{0,4},{4,0},{1,5},{5,1},{2,6},{6,2},{3,7},{7,3},{8,12},{12,8},{9,1... | collective-permute-start | bytes 786440 | tf_op jit(solution)/shard_map/ppermute | solution.py:438
  1.8 8.8 %collective-permute-start.1 = (bf16[256,256]{1,0:T(8,128)(2,1)S(1)}, bf16[256,256]{1,0:T(8,128)(2,1)S(1)}, u32[]{:S(2)}, u32[]{:S(2)}) collective-permute-start(bf16[256,256]{1,0:T(8,128)(2,1)S(1)} %get-tuple-element.32), channel_id=1, source_target_pairs={{0,16},{8,24},{16,0},{24,8},{1,17},{9,25},{17,1},{25,9},{2,18},{10... | collective-permute-start | bytes 393224 | tf_op jit(solution)/shard_map/ppermute | solution.py:438
  4.9 3.2 %copy-start.1 = (s32[128]{0:T(128)S(1)}, s32[128]{0:T(128)}, u32[]{:S(2)}) copy-start(s32[128]{0:T(128)} %param.15) | copy-start | bytes 1540
  4.9 3.2 %copy-start.2 = (s32[16]{0:T(128)S(1)}, s32[16]{0:T(128)}, u32[]{:S(2)}) copy-start(s32[16]{0:T(128)} %param.14) | copy-start | bytes 196
  4.9 7.2 %collective-permute-start.2 = (bf16[256,256]{1,0:T(8,128)(2,1)S(1)}, bf16[256,256]{1,0:T(8,128)(2,1)S(1)}, u32[]{:S(2)}, u32[]{:S(2)}) collective-permute-start(bf16[256,256]{1,0:T(8,128)(2,1)S(1)} %get-tuple-element.33), channel_id=1, source_target_pairs={{0,8},{8,16},{16,24},{24,0},{1,9},{9,17},{17,25},{25,1},{2,10},{10... | collective-permute-start | bytes 393224 | tf_op jit(solution)/shard_map/ppermute | solution.py:438
  5.5 6.7 %collective-permute-start.3 = (bf16[256,256]{1,0:T(8,128)(2,1)S(1)}, bf16[256,256]{1,0:T(8,128)(2,1)S(1)}, u32[]{:S(2)}, u32[]{:S(2)}) collective-permute-start(bf16[256,256]{1,0:T(8,128)(2,1)S(1)} %get-tuple-element.34), channel_id=1, source_target_pairs={{0,24},{8,0},{16,8},{24,16},{1,25},{9,1},{17,9},{25,17},{2,26},{10... | collective-permute-start | bytes 393224 | tf_op jit(solution)/shard_map/ppermute | solution.py:438
  12.8 14.9 %collective-permute-start.4 = (bf16[768,256]{1,0:T(8,128)(2,1)S(1)}, bf16[768,256]{1,0:T(8,128)(2,1)S(1)}, u32[]{:S(2)}, u32[]{:S(2)}) collective-permute-start(bf16[768,256]{1,0:T(8,128)(2,1)S(1)} %get-tuple-element.39.refs_5_.refs_0_), channel_id=1, source_target_pairs={{0,32},{32,64},{64,96},{96,128},{128,160},{160,192},{192,224},{224... | collective-permute-start | bytes 1179656 | tf_op jit(solution)/shard_map/ppermute | solution.py:438
  14.8 12.9 %collective-permute-start.5 = (bf16[768,256]{1,0:T(8,128)(2,1)S(1)}, bf16[768,256]{1,0:T(8,128)(2,1)S(1)}, u32[]{:S(2)}, u32[]{:S(2)}) collective-permute-start(bf16[768,256]{1,0:T(8,128)(2,1)S(1)} %get-tuple-element.39.refs_5_.refs_0_), channel_id=1, source_target_pairs={{0,224},{32,0},{64,32},{96,64},{128,96},{160,128},{192,160},{224,1... | collective-permute-start | bytes 1179656 | tf_op jit(solution)/shard_map/ppermute | solution.py:438
  18.8 12.2 %collective-permute-start.8 = (bf16[256,512]{1,0:T(8,128)(2,1)S(1)}, bf16[256,512]{1,0:T(8,128)(2,1)S(1)}, u32[]{:S(2)}, u32[]{:S(2)}) collective-permute-start(bf16[256,512]{1,0:T(8,128)(2,1)S(1)} %shard_map.83), channel_id=1, source_target_pairs={{0,2},{1,3},{2,0},{3,1},{4,20},{5,21},{6,22},{7,23},{8,10},{9,11},... | collective-permute-start | bytes 786440 | tf_op jit(solution)/shard_map/ppermute | solution.py:453
  21.1 9.9 %collective-permute-start.7 = (bf16[256,512]{1,0:T(8,128)(2,1)S(1)}, bf16[256,512]{1,0:T(8,128)(2,1)S(1)}, u32[]{:S(2)}, u32[]{:S(2)}) collective-permute-start(bf16[256,512]{1,0:T(8,128)(2,1)S(1)} %shard_map.83), channel_id=1, source_target_pairs={{0,1},{1,2},{2,3},{3,0},{4,12},{5,13},{6,14},{7,15},{8,9},{9,10},{... | collective-permute-start | bytes 786440 | tf_op jit(solution)/shard_map/ppermute | solution.py:453
  21.1 9.9 %collective-permute-start.6 = (bf16[256,512]{1,0:T(8,128)(2,1)S(1)}, bf16[256,512]{1,0:T(8,128)(2,1)S(1)}, u32[]{:S(2)}, u32[]{:S(2)}) collective-permute-start(bf16[256,512]{1,0:T(8,128)(2,1)S(1)} %shard_map.83), channel_id=1, source_target_pairs={{0,3},{1,0},{2,1},{3,2},{4,28},{5,29},{6,30},{7,31},{8,11},{9,8},{... | collective-permute-start | bytes 786440 | tf_op jit(solution)/shard_map/ppermute | solution.py:453
  27.7 11.4 %collective-permute-start.12 = (bf16[768,256]{1,0:T(8,128)(2,1)S(1)}, bf16[768,256]{1,0:T(8,128)(2,1)S(1)}, u32[]{:S(2)}, u32[]{:S(2)}) collective-permute-start(bf16[768,256]{1,0:T(8,128)(2,1)S(1)} %collective-permute-done.4.refs_6_.refs_1_), channel_id=1, source_target_pairs={{0,32},{32,64},{64,96},{96,128},{128,160},{160,192},{192,224},{224... | collective-permute-start | bytes 1179656 | tf_op jit(solution)/shard_map/ppermute | solution.py:438
  27.7 11.4 %collective-permute-start.13 = (bf16[768,256]{1,0:T(8,128)(2,1)S(1)}, bf16[768,256]{1,0:T(8,128)(2,1)S(1)}, u32[]{:S(2)}, u32[]{:S(2)}) collective-permute-start(bf16[768,256]{1,0:T(8,128)(2,1)S(1)} %collective-permute-done.5.refs_7_.refs_2_), channel_id=1, source_target_pairs={{0,224},{32,0},{64,32},{96,64},{128,96},{160,128},{192,160},{224,1... | collective-permute-start | bytes 1179656 | tf_op jit(solution)/shard_map/ppermute | solution.py:438
  31.1 26.5 %collective-permute-start.11 = (bf16[4,256,512]{2,1,0:T(8,128)(2,1)S(1)}, bf16[4,256,512]{2,1,0:T(8,128)(2,1)S(1)}, u32[]{:S(2)}, u32[]{:S(2)}) collective-permute-start(bf16[4,256,512]{2,1,0:T(8,128)(2,1)S(1)} %pad_maximum_fusion.refs_1_), channel_id=1, source_target_pairs={{0,16},{1,17},{2,18},{3,19},{4,6},{5,7},{6,4},{7,5},{8,24},{9,25},... | collective-permute-start | bytes 3145736 | tf_op jit(solution)/shard_map/ppermute | solution.py:453
  33.3 25.5 %collective-permute-start.10 = (bf16[4,256,512]{2,1,0:T(8,128)(2,1)S(1)}, bf16[4,256,512]{2,1,0:T(8,128)(2,1)S(1)}, u32[]{:S(2)}, u32[]{:S(2)}) collective-permute-start(bf16[4,256,512]{2,1,0:T(8,128)(2,1)S(1)} %pad_maximum_fusion.refs_1_), channel_id=1, source_target_pairs={{0,8},{1,9},{2,10},{3,11},{4,5},{5,6},{6,7},{7,4},{8,16},{9,17},{1... | collective-permute-start | bytes 3145736 | tf_op jit(solution)/shard_map/ppermute | solution.py:453
  34.5 24.3 %collective-permute-start.9 = (bf16[4,256,512]{2,1,0:T(8,128)(2,1)S(1)}, bf16[4,256,512]{2,1,0:T(8,128)(2,1)S(1)}, u32[]{:S(2)}, u32[]{:S(2)}) collective-permute-start(bf16[4,256,512]{2,1,0:T(8,128)(2,1)S(1)} %pad_maximum_fusion.refs_1_), channel_id=1, source_target_pairs={{0,24},{1,25},{2,26},{3,27},{4,7},{5,4},{6,5},{7,6},{8,0},{9,1},{1... | collective-permute-start | bytes 3145736 | tf_op jit(solution)/shard_map/ppermute | solution.py:453
  39.1 10.5 %collective-permute-start.14 = (bf16[768,256]{1,0:T(8,128)(2,1)S(1)}, bf16[768,256]{1,0:T(8,128)(2,1)S(1)}, u32[]{:S(2)}, u32[]{:S(2)}) collective-permute-start(bf16[768,256]{1,0:T(8,128)(2,1)S(1)} %collective-permute-done.12.refs_8_.refs_0_), channel_id=1, source_target_pairs={{0,32},{32,64},{64,96},{96,128},{128,160},{160,192},{192,224},{224... | collective-permute-start | bytes 1179656 | tf_op jit(solution)/shard_map/ppermute | solution.py:438
  39.1 10.6 %collective-permute-start.15 = (bf16[768,256]{1,0:T(8,128)(2,1)S(1)}, bf16[768,256]{1,0:T(8,128)(2,1)S(1)}, u32[]{:S(2)}, u32[]{:S(2)}) collective-permute-start(bf16[768,256]{1,0:T(8,128)(2,1)S(1)} %collective-permute-done.13.refs_9_.refs_1_), channel_id=1, source_target_pairs={{0,224},{32,0},{64,32},{96,64},{128,96},{160,128},{192,160},{224,1... | collective-permute-start | bytes 1179656 | tf_op jit(solution)/shard_map/ppermute | solution.py:438
  49.6 8.0 %collective-permute-start.16 = (bf16[576,256]{1,0:T(8,128)(2,1)S(1)}, bf16[576,256]{1,0:T(8,128)(2,1)S(1)}, u32[]{:S(2)}, u32[]{:S(2)}) collective-permute-start(bf16[576,256]{1,0:T(8,128)(2,1)S(1)} %slice.8), channel_id=1, source_target_pairs={{0,32},{32,64},{64,96},{96,128},{128,160},{160,192},{192,224},{224... | collective-permute-start | bytes 884744 | tf_op jit(solution)/shard_map/ppermute | solution.py:438
  49.7 5.5 %collective-permute-start.17 = (bf16[192,256]{1,0:T(8,128)(2,1)S(1)}, bf16[192,256]{1,0:T(8,128)(2,1)S(1)}, u32[]{:S(2)}, u32[]{:S(2)}) collective-permute-start(bf16[192,256]{1,0:T(8,128)(2,1)S(1)} %slice.9), channel_id=1, source_target_pairs={{0,224},{32,0},{64,32},{96,64},{128,96},{160,128},{192,160},{224,1... | collective-permute-start | bytes 294920 | tf_op jit(solution)/shard_map/ppermute | solution.py:438
  55.2 7.8 %collective-permute-start.20 = (bf16[2048,256]{1,0:T(8,128)(2,1)S(1)}, bf16[2048,256]{1,0:T(8,128)(2,1)S(1)}, u32[]{:S(2)}, u32[]{:S(2)}) collective-permute-start(bf16[2048,256]{1,0:T(8,128)(2,1)S(1)} %shard_map.89), channel_id=1, source_target_pairs={{0,4},{4,0},{1,5},{5,1},{2,6},{6,2},{3,7},{7,3},{8,12},{12,8},{9,1... | collective-permute-start | bytes 3145736 | tf_op jit(solution)/shard_map/ppermute | solution.py:438
  57.6 3.6 %collective-permute-start.19 = (bf16[1536,256]{1,0:T(8,128)(2,1)S(1)}, bf16[1536,256]{1,0:T(8,128)(2,1)S(1)}, u32[]{:S(2)}, u32[]{:S(2)}) collective-permute-start(bf16[1536,256]{1,0:T(8,128)(2,1)S(1)} %shard_map.88), channel_id=1, source_target_pairs={{0,4},{4,0},{1,5},{5,1},{2,6},{6,2},{3,7},{7,3},{8,12},{12,8},{9,1... | collective-permute-start | bytes 2359304 | tf_op jit(solution)/shard_map/ppermute | solution.py:438
  60.6 2.4 %collective-permute-start.18 = (f32[4,128,256]{2,1,0:T(8,128)S(1)}, f32[4,128,256]{2,1,0:T(8,128)S(1)}, u32[]{:S(2)}, u32[]{:S(2)}) collective-permute-start(f32[4,128,256]{2,1,0:T(8,128)S(1)} %get-tuple-element.50), channel_id=1, source_target_pairs={{0,4},{4,0},{1,5},{5,1},{2,6},{6,2},{3,7},{7,3},{8,12},{12,8},{9,1... | collective-permute-start | bytes 1572872 | tf_op jit(solution)/shard_map/ppermute | solution.py:438
  60.7 2.3 %collective-permute-start.21 = (bf16[512,256]{1,0:T(8,128)(2,1)S(1)}, bf16[512,256]{1,0:T(8,128)(2,1)S(1)}, u32[]{:S(2)}, u32[]{:S(2)}) collective-permute-start(bf16[512,256]{1,0:T(8,128)(2,1)S(1)} %shard_map.86), channel_id=1, source_target_pairs={{0,4},{4,0},{1,5},{5,1},{2,6},{6,2},{3,7},{7,3},{8,12},{12,8},{9,1... | collective-permute-start | bytes 786440 | tf_op jit(solution)/shard_map/ppermute | solution.py:438
  66.9 1.4 %collective-permute-start.22 = (bf16[512,128]{1,0:T(8,128)(2,1)S(1)}, bf16[512,128]{1,0:T(8,128)(2,1)S(1)}, u32[]{:S(2)}, u32[]{:S(2)}) collective-permute-start(bf16[512,128]{1,0:T(8,128)(2,1)S(1)} %shard_map.90.refs_5_), channel_id=1, source_target_pairs={{0,4},{4,0},{1,5},{5,1},{2,6},{6,2},{3,7},{7,3},{8,12},{12,8},{9,1... | collective-permute-start | bytes 393224 | tf_op jit(solution)/shard_map/ppermute | solution.py:438
